TPU v7x, 32 devices: a whole 2x2x4 slice. The times are simulated.
32 devices in a mesh: ulysses: 4 (over y, core), blk: 8 (over z, x).
Axes of the slice: x: 2, y: 2, z: 4, core: 2. Of those that a mesh axis runs over, the one named last changes fastest.
Arguments:
- block_input: bfloat16 [4096, 2048], P(('blk', 'ulysses')), may hold values from -6 to 6
- w_query: float32 [2048, 2048], P(('ulysses', 'blk')), may hold values from -0.125 to 0.125
- w_key: float32 [2048, 2048], P(('ulysses', 'blk')), may hold values from -0.125 to 0.125
- w_value: float32 [2048, 2048], P(('ulysses', 'blk')), may hold values from -0.125 to 0.125
- w_out: float32 [2048, 2048], P(('ulysses', 'blk')), may hold values from -1 to 1
- attn_gain: float32 [2048], P(('ulysses', 'blk')), may hold values from 0.1 to 1.9
- ffn_gain: float32 [2048], P(('ulysses', 'blk')), may hold values from 0.1 to 1.9
- query_gain: float32 [2048], P(('ulysses', 'blk')), may hold values from 1.2 to 1.6
- key_gain: float32 [2048], P(('ulysses', 'blk')), may hold values from 1.2 to 1.6
- router: float32 [2048, 16], P(('ulysses', 'blk')), may hold values from -0.0625 to 0.0625
- w_gate: float32 [16, 2048, 1024], P('blk', None, 'ulysses'), may hold values from -0.125 to 0.125
- w_up: float32 [16, 2048, 1024], P('blk', None, 'ulysses'), may hold values from -0.125 to 0.125
- w_down: float32 [16, 1024, 2048], P('blk', 'ulysses'), may hold values from -4 to 4
- expert_ids: int32 [4096, 8], P(('blk', 'ulysses')), may hold values from 0 to 15, as said below
- slot_ids: int32 [4096, 8], P(('blk', 'ulysses')), may hold values from 0 to 79, as said below
- doc_starts: int32 [8], replicated, may hold values from 0 to 4095, as said below
- cotangent: bfloat16 [4096, 2048], P(('blk', 'ulysses')), may hold values from -6 to 6
Outputs:
- mixed: bfloat16 [4096, 2048], P(('blk', 'ulysses'))
- input_grad: bfloat16 [4096, 2048], P(('blk', 'ulysses'))
- grad_w_query: float32 [2048, 2048], P(('ulysses', 'blk'))
- grad_w_key: float32 [2048, 2048], P(('ulysses', 'blk'))
- grad_w_value: float32 [2048, 2048], P(('ulysses', 'blk'))
- grad_w_out: float32 [2048, 2048], P(('ulysses', 'blk'))
- grad_attn_gain: float32 [2048], P(('ulysses', 'blk'))
- grad_ffn_gain: float32 [2048], P(('ulysses', 'blk'))
- grad_query_gain: float32 [2048], P(('ulysses', 'blk'))
- grad_key_gain: float32 [2048], P(('ulysses', 'blk'))
- grad_router: float32 [2048, 16], P(('ulysses', 'blk'))
- grad_w_gate: float32 [16, 2048, 1024], P('blk', None, 'ulysses')
- grad_w_up: float32 [16, 2048, 1024], P('blk', None, 'ulysses')
- grad_w_down: float32 [16, 1024, 2048], P('blk', 'ulysses')
Inputs may be any that keep to these rules, and one draw needn't show every extreme that they name: `expert_ids`: each row names 8 different experts. In each aligned block of 128 rows (the rows of one device) no expert is named by more than 80 rows, and one expert is named by exactly 80 rows in every block. `slot_ids`: within one aligned block of 128 rows, the choices that name the same expert carry different slots. `doc_starts`: strictly rising, the first is 0; the second lies below 512 and the last 6 lie among the last 512 tokens.
All inputs are finite; a program needn't handle non-finite values.
Results may differ from a plain program's by a relative error of at most 0.02.
The roundings to bfloat16 on the way count: a program that leaves them out, or rounds other values in their place, can miss the bound.
Values may be sent and summed in bfloat16 or wider, within the bound.
No kernel may reach another device: no remote copies, remote signals or barrier semaphores. Data moves between devices by JAX's collectives and lax.ppermute only.
A program may use at most 320 MiB of HBM per device.

v0:
```python
import jax
import jax.numpy as jnp
from jax import lax
from jax.sharding import PartitionSpec as P

HEAD_DIM = 128


NORM_EPSILON = 1e-05
ROPE_BASE = 10000.0
MASKED_SCORE = -1e30


def norm_parts(values):
    recip_factor = lax.rsqrt(jnp.mean(values * values, axis=-1, keepdims=True) + NORM_EPSILON)
    return (values * recip_factor, recip_factor)


def norm_back(grad_in, hat_values, recip_factor):
    return recip_factor * (
        grad_in - hat_values * jnp.mean(grad_in * hat_values, axis=-1, keepdims=True)
    )


def doc_tables(doc_starts, first_token, token_count):
    tokens_at = first_token + jnp.arange(token_count, dtype=jnp.int32)
    segment = jnp.sum((doc_starts[None, :] <= tokens_at[:, None]).astype(jnp.int32), axis=1) - 1
    picked = jnp.arange(doc_starts.shape[0], dtype=jnp.int32)[None, :] == segment[:, None]
    begins = jnp.sum(jnp.where(picked, doc_starts[None, :], 0), axis=1)
    return (segment, tokens_at - begins)


def angles(position, head_size):
    half_size = head_size // 2
    frequency = ROPE_BASE ** (-(jnp.arange(half_size, dtype=jnp.float32) * 2.0 / head_size))
    turned = position.astype(jnp.float32)[:, None] * frequency[None, :]
    return (jnp.cos(turned)[:, None, :], jnp.sin(turned)[:, None, :])


def rotate(values, cosine_table, sine_table):
    half_size = values.shape[-1] // 2
    first_half = values[..., :half_size]
    second_half = values[..., half_size:]
    return jnp.concatenate(
        [
            first_half * cosine_table - second_half * sine_table,
            second_half * cosine_table + first_half * sine_table,
        ],
        axis=-1,
    )


def rotate_back(values, cosine_table, sine_table):
    half_size = values.shape[-1] // 2
    first_half = values[..., :half_size]
    second_half = values[..., half_size:]
    return jnp.concatenate(
        [
            first_half * cosine_table + second_half * sine_table,
            second_half * cosine_table - first_half * sine_table,
        ],
        axis=-1,
    )


def head_cols(source, head_index):
    return lax.dynamic_slice_in_dim(source, head_index * HEAD_DIM, HEAD_DIM, 1)


def regroup(stacked):
    return jnp.transpose(stacked, (1, 0, 2)).reshape(
        stacked.shape[1], stacked.shape[0] * stacked.shape[2]
    )


def per_device(
    block_input,
    w_query,
    w_key,
    w_value,
    w_out,
    attn_gain,
    ffn_gain,
    query_gain,
    key_gain,
    router,
    w_gate,
    w_up,
    w_down,
    expert_ids,
    slot_ids,
    doc_starts,
    cotangent,
):
    bfloat = jnp.bfloat16
    single = jnp.float32
    ulysses_size = lax.axis_size("ulysses")
    token_count, model_width = block_input.shape
    picks_per_row = expert_ids.shape[1]
    experts = router.shape[1]
    capacity = 5 * token_count * picks_per_row // (4 * experts)
    blk_index = lax.axis_index("blk")
    ulysses_index = lax.axis_index("ulysses")
    first_token = (blk_index * ulysses_size + ulysses_index) * token_count
    row_count = ulysses_size * token_count
    first_row = blk_index * row_count
    local_width = model_width // ulysses_size
    local_heads = local_width // HEAD_DIM
    score_scale = HEAD_DIM ** (-0.5)

    def gather_weights():
        return (
            lax.all_gather(w_query.astype(bfloat), ("ulysses", "blk"), axis=0, tiled=True),
            lax.all_gather(w_key.astype(bfloat), ("ulysses", "blk"), axis=0, tiled=True),
            lax.all_gather(w_value.astype(bfloat), ("ulysses", "blk"), axis=0, tiled=True),
            lax.all_gather(w_out.astype(bfloat), ("ulysses", "blk"), axis=0, tiled=True),
            lax.all_gather(attn_gain.astype(bfloat), ("ulysses", "blk"), axis=0, tiled=True),
            lax.all_gather(ffn_gain.astype(bfloat), ("ulysses", "blk"), axis=0, tiled=True),
            lax.all_gather(query_gain.astype(bfloat), ("ulysses", "blk"), axis=0, tiled=True),
            lax.all_gather(key_gain.astype(bfloat), ("ulysses", "blk"), axis=0, tiled=True),
            lax.all_gather(router.astype(bfloat), ("ulysses", "blk"), axis=0, tiled=True),
        )

    def gather_keys(k_heads, v_heads):
        return (
            lax.all_gather(k_heads, "blk", axis=0, tiled=True),
            lax.all_gather(v_heads, "blk", axis=0, tiled=True),
        )

    gathered = gather_weights()
    query_full, key_full, value_full, out_full = (
        gathered[0],
        gathered[1],
        gathered[2],
        gathered[3],
    )
    attn_g = gathered[4].astype(single)
    ffn_g = gathered[5].astype(single)
    query_g = gathered[6].astype(single)
    key_g = gathered[7].astype(single)
    router_full = gathered[8]
    expert_gate, expert_up, expert_down = (
        lax.all_gather(w_gate.astype(bfloat), "ulysses", axis=2, tiled=True),
        lax.all_gather(w_up.astype(bfloat), "ulysses", axis=2, tiled=True),
        lax.all_gather(w_down.astype(bfloat), "ulysses", axis=1, tiled=True),
    )
    inputs = block_input.astype(single)
    hat_one, recip_one = norm_parts(inputs)
    normed = (hat_one * attn_g).astype(bfloat)
    q_lin = jnp.dot(normed, query_full, preferred_element_type=single)
    k_lin = jnp.dot(normed, key_full, preferred_element_type=single)
    v_lin = jnp.dot(normed, value_full, preferred_element_type=single)
    q_hat, q_recip = norm_parts(q_lin)
    k_hat, k_recip = norm_parts(k_lin)
    _, position = doc_tables(doc_starts, first_token, token_count)
    cosine_table, sine_table = angles(position, HEAD_DIM)
    q_rot = rotate((q_hat * query_g).reshape(token_count, -1, HEAD_DIM), cosine_table, sine_table)
    k_rot = rotate((k_hat * key_g).reshape(token_count, -1, HEAD_DIM), cosine_table, sine_table)
    q_rot = q_rot.reshape(token_count, model_width).astype(bfloat)
    k_rot = k_rot.reshape(token_count, model_width).astype(bfloat)
    v_low = v_lin.astype(bfloat)
    q_heads, k_heads, v_heads = (
        lax.all_to_all(q_rot, "ulysses", split_axis=1, concat_axis=0, tiled=True),
        lax.all_to_all(k_rot, "ulysses", split_axis=1, concat_axis=0, tiled=True),
        lax.all_to_all(v_low, "ulysses", split_axis=1, concat_axis=0, tiled=True),
    )
    k_all, v_all = gather_keys(k_heads, v_heads)
    key_total = k_all.shape[0]
    segment_all, _ = doc_tables(doc_starts, 0, key_total)
    segment_rows = lax.dynamic_slice_in_dim(segment_all, first_row, row_count, 0)
    row_at = first_row + jnp.arange(row_count, dtype=jnp.int32)
    every_index = jnp.arange(key_total, dtype=jnp.int32)
    key_mask = (segment_rows[:, None] == segment_all[None, :]) & (
        every_index[None, :] <= row_at[:, None]
    )

    def attend_head(head_index):
        q_one = head_cols(q_heads, head_index)
        k_one = head_cols(k_all, head_index)
        v_one = head_cols(v_all, head_index)
        scores = jnp.einsum("qd,kd->qk", q_one, k_one, preferred_element_type=single) * score_scale
        scores = jnp.where(key_mask, scores, MASKED_SCORE)
        top_score = jnp.max(scores, axis=1, keepdims=True)
        shifted = jnp.exp(scores - top_score)
        weight_total = jnp.sum(shifted, axis=1, keepdims=True)
        attn_probs = (shifted / weight_total).astype(bfloat)
        head_out = jnp.dot(attn_probs, v_one, preferred_element_type=single).astype(bfloat)
        return (head_out, (top_score + jnp.log(weight_total))[:, 0])

    heads_result, log_totals = lax.map(attend_head, jnp.arange(local_heads, dtype=jnp.int32))
    attended = regroup(heads_result)
    out_rows = lax.all_to_all(attended, "ulysses", split_axis=0, concat_axis=1, tiled=True)
    residual_mid = inputs + jnp.dot(out_rows, out_full, preferred_element_type=single)
    hat_two, recip_two = norm_parts(residual_mid)
    ffn_in = (hat_two * ffn_g).astype(bfloat)
    logits = jnp.dot(ffn_in, router_full, preferred_element_type=single)
    shifted_logits = jnp.exp(logits - jnp.max(logits, axis=1, keepdims=True))
    router_probs = shifted_logits / jnp.sum(shifted_logits, axis=1, keepdims=True)
    choice_onehot = expert_ids[:, :, None] == jnp.arange(experts, dtype=jnp.int32)[None, None, :]
    gate_vals = jnp.sum(jnp.where(choice_onehot, router_probs[:, None, :], 0.0), axis=2)
    slot_index = (expert_ids * capacity + slot_ids).reshape(-1)
    slot_hits = slot_index[None, :] == jnp.arange(experts * capacity, dtype=jnp.int32)[:, None]
    owner_pair = jnp.sum(
        jnp.where(slot_hits, jnp.arange(token_count * picks_per_row, dtype=jnp.int32)[None, :], 0),
        axis=1,
    )
    slot_filled = jnp.any(slot_hits, axis=1)
    owner_token = owner_pair // picks_per_row
    outgoing = jnp.where(
        slot_filled[:, None], jnp.take(ffn_in, owner_token, axis=0), jnp.zeros((), bfloat)
    )
    received = lax.all_to_all(
        outgoing.reshape(experts, capacity, model_width),
        "blk",
        split_axis=0,
        concat_axis=1,
        tiled=True,
    )
    gate_val = jnp.einsum("erd,edf->erf", received, expert_gate, preferred_element_type=single)
    up_val = jnp.einsum("erd,edf->erf", received, expert_up, preferred_element_type=single)
    sigmoid_gate = jax.nn.sigmoid(gate_val)
    hidden_low = (gate_val * sigmoid_gate * up_val).astype(bfloat)
    expert_out = jnp.einsum(
        "erf,efd->erd", hidden_low, expert_down, preferred_element_type=single
    ).astype(bfloat)
    returned_all = lax.all_to_all(
        expert_out, "blk", split_axis=1, concat_axis=0, tiled=True
    ).reshape(experts * capacity, model_width)
    returned = jnp.take(returned_all, slot_index, axis=0).reshape(
        token_count, picks_per_row, model_width
    )
    mixed = residual_mid + jnp.sum(gate_vals[:, :, None] * returned.astype(single), axis=1)
    cot_rows = cotangent.astype(single)
    d_gate_vals = jnp.sum(cot_rows[:, None, :] * returned.astype(single), axis=2)
    gate_flat = gate_vals.reshape(-1)
    slot_grad = jnp.where(
        slot_filled[:, None],
        jnp.take(gate_flat, owner_pair)[:, None] * jnp.take(cot_rows, owner_token, axis=0),
        0.0,
    )
    slot_grad = slot_grad.astype(bfloat).reshape(experts, capacity, model_width)
    d_expert_out = lax.all_to_all(slot_grad, "blk", split_axis=0, concat_axis=1, tiled=True)
    grad_down_part = jnp.einsum(
        "erf,erd->efd", hidden_low, d_expert_out, preferred_element_type=single
    )
    d_hidden = jnp.einsum("erd,efd->erf", d_expert_out, expert_down, preferred_element_type=single)
    d_gate = (d_hidden * up_val * sigmoid_gate * (1.0 + gate_val * (1.0 - sigmoid_gate))).astype(
        bfloat
    )
    d_up = (d_hidden * gate_val * sigmoid_gate).astype(bfloat)
    grad_gate_part = jnp.einsum("erd,erf->edf", received, d_gate, preferred_element_type=single)
    grad_up_part = jnp.einsum("erd,erf->edf", received, d_up, preferred_element_type=single)
    d_received = (
        jnp.einsum("erf,edf->erd", d_gate, expert_gate, preferred_element_type=single)
        + jnp.einsum("erf,edf->erd", d_up, expert_up, preferred_element_type=single)
    ).astype(bfloat)
    d_returned = lax.all_to_all(d_received, "blk", split_axis=1, concat_axis=0, tiled=True).reshape(
        experts * capacity, model_width
    )
    grad_w_gate, grad_w_up, grad_w_down = (
        lax.psum_scatter(
            grad_gate_part.astype(jnp.bfloat16), "ulysses", scatter_dimension=2, tiled=True
        ).astype(jnp.float32),
        lax.psum_scatter(
            grad_up_part.astype(jnp.bfloat16), "ulysses", scatter_dimension=2, tiled=True
        ).astype(jnp.float32),
        lax.psum_scatter(
            grad_down_part.astype(jnp.bfloat16), "ulysses", scatter_dimension=1, tiled=True
        ).astype(jnp.float32),
    )
    gathered_back = gather_weights()
    query_back, key_back, value_back, out_back = (
        gathered_back[0],
        gathered_back[1],
        gathered_back[2],
        gathered_back[3],
    )
    router_back = gathered_back[8]
    d_ffn_in = jnp.sum(
        jnp.take(d_returned, slot_index, axis=0)
        .reshape(token_count, picks_per_row, model_width)
        .astype(single),
        axis=1,
    )
    d_probs = jnp.sum(jnp.where(choice_onehot, d_gate_vals[:, :, None], 0.0), axis=1)
    d_logits = (
        router_probs * (d_probs - jnp.sum(router_probs * d_probs, axis=1, keepdims=True))
    ).astype(bfloat)
    grad_router_part = jnp.einsum("td,te->de", ffn_in, d_logits, preferred_element_type=single)
    d_ffn_in = d_ffn_in + jnp.einsum(
        "te,de->td", d_logits, router_back, preferred_element_type=single
    )
    grad_ffn_part = jnp.sum(d_ffn_in * hat_two, axis=0)
    d_mid = cot_rows + norm_back(d_ffn_in * ffn_g, hat_two, recip_two)
    d_attn_out = d_mid.astype(bfloat)
    grad_out_part = jnp.einsum("ti,to->io", out_rows, d_attn_out, preferred_element_type=single)
    d_out_rows = jnp.einsum(
        "to,io->ti", d_attn_out, out_back, preferred_element_type=single
    ).astype(bfloat)
    d_heads = lax.all_to_all(d_out_rows, "ulysses", split_axis=1, concat_axis=0, tiled=True)
    k_back, v_back = gather_keys(k_heads, v_heads)

    def head_grads(head_index):
        q_one = head_cols(q_heads, head_index)
        k_one = head_cols(k_back, head_index)
        v_one = head_cols(v_back, head_index)
        grad_one = head_cols(d_heads, head_index)
        log_one = log_totals[head_index]
        scores = jnp.einsum("qd,kd->qk", q_one, k_one, preferred_element_type=single) * score_scale
        attn_probs = jnp.where(key_mask, jnp.exp(scores - log_one[:, None]), 0.0)
        d_attn_probs = jnp.einsum("qd,kd->qk", grad_one, v_one, preferred_element_type=single)
        row_dot = jnp.sum(attn_probs * d_attn_probs, axis=1, keepdims=True)
        d_scores = (attn_probs * (d_attn_probs - row_dot)).astype(bfloat)
        d_query = (
            jnp.einsum("qk,kd->qd", d_scores, k_one, preferred_element_type=single) * score_scale
        )
        d_key = (
            jnp.einsum("qk,qd->kd", d_scores, q_one, preferred_element_type=single) * score_scale
        )
        d_value = jnp.einsum(
            "qk,qd->kd", attn_probs.astype(bfloat), grad_one, preferred_element_type=single
        )
        d_key_own, d_value_own = (
            lax.psum_scatter(
                d_key.astype(jnp.bfloat16), "blk", scatter_dimension=0, tiled=True
            ).astype(jnp.float32),
            lax.psum_scatter(
                d_value.astype(jnp.bfloat16), "blk", scatter_dimension=0, tiled=True
            ).astype(jnp.float32),
        )
        return (d_query, d_key_own, d_value_own)

    dq_heads, dk_heads, dv_heads = lax.map(head_grads, jnp.arange(local_heads, dtype=jnp.int32))
    dq_rows, dk_rows, dv_rows = (
        lax.all_to_all(
            regroup(dq_heads).astype(jnp.bfloat16),
            "ulysses",
            split_axis=0,
            concat_axis=1,
            tiled=True,
        ).astype(jnp.float32),
        lax.all_to_all(
            regroup(dk_heads).astype(jnp.bfloat16),
            "ulysses",
            split_axis=0,
            concat_axis=1,
            tiled=True,
        ).astype(jnp.float32),
        lax.all_to_all(
            regroup(dv_heads).astype(jnp.bfloat16),
            "ulysses",
            split_axis=0,
            concat_axis=1,
            tiled=True,
        ).astype(jnp.float32),
    )
    dq_norm = rotate_back(
        dq_rows.reshape(token_count, -1, HEAD_DIM), cosine_table, sine_table
    ).reshape(token_count, model_width)
    dk_norm = rotate_back(
        dk_rows.reshape(token_count, -1, HEAD_DIM), cosine_table, sine_table
    ).reshape(token_count, model_width)
    grad_qgain_part = jnp.sum(dq_norm * q_hat, axis=0)
    grad_kgain_part = jnp.sum(dk_norm * k_hat, axis=0)
    d_q_lin = norm_back(dq_norm * query_g, q_hat, q_recip).astype(bfloat)
    d_k_lin = norm_back(dk_norm * key_g, k_hat, k_recip).astype(bfloat)
    d_v_lin = dv_rows.astype(bfloat)
    grad_query_part = jnp.einsum("td,to->do", normed, d_q_lin, preferred_element_type=single)
    grad_key_part = jnp.einsum("td,to->do", normed, d_k_lin, preferred_element_type=single)
    grad_value_part = jnp.einsum("td,to->do", normed, d_v_lin, preferred_element_type=single)
    d_normed = (
        jnp.einsum("to,do->td", d_q_lin, query_back, preferred_element_type=single)
        + jnp.einsum("to,do->td", d_k_lin, key_back, preferred_element_type=single)
        + jnp.einsum("to,do->td", d_v_lin, value_back, preferred_element_type=single)
    )
    grad_attn_part = jnp.sum(d_normed * hat_one, axis=0)
    input_grad = d_mid + norm_back(d_normed * attn_g, hat_one, recip_one)
    summed = (
        lax.psum_scatter(grad_query_part, ("ulysses", "blk"), scatter_dimension=0, tiled=True),
        lax.psum_scatter(grad_key_part, ("ulysses", "blk"), scatter_dimension=0, tiled=True),
        lax.psum_scatter(grad_value_part, ("ulysses", "blk"), scatter_dimension=0, tiled=True),
        lax.psum_scatter(grad_out_part, ("ulysses", "blk"), scatter_dimension=0, tiled=True),
        lax.psum_scatter(grad_attn_part, ("ulysses", "blk"), scatter_dimension=0, tiled=True),
        lax.psum_scatter(grad_ffn_part, ("ulysses", "blk"), scatter_dimension=0, tiled=True),
        lax.psum_scatter(grad_qgain_part, ("ulysses", "blk"), scatter_dimension=0, tiled=True),
        lax.psum_scatter(grad_kgain_part, ("ulysses", "blk"), scatter_dimension=0, tiled=True),
        lax.psum_scatter(grad_router_part, ("ulysses", "blk"), scatter_dimension=0, tiled=True),
    )
    return (
        mixed.astype(bfloat),
        input_grad.astype(bfloat),
        summed[0],
        summed[1],
        summed[2],
        summed[3],
        summed[4],
        summed[5],
        summed[6],
        summed[7],
        summed[8],
        grad_w_gate,
        grad_w_up,
        grad_w_down,
    )


def solution(mesh):
    in_specs = (
        P(("blk", "ulysses"), None),
        P(("ulysses", "blk"), None),
        P(("ulysses", "blk"), None),
        P(("ulysses", "blk"), None),
        P(("ulysses", "blk"), None),
        P(("ulysses", "blk")),
        P(("ulysses", "blk")),
        P(("ulysses", "blk")),
        P(("ulysses", "blk")),
        P(("ulysses", "blk"), None),
        P("blk", None, "ulysses"),
        P("blk", None, "ulysses"),
        P("blk", "ulysses", None),
        P(("blk", "ulysses"), None),
        P(("blk", "ulysses"), None),
        P(),
        P(("blk", "ulysses"), None),
    )
    out_specs = (
        P(("blk", "ulysses"), None),
        P(("blk", "ulysses"), None),
        P(("ulysses", "blk"), None),
        P(("ulysses", "blk"), None),
        P(("ulysses", "blk"), None),
        P(("ulysses", "blk"), None),
        P(("ulysses", "blk")),
        P(("ulysses", "blk")),
        P(("ulysses", "blk")),
        P(("ulysses", "blk")),
        P(("ulysses", "blk"), None),
        P("blk", None, "ulysses"),
        P("blk", None, "ulysses"),
        P("blk", "ulysses", None),
    )
    return jax.shard_map(
        per_device, mesh=mesh, in_specs=in_specs, out_specs=out_specs, check_vma=False
    )
```

profile of v0, /device:TPU:0, one launch (start us, length us, event | category | flops | bytes accessed | tf_op | source)
XLA Modules:
  0.0 3674.2 jit_solution(1149127375365280203)
XLA Ops:
  16.3 42.5 %all-reduce.9 = (bf16[2048]{0:T(1024)(128)(2,1)S(1)}, bf16[2048]{0:T(1024)(128)(2,1)S(1)}, bf16[2048]{0:T(1024)(128)(2,1)S(1)}, bf16[2048]{0:T(1024)(128)(2,1)S(1)}) all-reduce(bf16[2048]{0:T(1024)(128)(2,1)S(1)} %dynamic-update-slice, bf16[2048]{0:T(1024)(128)(2,1)S(1)} %dynamic-update-slice.1, ...), channel_id=1, replica_groups=mesh['ulysses'=4,'blk'=8] {'ulysses','blk'}, use_global_device_ids=true, to_apply=%add | all-reduce | flops 8192 | bytes 32768
  61.8 30.0 all-gather.11.cloned.1.call-done
  98.2 73.2 %all-gather.13.cloned.1.call-done = bf16[2048,2048]{1,0:T(8,128)(2,1)} async-done(((bf16[64,2048]{1,0:T(8,128)(2,1)}), bf16[2048,2048]{1,0:T(8,128)(2,1)}) %all-gather.13.cloned.1.call-update) | async-done | bytes 8388624 | tf_op jit(solution)/shard_map/all_gather | solution.py:114
  193.6 58.8 %all-gather.17.cloned.1.call-done = bf16[2048,2048]{1,0:T(8,128)(2,1)} async-done(((bf16[64,2048]{1,0:T(8,128)(2,1)}), bf16[2048,2048]{1,0:T(8,128)(2,1)}) %all-gather.17.cloned.1.call-update) | async-done | bytes 8388624 | tf_op jit(solution)/shard_map/all_gather | solution.py:115
  295.2 32.1 all-gather.15.cloned.1.call-done
  327.3 73.4 %all-gather.19.cloned.1.call-done = bf16[4096,512]{1,0:T(8,128)(2,1)} async-done(((bf16[512,512]{1,0:T(8,128)(2,1)}), bf16[4096,512]{1,0:T(8,128)(2,1)}) %all-gather.19.cloned.1.call-update) | async-done | bytes 4194320 | tf_op jit(solution)/shard_map/all_gather | solution.py:127
  400.7 64.5 %while.28 = (s32[]{:T(128)}, bf16[4,512,128]{2,1,0:T(8,128)(2,1)S(1)}, f32[4,512]{1,0:T(4,128)}, s32[4]{0:T(128)S(1)}, bf16[512,512]{1,0:T(8,128)(2,1)S(1)}, /*i...) while((s32[]{:T(128)}, ...), condition=%wide.region_9.10_spmd.clone, body=%wide.region_6.9_spmd.clone.sunk | while | flops 1096875520 | bytes 61122272 | solution.py:190
  494.9 120.7 %all_to_all.193 = bf16[16,80,2048]{2,1,0:T(8,128)(2,1)S(1)} all-to-all(bf16[16,80,2048]{2,1,0:T(8,128)(2,1)S(1)} %select_select_fusion), channel_id=1, replica_groups=mesh['ulysses'=4,'blk'=8] {'blk'}, dimensions={0} | all-to-all | bytes 10485760 | tf_op jit(solution)/shard_map/all_to_all | solution.py:212
  630.1 12.7 multiply_convert_fusion.3
  642.9 19.1 all-gather.27.cloned.1.call-done
  689.3 171.8 %all-gather = bf16[32,64,16]{1,2,0:T(8,128)(2,1)S(1)} all-gather(bf16[1,64,16]{1,2,0:T(8,128)(2,1)S(1)} %convert_bitcast_fusion.6), channel_id=1, replica_groups=mesh['ulysses'=4,'blk'=8] {'ulysses','blk'}, dimensions={0}, use_global_device_ids=true | all-gather | bytes 67584 | tf_op jit(solution)/shard_map/all_gather | solution.py:121
  902.7 116.1 %all_to_all.194 = bf16[16,80,2048]{2,1,0:T(8,128)(2,1)S(1)} all-to-all(bf16[16,80,2048]{2,1,0:T(8,128)(2,1)S(1)} %select_convert_fusion), channel_id=1, replica_groups=mesh['ulysses'=4,'blk'=8] {'blk'}, dimensions={0} | all-to-all | bytes 10485760 | tf_op jit(solution)/shard_map/all_to_all | solution.py:242
  1019.2 15.7 multiply_convert_fusion.1
  1047.2 12.6 add_convert_fusion
  1075.2 114.1 %all-to-all-done.7 = bf16[2,640,2048]{2,0,1:T(2,128)(2,1)} async-done(((bf16[2,640,2048]{2,0,1:T(2,128)(2,1)}), bf16[2,640,2048]{2,0,1:T(2,128)(2,1)}, u32[]{:S(2)}, u32[]{:S(2)}) %all-to-all-start.7) | async-done | bytes 5242912 | tf_op jit(solution)/shard_map/all_to_all | solution.py:257
  1240.6 627.7 %while.29 = (s32[]{:T(128)}, bf16[4,512,128]{2,1,0:T(8,128)(2,1)S(1)}, bf16[4,512,128]{2,1,0:T(8,128)(2,1)S(1)}, bf16[4,512,128]{2,1,0:T(8,128)(2,1)}, s32[4]{0:...) while((s32[]{:T(128)}, ...), condition=%wide.region_26.28_spmd.clone, body=%wide.region_22.27_spmd.clone.sunk | while | flops 2711289344 | bytes 131367392 | solution.py:333
  1277.0 52.1 %reduce-scatter.29.cloned.1.call-done = bf16[512,128]{1,0:T(8,128)(2,1)} async-done(((bf16[4096,128]{1,0:T(8,128)(2,1)}), bf16[512,128]{1,0:T(8,128)(2,1)}) %reduce-scatter.29.cloned.1.call-update) | async-done | bytes 131088 | tf_op jit(solution)/shard_map/while/body/eval_jaxpr/reduce_scatter | solution.py:324
  1330.0 65.3 %reduce-scatter.31.cloned.1.call-done = bf16[512,128]{1,0:T(8,128)(2,1)} async-done(((bf16[4096,128]{1,0:T(8,128)(2,1)}), bf16[512,128]{1,0:T(8,128)(2,1)}) %reduce-scatter.31.cloned.1.call-update) | async-done | bytes 131088 | tf_op jit(solution)/shard_map/while/body/eval_jaxpr/reduce_scatter | solution.py:327
  1433.4 52.8 %reduce-scatter.29.cloned.1.call-done = bf16[512,128]{1,0:T(8,128)(2,1)} async-done(((bf16[4096,128]{1,0:T(8,128)(2,1)}), bf16[512,128]{1,0:T(8,128)(2,1)}) %reduce-scatter.29.cloned.1.call-update) | async-done | bytes 131088 | tf_op jit(solution)/shard_map/while/body/eval_jaxpr/reduce_scatter | solution.py:324
  1487.2 65.4 %reduce-scatter.31.cloned.1.call-done = bf16[512,128]{1,0:T(8,128)(2,1)} async-done(((bf16[4096,128]{1,0:T(8,128)(2,1)}), bf16[512,128]{1,0:T(8,128)(2,1)}) %reduce-scatter.31.cloned.1.call-update) | async-done | bytes 131088 | tf_op jit(solution)/shard_map/while/body/eval_jaxpr/reduce_scatter | solution.py:327
  1590.7 53.0 %reduce-scatter.29.cloned.1.call-done = bf16[512,128]{1,0:T(8,128)(2,1)} async-done(((bf16[4096,128]{1,0:T(8,128)(2,1)}), bf16[512,128]{1,0:T(8,128)(2,1)}) %reduce-scatter.29.cloned.1.call-update) | async-done | bytes 131088 | tf_op jit(solution)/shard_map/while/body/eval_jaxpr/reduce_scatter | solution.py:324
  1644.6 65.1 %reduce-scatter.31.cloned.1.call-done = bf16[512,128]{1,0:T(8,128)(2,1)} async-done(((bf16[4096,128]{1,0:T(8,128)(2,1)}), bf16[512,128]{1,0:T(8,128)(2,1)}) %reduce-scatter.31.cloned.1.call-update) | async-done | bytes 131088 | tf_op jit(solution)/shard_map/while/body/eval_jaxpr/reduce_scatter | solution.py:327
  1747.7 52.9 %reduce-scatter.29.cloned.1.call-done = bf16[512,128]{1,0:T(8,128)(2,1)} async-done(((bf16[4096,128]{1,0:T(8,128)(2,1)}), bf16[512,128]{1,0:T(8,128)(2,1)}) %reduce-scatter.29.cloned.1.call-update) | async-done | bytes 131088 | tf_op jit(solution)/shard_map/while/body/eval_jaxpr/reduce_scatter | solution.py:324
  1801.5 65.1 %reduce-scatter.31.cloned.1.call-done = bf16[512,128]{1,0:T(8,128)(2,1)} async-done(((bf16[4096,128]{1,0:T(8,128)(2,1)}), bf16[512,128]{1,0:T(8,128)(2,1)}) %reduce-scatter.31.cloned.1.call-update) | async-done | bytes 131088 | tf_op jit(solution)/shard_map/while/body/eval_jaxpr/reduce_scatter | solution.py:327
  1980.8 12.4 all_to_all.195
  2025.4 37.8 %all-reduce.8 = (f32[2048]{0:T(1024)S(1)}, f32[2048]{0:T(1024)S(1)}, f32[2048]{0:T(1024)S(1)}, f32[2048]{0:T(1024)S(1)}) all-reduce(f32[2048]{0:T(1024)S(1)} %get-tuple-element.184, f32[2048]{0:T(1024)S(1)} %copy-done.40, f32[2048]{0:T(1024)S(1)} %get-tuple-element.180, ...), channel_id=8, replica_groups=mesh['ulysses'=4,'blk'=8] {'ulysses','blk'}, use_global_device_ids=true, to_apply=%region_35.37.clone | all-reduce | flops 8192 | bytes 65536
  2081.6 69.9 %reduce-scatter.21.cloned.1.call-done = bf16[2,2048,256]{2,1,0:T(8,128)(2,1)} async-done(((bf16[2,2048,1024]{2,1,0:T(8,128)(2,1)}), bf16[2,2048,256]{2,1,0:T(8,128)(2,1)}) %reduce-scatter.21.cloned.1.call-update) | async-done | bytes 2097168 | tf_op jit(solution)/shard_map/reduce_scatter | solution.py:261
  2155.4 70.6 %reduce-scatter.23.cloned.1.call-done = bf16[2,2048,256]{2,1,0:T(8,128)(2,1)} async-done(((bf16[2,2048,1024]{2,1,0:T(8,128)(2,1)}), bf16[2,2048,256]{2,1,0:T(8,128)(2,1)}) %reduce-scatter.23.cloned.1.call-update) | async-done | bytes 2097168 | tf_op jit(solution)/shard_map/reduce_scatter | solution.py:264
  2229.9 357.0 %reduce-scatter.19.cloned.1.call-done = f32[64,2048]{1,0:T(8,128)} async-done(((f32[2048,2048]{1,0:T(8,128)}), f32[64,2048]{1,0:T(8,128)}) %reduce-scatter.19.cloned.1.call-update) | async-done | bytes 524304 | tf_op jit(solution)/shard_map/reduce_scatter | solution.py:382
  2586.9 360.3 %reduce-scatter.15.cloned.1.call-done = f32[64,2048]{1,0:T(8,128)} async-done(((f32[2048,2048]{1,0:T(8,128)}), f32[64,2048]{1,0:T(8,128)}) %reduce-scatter.15.cloned.1.call-update) | async-done | bytes 524304 | tf_op jit(solution)/shard_map/reduce_scatter | solution.py:380
  2947.2 360.1 %reduce-scatter.13.cloned.1.call-done = f32[64,2048]{1,0:T(8,128)} async-done(((f32[2048,2048]{1,0:T(8,128)}), f32[64,2048]{1,0:T(8,128)}) %reduce-scatter.13.cloned.1.call-update) | async-done | bytes 524304 | tf_op jit(solution)/shard_map/reduce_scatter | solution.py:379
  3307.3 360.3 %reduce-scatter.17.cloned.1.call-done = f32[64,2048]{1,0:T(8,128)} async-done(((f32[2048,2048]{1,0:T(8,128)}), f32[64,2048]{1,0:T(8,128)}) %reduce-scatter.17.cloned.1.call-update) | async-done | bytes 524304 | tf_op jit(solution)/shard_map/reduce_scatter | solution.py:381
  (445 shorter events, 652.7 us)
Async XLA Ops:
  7.2 84.7 %all-gather.11.cloned.1.call-start = ((), (), s32[]{:S(2)}) async-start(), calls=%async_computation.22 | async-start | bytes 8650752 | tf_op jit(solution)/shard_map/all_gather | solution.py:113
  9.0 162.4 %all-gather.13.cloned.1.call-start = ((), (), s32[]{:S(2)}) async-start(), calls=%async_computation.23 | async-start | bytes 8650752 | tf_op jit(solution)/shard_map/all_gather | solution.py:114
  10.9 241.5 %all-gather.17.cloned.1.call-start = ((), (), s32[]{:S(2)}) async-start(), calls=%async_computation.25 | async-start | bytes 8650752 | tf_op jit(solution)/shard_map/all_gather | solution.py:115
  12.7 314.5 %all-gather.15.cloned.1.call-start = ((), (), s32[]{:S(2)}) async-start(), calls=%async_computation.24 | async-start | bytes 4718592 | tf_op jit(solution)/shard_map/all_gather | solution.py:126
  193.5 207.2 %all-gather.19.cloned.1.call-start = ((), (), s32[]{:S(2)}) async-start(), calls=%async_computation.26 | async-start | bytes 4718592 | tf_op jit(solution)/shard_map/all_gather | solution.py:127
  269.1 210.7 %all-gather.21.cloned.1.call-start = ((), (), s32[]{:S(2)}) async-start(), calls=%async_computation.27 | async-start | bytes 8650752 | tf_op jit(solution)/shard_map/all_gather | solution.py:116
  269.9 348.7 %all-gather.23.cloned.1.call-start = ((), (), s32[]{:S(2)}) async-start(), calls=%async_computation.28 | async-start | bytes 10485760 | tf_op jit(solution)/shard_map/all_gather | solution.py:143
  273.7 356.4 %all-gather.25.cloned.1.call-start = ((), (), s32[]{:S(2)}) async-start(), calls=%async_computation.29 | async-start | bytes 10485760 | tf_op jit(solution)/shard_map/all_gather | solution.py:144
  277.6 384.4 %all-gather.27.cloned.1.call-start = ((), (), s32[]{:S(2)}) async-start(), calls=%async_computation.30 | async-start | bytes 10485760 | tf_op jit(solution)/shard_map/all_gather | solution.py:145
  282.4 12.5 all-to-all-start
  466.6 12.3 all-to-all-start.3
  683.5 185.5 %all-to-all-start.5 = ((bf16[2,640,2048]{2,0,1:T(2,128)(2,1)}), bf16[2,640,2048]{2,0,1:T(2,128)(2,1)}, u32[]{:S(2)}, u32[]{:S(2)}) async-start(bf16[2,640,2048]{2,0,1:T(2,128)(2,1)} %copy.136), calls=%async_computation.7 | async-start | bytes 10485760 | tf_op jit(solution)/shard_map/all_to_all | solution.py:226
  1070.0 119.3 %all-to-all-start.7 = ((bf16[2,640,2048]{2,0,1:T(2,128)(2,1)}), bf16[2,640,2048]{2,0,1:T(2,128)(2,1)}, u32[]{:S(2)}, u32[]{:S(2)}) async-start(bf16[2,640,2048]{2,0,1:T(2,128)(2,1)} %copy.140), calls=%async_computation.9 | async-start | bytes 10485760 | tf_op jit(solution)/shard_map/all_to_all | solution.py:257
  1228.2 12.4 all-to-all-start.8
  1240.6 88.5 %reduce-scatter.29.cloned.1.call-start = ((), (), s32[]{:S(2)}) async-start(), calls=%async_computation.39 | async-start | bytes 1179648 | tf_op jit(solution)/shard_map/while/body/eval_jaxpr/reduce_scatter | solution.py:324
  1267.4 128.0 %reduce-scatter.31.cloned.1.call-start = ((), (), s32[]{:S(2)}) async-start(), calls=%async_computation.40 | async-start | bytes 1179648 | tf_op jit(solution)/shard_map/while/body/eval_jaxpr/reduce_scatter | solution.py:327
  1397.1 89.2 %reduce-scatter.29.cloned.1.call-start = ((), (), s32[]{:S(2)}) async-start(), calls=%async_computation.39 | async-start | bytes 1179648 | tf_op jit(solution)/shard_map/while/body/eval_jaxpr/reduce_scatter | solution.py:324
  1423.8 128.8 %reduce-scatter.31.cloned.1.call-start = ((), (), s32[]{:S(2)}) async-start(), calls=%async_computation.40 | async-start | bytes 1179648 | tf_op jit(solution)/shard_map/while/body/eval_jaxpr/reduce_scatter | solution.py:327
  1554.3 89.3 %reduce-scatter.29.cloned.1.call-start = ((), (), s32[]{:S(2)}) async-start(), calls=%async_computation.39 | async-start | bytes 1179648 | tf_op jit(solution)/shard_map/while/body/eval_jaxpr/reduce_scatter | solution.py:324
  1581.0 128.7 %reduce-scatter.31.cloned.1.call-start = ((), (), s32[]{:S(2)}) async-start(), calls=%async_computation.40 | async-start | bytes 1179648 | tf_op jit(solution)/shard_map/while/body/eval_jaxpr/reduce_scatter | solution.py:327
  1711.4 89.2 %reduce-scatter.29.cloned.1.call-start = ((), (), s32[]{:S(2)}) async-start(), calls=%async_computation.39 | async-start | bytes 1179648 | tf_op jit(solution)/shard_map/while/body/eval_jaxpr/reduce_scatter | solution.py:324
  1738.1 128.6 %reduce-scatter.31.cloned.1.call-start = ((), (), s32[]{:S(2)}) async-start(), calls=%async_computation.40 | async-start | bytes 1179648 | tf_op jit(solution)/shard_map/while/body/eval_jaxpr/reduce_scatter | solution.py:327
  1868.4 137.1 %reduce-scatter.27.cloned.1.call-start = ((), (), s32[]{:S(2)}) async-start(), calls=%async_computation.38 | async-start | bytes 1081344
  1868.9 208.5 %reduce-scatter.25.cloned.1.call-start = ((), (), s32[]{:S(2)}) async-start(), calls=%async_computation.37 | async-start | bytes 10485760 | tf_op jit(solution)/shard_map/reduce_scatter | solution.py:267
  1881.0 270.5 %reduce-scatter.21.cloned.1.call-start = ((), (), s32[]{:S(2)}) async-start(), calls=%async_computation.35 | async-start | bytes 10485760 | tf_op jit(solution)/shard_map/reduce_scatter | solution.py:261
  1893.2 332.8 %reduce-scatter.23.cloned.1.call-start = ((), (), s32[]{:S(2)}) async-start(), calls=%async_computation.36 | async-start | bytes 10485760 | tf_op jit(solution)/shard_map/reduce_scatter | solution.py:264
  1905.1 681.8 %reduce-scatter.19.cloned.1.call-start = ((), (), s32[]{:S(2)}) async-start(), calls=%async_computation.34 | async-start | bytes 17301504 | tf_op jit(solution)/shard_map/reduce_scatter | solution.py:382
  1915.9 12.6 all-to-all-start.9
  1928.5 12.6 all-to-all-start.10
  1932.0 1015.2 %reduce-scatter.15.cloned.1.call-start = ((), (), s32[]{:S(2)}) async-start(), calls=%async_computation.32 | async-start | bytes 17301504 | tf_op jit(solution)/shard_map/reduce_scatter | solution.py:380
  1963.1 1344.2 %reduce-scatter.13.cloned.1.call-start = ((), (), s32[]{:S(2)}) async-start(), calls=%async_computation.31 | async-start | bytes 17301504 | tf_op jit(solution)/shard_map/reduce_scatter | solution.py:379
  1979.1 1688.4 %reduce-scatter.17.cloned.1.call-start = ((), (), s32[]{:S(2)}) async-start(), calls=%async_computation.33 | async-start | bytes 17301504 | tf_op jit(solution)/shard_map/reduce_scatter | solution.py:381
  (76 other events, 2033.5 us)
Sparse Core Ops, SparseCore 0:
  11.6 80.2 all-gather.10
  95.4 75.9 all-gather.12
  175.0 77.3 all-gather.16
  255.0 72.2 all-gather.14
  329.2 71.3 all-gather.18
  404.1 75.7 all-gather.20
  481.9 57.9 all-gather.22
  542.1 59.3 all-gather.24
  603.7 58.2 all-gather.26
  1267.5 61.5 reduce-scatter.28
  1332.9 62.4 reduce-scatter.30
  1423.9 62.3 reduce-scatter.28
  1490.0 62.5 reduce-scatter.30
  1581.1 62.4 reduce-scatter.28
  1647.3 62.3 reduce-scatter.30
  1738.2 62.3 reduce-scatter.28
  1804.3 62.3 reduce-scatter.30
  1871.1 134.3 reduce-scatter.26
  2008.2 69.1 reduce-scatter.24
  2079.9 71.5 reduce-scatter.20
  2154.2 71.6 reduce-scatter.22
  2228.9 358.0 reduce-scatter.18
  2589.8 357.3 reduce-scatter.14
  2949.9 357.3 reduce-scatter.12
  3310.1 357.3 reduce-scatter.16
where the time goes:
time: 3680 us; the launch traced here: 3670 us
  waiting for transfers between devices  2500 us (68%)
  blocking collectives  525 us (14%)
  matrix products  317 us (9%)
  local copies, waits for them, and re-layouts  149 us (4%)
  other arithmetic  121 us (3%)
    reduce_scatter x1, waiting for transfers between devices, per_device(): lax.psum_scatter(grad_key_part, ('ulysses', 'blk'), scatter_dimension=0,...  360 us
    reduce_scatter x1, waiting for transfers between devices, per_device(): lax.psum_scatter(grad_value_part, ('ulysses', 'blk'), scatter_dimension=0...  360 us
    reduce_scatter x1, waiting for transfers between devices, per_device(): lax.psum_scatter(grad_query_part, ('ulysses', 'blk'), scatter_dimension=0...  360 us
    reduce_scatter x1, waiting for transfers between devices, per_device(): lax.psum_scatter(grad_out_part, ('ulysses', 'blk'), scatter_dimension=0,...  357 us
    reduce_scatter x4, waiting for transfers between devices, head_grads(): lax.psum_scatter(d_value.astype(jnp.bfloat16), 'blk', scatter_dimension=0...  261 us
    reduce_scatter x4, waiting for transfers between devices, head_grads(): lax.psum_scatter(d_key.astype(jnp.bfloat16), 'blk', scatter_dimension=0,...  211 us
    all_gather x1, blocking collectives, gather_weights(): lax.all_gather(router.astype(bfloat), ('ulysses', 'blk'), axis=0, tiled=T...  172 us
    all_to_all x1, blocking collectives, per_device(): lax.all_to_all(outgoing.reshape(experts, capacity, model_width), 'blk', s...  121 us
  transfers between devices with their start and end apart: 32, of which 29 were waited for; matrix products, arithmetic and copies ran while one was open for 9% of the time, Pallas kernels for 0%

commit v1 on v0

v1 whole, which is shorter than its diff:
```python
import math

import jax
import jax.numpy as jnp
from jax import lax
from jax.experimental import pallas as pl
from jax.experimental.pallas import tpu as pltpu
from jax.sharding import PartitionSpec as P

HEAD_DIM = 128
NORM_EPSILON = 1e-05
ROPE_BASE = 10000.0
MASKED_SCORE = -1e30
SCORE_SCALE = HEAD_DIM ** (-0.5)
LOG2_SCALE = SCORE_SCALE * math.log2(math.e)
QUERY_ROWS = 256
KEY_ROWS = 512
bfloat = jnp.bfloat16
single = jnp.float32


def norm_parts(values):
    recip_factor = lax.rsqrt(jnp.mean(values * values, axis=-1, keepdims=True) + NORM_EPSILON)
    return (values * recip_factor, recip_factor)


def norm_back(grad_in, hat_values, recip_factor):
    return recip_factor * (
        grad_in - hat_values * jnp.mean(grad_in * hat_values, axis=-1, keepdims=True)
    )


def doc_begins(doc_starts, tokens_at):
    at_or_before = doc_starts[:, None] <= tokens_at.reshape(1, -1)
    begins = jnp.max(jnp.where(at_or_before, doc_starts[:, None], 0), axis=0)
    return begins.reshape(tokens_at.shape)


def angles(position, head_size):
    half_size = head_size // 2
    frequency = ROPE_BASE ** (-(jnp.arange(half_size, dtype=jnp.float32) * 2.0 / head_size))
    turned = position.astype(jnp.float32)[:, None] * frequency[None, :]
    return (jnp.cos(turned)[:, None, :], jnp.sin(turned)[:, None, :])


def rotate(values, cosine_table, sine_table):
    half_size = values.shape[-1] // 2
    first_half = values[..., :half_size]
    second_half = values[..., half_size:]
    return jnp.concatenate(
        [
            first_half * cosine_table - second_half * sine_table,
            second_half * cosine_table + first_half * sine_table,
        ],
        axis=-1,
    )


def rotate_back(values, cosine_table, sine_table):
    return rotate(values, cosine_table, -sine_table)


def swap(values, bit):
    size = lax.axis_size("ulysses")
    return lax.ppermute(values, "ulysses", [(i, i ^ bit) for i in range(size)])


def gather_ulysses(values):
    me = lax.axis_index("ulysses")
    beyond = swap(values, 2)
    core = swap(values, 1)
    beyond_core = swap(beyond, 1)
    out = jnp.zeros((4,) + values.shape, values.dtype)
    for bit, part in enumerate((values, core, beyond, beyond_core)):
        out = lax.dynamic_update_index_in_dim(out, part, me ^ bit, 0)
    return out


def scatter_sum_ulysses(parts):
    far = swap(parts(3).astype(bfloat), 1)
    near = swap(parts(1).astype(bfloat), 1)
    across = swap((parts(2) + far.astype(single)).astype(bfloat), 2)
    return parts(0) + near.astype(single) + across.astype(single)


def sum_ulysses(values):
    return lax.psum(values, "ulysses")


def to_heads(arrays, blk_size):
    core = lax.axis_index("ulysses") % 2
    count = len(arrays)
    tokens, width = arrays[0].shape
    heads = width // HEAD_DIM
    half = tokens // 2
    stacked = jnp.stack(arrays).reshape(count, 2, half, heads, HEAD_DIM)
    stacked = jnp.transpose(stacked, (1, 0, 3, 2, 4))
    keep = lax.dynamic_index_in_dim(stacked, core, 0, keepdims=False)
    send = lax.dynamic_index_in_dim(stacked, 1 - core, 0, keepdims=False)
    got = swap(send, 1)
    both = jnp.where(
        core == 0, jnp.concatenate([keep, got], 1), jnp.concatenate([got, keep], 1)
    )
    groups = blk_size // (2 * heads)
    both = both.reshape(count, 2 * heads, groups, half // groups, HEAD_DIM)
    both = jnp.transpose(both, (1, 2, 0, 3, 4)).reshape(
        blk_size, count, half // groups, HEAD_DIM
    )
    return lax.all_to_all(both, "blk", split_axis=0, concat_axis=0, tiled=True)


def from_heads(stacked, blk_size, heads):
    core = lax.axis_index("ulysses") % 2
    count, rows = stacked.shape[1], stacked.shape[2]
    groups = blk_size // (2 * heads)
    half = rows * groups
    back = lax.all_to_all(stacked, "blk", split_axis=0, concat_axis=0, tiled=True)
    back = back.reshape(2, heads, groups, count, rows, HEAD_DIM)
    back = jnp.transpose(back, (0, 3, 2, 4, 1, 5)).reshape(2, count, half, heads, HEAD_DIM)
    keep = lax.dynamic_index_in_dim(back, core, 0, keepdims=False)
    send = lax.dynamic_index_in_dim(back, 1 - core, 0, keepdims=False)
    got = swap(send, 1)
    whole = jnp.where(
        core == 0, jnp.concatenate([keep, got], 1), jnp.concatenate([got, keep], 1)
    ).reshape(count, 2 * half, heads * HEAD_DIM)
    return [whole[i] for i in range(count)]


def join_halves(mine, other):
    core = lax.axis_index("ulysses") % 2
    return jnp.where(core == 0, jnp.stack([mine, other], 1), jnp.stack([other, mine], 1))


def head_groups(blk_size, groups):
    return [[j * groups + p for p in range(groups)] for j in range(blk_size // groups)]


def gather_keys(part, blk_size, groups):
    if groups > 1:
        part = lax.all_gather(part, "blk", axis=1, axis_index_groups=head_groups(blk_size, groups))
        part = part.reshape(blk_size, -1, HEAD_DIM)
    return join_halves(part, swap(part, 1)).reshape(-1, HEAD_DIM)


def scatter_keys(total, blk_size, groups):
    core = lax.axis_index("ulysses") % 2
    halves = total.reshape(blk_size, 2, -1, HEAD_DIM)
    keep = lax.dynamic_index_in_dim(halves, core, 1, keepdims=False)
    send = lax.dynamic_index_in_dim(halves, 1 - core, 1, keepdims=False)
    mine = (keep + swap(send.astype(bfloat), 1).astype(single)).astype(bfloat)
    if groups > 1:
        mine = mine.reshape(blk_size, groups, -1, HEAD_DIM)
        mine = lax.psum_scatter(
            mine, "blk", scatter_dimension=1, axis_index_groups=head_groups(blk_size, groups)
        )
    return mine


def dot_nt(a, b):
    return lax.dot_general(a, b, (((1,), (1,)), ((), ())), preferred_element_type=single)


def key_loops(low_ref, open_ref, close_ref, high_ref, index, step, carry):
    low, opened = low_ref[index], open_ref[index]
    closed, high = close_ref[index], high_ref[index]
    carry = lax.fori_loop(low, opened, lambda kb, c: step(kb, c, True), carry)
    carry = lax.fori_loop(opened, closed, lambda kb, c: step(kb, c, False), carry)
    return lax.fori_loop(closed, high, lambda kb, c: step(kb, c, True), carry)


def allowed(start, pos, begin):
    key_at = start + lax.broadcasted_iota(jnp.int32, (KEY_ROWS, pos.shape[1]), 0)
    return (key_at <= pos) & (key_at >= begin)


def forward_kernel(low_ref, open_ref, close_ref, high_ref, pos_ref, begin_ref, q_ref, k_ref, vt_ref, o_ref, lse_ref):
    index = pl.program_id(0)
    query = q_ref[...]
    pos, begin = pos_ref[0], begin_ref[0]
    rows = query.shape[0]

    def step(block, carry, masked):
        top, total, acc = carry
        start = pl.multiple_of(block * KEY_ROWS, KEY_ROWS)
        scores = dot_nt(k_ref[pl.ds(start, KEY_ROWS), :], query) * LOG2_SCALE
        if masked:
            scores = jnp.where(allowed(start, pos, begin), scores, MASKED_SCORE)
        new_top = jnp.maximum(top, jnp.max(scores, axis=0, keepdims=True))
        probs = jnp.exp2(scores - new_top)
        shrink = jnp.exp2(top - new_top)
        total = total * shrink + jnp.sum(probs, axis=0, keepdims=True)
        acc = acc * shrink + jnp.dot(
            vt_ref[:, pl.ds(start, KEY_ROWS)], probs.astype(bfloat), preferred_element_type=single
        )
        return new_top, total, acc

    carry = (
        jnp.full((1, rows), MASKED_SCORE, single),
        jnp.zeros((1, rows), single),
        jnp.zeros((HEAD_DIM, rows), single),
    )
    top, total, acc = key_loops(low_ref, open_ref, close_ref, high_ref, index, step, carry)
    o_ref[...] = jnp.transpose(acc / total)
    lse_ref[0] = top + jnp.log2(total)


def backward_kernel(
    low_ref, open_ref, close_ref, high_ref, pos_ref, begin_ref, lse_ref, delta_ref,
    q_ref, do_ref, k_ref, v_ref, kt_ref, dq_ref, dk_ref, dv_ref,
):
    index = pl.program_id(0)

    @pl.when(index == 0)
    def _():
        dk_ref[...] = jnp.zeros_like(dk_ref)
        dv_ref[...] = jnp.zeros_like(dv_ref)

    query, d_out = q_ref[...], do_ref[...]
    pos, begin = pos_ref[0], begin_ref[0]
    lse, delta = lse_ref[0], delta_ref[0]

    def step(block, acc, masked):
        start = pl.multiple_of(block * KEY_ROWS, KEY_ROWS)
        rows = pl.ds(start, KEY_ROWS)
        scores = dot_nt(k_ref[rows, :], query) * LOG2_SCALE
        probs = jnp.exp2(scores - lse)
        if masked:
            probs = jnp.where(allowed(start, pos, begin), probs, 0.0)
        d_probs = dot_nt(v_ref[rows, :], d_out)
        d_scores = (probs * (d_probs - delta)).astype(bfloat)
        dv_ref[rows, :] += jnp.dot(probs.astype(bfloat), d_out, preferred_element_type=single)
        dk_ref[rows, :] += jnp.dot(d_scores, query, preferred_element_type=single)
        return acc + jnp.dot(kt_ref[:, rows], d_scores, preferred_element_type=single)

    acc = jnp.zeros((HEAD_DIM, query.shape[0]), single)
    acc = key_loops(low_ref, open_ref, close_ref, high_ref, index, step, acc)
    dq_ref[...] = jnp.transpose(acc) * SCORE_SCALE


def block_bounds(pos, begin):
    first, last = jnp.min(begin, axis=1), jnp.max(begin, axis=1)
    low = first // KEY_ROWS
    high = jnp.max(pos, axis=1) // KEY_ROWS + 1
    opened = jnp.clip((last + KEY_ROWS - 1) // KEY_ROWS, low, high)
    closed = jnp.clip((jnp.min(pos, axis=1) + 1) // KEY_ROWS, opened, high)
    return low, opened, closed, high


def row_spec(rows):
    return pl.BlockSpec((rows, HEAD_DIM), lambda i, *_: (i, 0))


def line_spec(rows):
    return pl.BlockSpec((1, 1, rows), lambda i, *_: (i, 0, 0))


def whole_spec(shape):
    return pl.BlockSpec(shape, lambda i, *_: (0, 0), pipeline_mode=pl.Buffered(1))


def attention_forward(bounds, pos, begin, query, key, value_t):
    blocks, rows = pos.shape
    keys = key.shape[0]
    return pl.pallas_call(
        forward_kernel,
        grid_spec=pltpu.PrefetchScalarGridSpec(
            num_scalar_prefetch=4,
            grid=(blocks,),
            in_specs=[
                line_spec(rows), line_spec(rows), row_spec(rows),
                whole_spec((keys, HEAD_DIM)), whole_spec((HEAD_DIM, keys)),
            ],
            out_specs=[row_spec(rows), line_spec(rows)],
        ),
        out_shape=[
            jax.ShapeDtypeStruct(query.shape, single),
            jax.ShapeDtypeStruct((blocks, 1, rows), single),
        ],
        compiler_params=pltpu.CompilerParams(vmem_limit_bytes=48 << 20),
        name="attention_forward",
    )(*bounds, pos[:, None], begin[:, None], query, key, value_t)


def attention_backward(bounds, pos, begin, lse, delta, query, d_out, key, value, key_t):
    blocks, rows = pos.shape
    keys = key.shape[0]
    return pl.pallas_call(
        backward_kernel,
        grid_spec=pltpu.PrefetchScalarGridSpec(
            num_scalar_prefetch=4,
            grid=(blocks,),
            in_specs=[
                line_spec(rows), line_spec(rows), line_spec(rows), line_spec(rows),
                row_spec(rows), row_spec(rows),
                whole_spec((keys, HEAD_DIM)), whole_spec((keys, HEAD_DIM)),
                whole_spec((HEAD_DIM, keys)),
            ],
            out_specs=[
                row_spec(rows), whole_spec((keys, HEAD_DIM)), whole_spec((keys, HEAD_DIM)),
            ],
        ),
        out_shape=[
            jax.ShapeDtypeStruct(query.shape, single),
            jax.ShapeDtypeStruct(key.shape, single),
            jax.ShapeDtypeStruct(key.shape, single),
        ],
        compiler_params=pltpu.CompilerParams(vmem_limit_bytes=56 << 20),
        name="attention_backward",
    )(*bounds, pos[:, None], begin[:, None], lse, delta, query, d_out, key, value, key_t)


def per_device(
    block_input, w_query, w_key, w_value, w_out, attn_gain, ffn_gain, query_gain, key_gain,
    router, w_gate, w_up, w_down, expert_ids, slot_ids, doc_starts, cotangent,
):
    ulysses_size = lax.axis_size("ulysses")
    blk_size = lax.axis_size("blk")
    blk = lax.axis_index("blk")
    uly = lax.axis_index("ulysses")
    core = uly % 2
    own_tokens, width = block_input.shape
    picks = expert_ids.shape[1]
    experts = router.shape[1]
    capacity = 5 * own_tokens * picks // (4 * experts)
    local_experts = experts // blk_size
    blk_tokens = ulysses_size * own_tokens
    local_width = width // ulysses_size
    local_heads = local_width // HEAD_DIM
    weight_rows = w_query.shape[0]
    groups = blk_size // (2 * local_heads)

    projections = jnp.stack([w_query, w_key, w_value]).astype(bfloat)
    projections = projections.reshape(3, weight_rows, ulysses_size, local_width)
    projections = lax.all_to_all(
        jnp.transpose(projections, (2, 0, 1, 3)), "ulysses", split_axis=0, concat_axis=0, tiled=True
    )
    projections = lax.all_gather(projections, "blk", axis=0)
    projections = jnp.transpose(projections, (2, 1, 0, 3, 4)).reshape(3, width, local_width)
    w_q, w_k, w_v = projections[0], projections[1], projections[2]
    w_o = lax.all_gather(w_out.astype(bfloat), "blk", axis=0, tiled=True)
    small = jnp.concatenate(
        [jnp.stack([attn_gain, ffn_gain, query_gain, key_gain]), router.T]
    ).astype(bfloat)
    small = lax.all_gather(small, ("ulysses", "blk"), axis=1, tiled=True)
    attn_g = small[0].astype(single)
    ffn_g = small[1].astype(single)
    query_g = lax.dynamic_slice_in_dim(small[2], uly * local_width, local_width).astype(single)
    key_g = lax.dynamic_slice_in_dim(small[3], uly * local_width, local_width).astype(single)
    router_t = small[4:]

    def gather_expert(weight, axis):
        mine = weight.astype(bfloat)
        beyond = swap(mine, 2)
        near = swap(mine, 1)
        far = swap(beyond, 1)
        return jnp.concatenate([mine, near, beyond, far], axis=axis)

    expert_gate = gather_expert(w_gate, 2)
    expert_up = gather_expert(w_up, 2)
    expert_down = gather_expert(w_down, 1)

    named = expert_ids[:, :, None] == jnp.arange(experts, dtype=jnp.int32)[None, None, :]
    slot_map = jnp.sum(jnp.where(named, slot_ids[:, :, None] + 1, 0), axis=1)
    slot_map = slot_map.T.astype(single).reshape(blk_size, local_experts, own_tokens)
    slot_map = lax.all_to_all(slot_map, "blk", split_axis=0, concat_axis=0, tiled=True)
    slot_at = jnp.arange(1, capacity + 1, dtype=jnp.int32).astype(single)
    picked = jnp.transpose(slot_map, (1, 0, 2))[:, :, None, :] == slot_at[None, None, :, None]
    picked_low = picked.astype(bfloat)

    inputs = block_input.astype(single)
    hat_one, recip_one = norm_parts(inputs)
    normed = gather_ulysses((hat_one * attn_g).astype(bfloat)).reshape(blk_tokens, width)
    q_lin = jnp.dot(normed, w_q, preferred_element_type=single)
    k_lin = jnp.dot(normed, w_k, preferred_element_type=single)
    v_lin = jnp.dot(normed, w_v, preferred_element_type=single)
    squares = jnp.stack([jnp.sum(q_lin * q_lin, axis=1), jnp.sum(k_lin * k_lin, axis=1)])
    recips = lax.rsqrt(sum_ulysses(squares) / width + NORM_EPSILON)
    q_recip, k_recip = recips[0][:, None], recips[1][:, None]
    q_hat, k_hat = q_lin * q_recip, k_lin * k_recip
    blk_at = blk * blk_tokens + jnp.arange(blk_tokens, dtype=jnp.int32)
    cosine_table, sine_table = angles(blk_at - doc_begins(doc_starts, blk_at), HEAD_DIM)

    def by_heads(fun, values):
        shaped = fun(values.reshape(blk_tokens, -1, HEAD_DIM), cosine_table, sine_table)
        return shaped.reshape(blk_tokens, local_width)

    q_rot = by_heads(rotate, q_hat * query_g).astype(bfloat)
    k_rot = by_heads(rotate, k_hat * key_g).astype(bfloat)
    heads_in = to_heads([q_rot, k_rot, v_lin.astype(bfloat)], blk_size)
    query = heads_in[:, 0].reshape(-1, HEAD_DIM)
    key = gather_keys(heads_in[:, 1], blk_size, groups)
    value = gather_keys(heads_in[:, 2], blk_size, groups)
    part_rows = heads_in.shape[2]
    query_at = (
        jnp.arange(blk_size, dtype=jnp.int32)[:, None] * blk_tokens
        + core * (blk_tokens // 2)
        + blk % groups * part_rows
        + jnp.arange(part_rows, dtype=jnp.int32)[None, :]
    ).reshape(-1, QUERY_ROWS)
    query_begin = doc_begins(doc_starts, query_at)
    bounds = block_bounds(query_at, query_begin)
    head_out, lse = attention_forward(bounds, query_at, query_begin, query, key, value.T)
    attended, = from_heads(
        head_out.astype(bfloat).reshape(blk_size, 1, part_rows, HEAD_DIM), blk_size, local_heads
    )
    out_part = jnp.dot(attended, w_o, preferred_element_type=single)

    def token_rows(values):
        return lambda bits: lax.dynamic_slice_in_dim(
            values, (uly ^ bits) * own_tokens, own_tokens, 0
        )

    residual_mid = inputs + scatter_sum_ulysses(token_rows(out_part))
    hat_two, recip_two = norm_parts(residual_mid)
    ffn_in = (hat_two * ffn_g).astype(bfloat)

    ffn_all = lax.all_gather(ffn_in, "blk", axis=0)
    cot_all = lax.all_gather(cotangent, "blk", axis=0)
    logits = dot_nt(ffn_all.reshape(-1, width), router_t)
    shifted_logits = jnp.exp(logits - jnp.max(logits, axis=1, keepdims=True))
    probs_all = shifted_logits / jnp.sum(shifted_logits, axis=1, keepdims=True)
    probs_all = probs_all.reshape(blk_size, own_tokens, experts)
    router_probs = lax.dynamic_index_in_dim(probs_all, blk, 0, keepdims=False)
    local_probs = lax.dynamic_slice_in_dim(probs_all, blk * local_experts, local_experts, 2)
    gate_rows = jnp.sum(
        jnp.where(picked, jnp.transpose(local_probs, (2, 0, 1))[:, :, None, :], 0.0), axis=3
    ).reshape(local_experts, -1, 1)

    def dispatch(rows):
        return jnp.einsum("esct,std->escd", picked_low, rows, preferred_element_type=single).astype(
            bfloat
        ).reshape(local_experts, -1, width)

    def combine(rows):
        rows = rows.reshape(local_experts, blk_size, capacity, width)
        total = jnp.einsum("esct,escd->std", picked_low, rows, preferred_element_type=single)
        return lax.psum_scatter(
            total.astype(bfloat), "blk", scatter_dimension=0
        ).astype(single)

    received = dispatch(ffn_all)
    cot_rows = dispatch(cot_all).astype(single)
    d_expert_out = (gate_rows * cot_rows).astype(bfloat)
    gate_val = jnp.einsum("erd,edf->erf", received, expert_gate, preferred_element_type=single)
    up_val = jnp.einsum("erd,edf->erf", received, expert_up, preferred_element_type=single)
    sigmoid_gate = jax.nn.sigmoid(gate_val)
    hidden_low = (gate_val * sigmoid_gate * up_val).astype(bfloat)
    d_hidden = jnp.einsum("erd,efd->erf", d_expert_out, expert_down, preferred_element_type=single)
    d_gate = (d_hidden * up_val * sigmoid_gate * (1.0 + gate_val * (1.0 - sigmoid_gate))).astype(
        bfloat
    )
    d_up = (d_hidden * gate_val * sigmoid_gate).astype(bfloat)
    d_received = (
        jnp.einsum("erf,edf->erd", d_gate, expert_gate, preferred_element_type=single)
        + jnp.einsum("erf,edf->erd", d_up, expert_up, preferred_element_type=single)
    ).astype(bfloat)
    d_ffn_in = combine(d_received)
    expert_out = jnp.einsum(
        "erf,efd->erd", hidden_low, expert_down, preferred_element_type=single
    ).astype(bfloat).astype(single)
    d_gate_rows = jnp.sum(cot_rows * expert_out, axis=2).reshape(
        local_experts, blk_size, capacity, 1
    )
    d_probs = jnp.transpose(jnp.sum(jnp.where(picked, d_gate_rows, 0.0), axis=2), (1, 0, 2))
    d_probs = lax.all_to_all(d_probs, "blk", split_axis=0, concat_axis=0, tiled=True)
    d_probs = d_probs.reshape(experts, own_tokens).T
    mixed = residual_mid + combine((gate_rows * expert_out).astype(bfloat))
    grad_gate_part = jnp.einsum("erd,erf->edf", received, d_gate, preferred_element_type=single)
    grad_up_part = jnp.einsum("erd,erf->edf", received, d_up, preferred_element_type=single)
    grad_down_part = jnp.einsum(
        "erf,erd->efd", hidden_low, d_expert_out, preferred_element_type=single
    )

    def scatter_expert(total, axis):
        size = total.shape[axis] // ulysses_size
        return scatter_sum_ulysses(
            lambda bits: lax.slice_in_dim(total, bits * size, (bits + 1) * size, axis=axis)
        )

    grad_w_gate = scatter_expert(grad_gate_part, 2)
    grad_w_up = scatter_expert(grad_up_part, 2)
    grad_w_down = scatter_expert(grad_down_part, 1)

    d_logits = (
        router_probs * (d_probs - jnp.sum(router_probs * d_probs, axis=1, keepdims=True))
    ).astype(bfloat)
    grad_router_part = jnp.einsum("td,te->de", ffn_in, d_logits, preferred_element_type=single)
    d_ffn_in = d_ffn_in + jnp.dot(d_logits, router_t, preferred_element_type=single)
    grad_ffn_part = jnp.sum(d_ffn_in * hat_two, axis=0)
    d_mid = cotangent.astype(single) + norm_back(d_ffn_in * ffn_g, hat_two, recip_two)

    d_attn_out = gather_ulysses(d_mid.astype(bfloat)).reshape(blk_tokens, width)
    d_attended = dot_nt(d_attn_out, w_o).astype(bfloat)
    grad_out_part = jnp.einsum("ti,to->io", attended, d_attn_out, preferred_element_type=single)
    d_out = to_heads([d_attended], blk_size).reshape(-1, HEAD_DIM)
    delta = jnp.sum(d_out.astype(single) * head_out, axis=1).reshape(lse.shape)
    dq_head, dk_head, dv_head = attention_backward(
        bounds, query_at, query_begin, lse, delta, query, d_out, key, value, key.T
    )
    dq_part = dq_head.astype(bfloat).reshape(blk_size, part_rows, HEAD_DIM)
    dk_part = scatter_keys(dk_head * SCORE_SCALE, blk_size, groups)
    dv_part = scatter_keys(dv_head, blk_size, groups)
    dq_rows, dk_rows, dv_rows = from_heads(
        jnp.stack([dq_part, dk_part, dv_part], 1), blk_size, local_heads
    )
    dq_norm = by_heads(rotate_back, dq_rows.astype(single))
    dk_norm = by_heads(rotate_back, dk_rows.astype(single))
    gain_parts = jnp.stack(
        [jnp.sum(dq_norm * q_hat, axis=0), jnp.sum(dk_norm * k_hat, axis=0)]
    )
    dq_norm, dk_norm = dq_norm * query_g, dk_norm * key_g
    means = sum_ulysses(
        jnp.stack([jnp.sum(dq_norm * q_hat, axis=1), jnp.sum(dk_norm * k_hat, axis=1)])
    ) / width
    d_q_lin = (q_recip * (dq_norm - q_hat * means[0][:, None])).astype(bfloat)
    d_k_lin = (k_recip * (dk_norm - k_hat * means[1][:, None])).astype(bfloat)
    d_normed_part = dot_nt(d_q_lin, w_q) + dot_nt(d_k_lin, w_k) + dot_nt(dv_rows, w_v)
    d_normed = scatter_sum_ulysses(token_rows(d_normed_part))
    grad_attn_part = jnp.sum(d_normed * hat_one, axis=0)
    input_grad = d_mid + norm_back(d_normed * attn_g, hat_one, recip_one)

    def grad_projection(d_lin):
        part = jnp.einsum("td,to->do", normed, d_lin, preferred_element_type=single)
        return part.astype(bfloat).reshape(ulysses_size, blk_size, weight_rows, local_width)

    grads = jnp.stack([grad_projection(d_q_lin), grad_projection(d_k_lin), grad_projection(dv_rows)])
    grads = lax.psum_scatter(
        jnp.transpose(grads, (2, 1, 0, 3, 4)), "blk", scatter_dimension=0
    )
    grads = lax.all_to_all(grads, "ulysses", split_axis=0, concat_axis=0, tiled=True)
    grads = jnp.transpose(grads, (1, 2, 0, 3)).reshape(3, weight_rows, width).astype(single)
    grad_w_out = lax.psum_scatter(
        grad_out_part.astype(bfloat), "blk", scatter_dimension=0, tiled=True
    ).astype(single)
    gain_grads = lax.psum_scatter(gain_parts, "blk", scatter_dimension=1, tiled=True)
    both = ("ulysses", "blk")
    wide = jnp.concatenate([jnp.stack([grad_attn_part, grad_ffn_part]), grad_router_part.T])
    wide = lax.psum_scatter(wide, both, scatter_dimension=1, tiled=True)
    return (
        mixed.astype(bfloat),
        input_grad.astype(bfloat),
        grads[0],
        grads[1],
        grads[2],
        grad_w_out,
        wide[0],
        wide[1],
        gain_grads[0],
        gain_grads[1],
        wide[2:].T,
        grad_w_gate,
        grad_w_up,
        grad_w_down,
    )


def solution(mesh):
    in_specs = (
        P(("blk", "ulysses"), None),
        P(("ulysses", "blk"), None),
        P(("ulysses", "blk"), None),
        P(("ulysses", "blk"), None),
        P(("ulysses", "blk"), None),
        P(("ulysses", "blk")),
        P(("ulysses", "blk")),
        P(("ulysses", "blk")),
        P(("ulysses", "blk")),
        P(("ulysses", "blk"), None),
        P("blk", None, "ulysses"),
        P("blk", None, "ulysses"),
        P("blk", "ulysses", None),
        P(("blk", "ulysses"), None),
        P(("blk", "ulysses"), None),
        P(),
        P(("blk", "ulysses"), None),
    )
    out_specs = (
        P(("blk", "ulysses"), None),
        P(("blk", "ulysses"), None),
        P(("ulysses", "blk"), None),
        P(("ulysses", "blk"), None),
        P(("ulysses", "blk"), None),
        P(("ulysses", "blk"), None),
        P(("ulysses", "blk")),
        P(("ulysses", "blk")),
        P(("ulysses", "blk")),
        P(("ulysses", "blk")),
        P(("ulysses", "blk"), None),
        P("blk", None, "ulysses"),
        P("blk", None, "ulysses"),
        P("blk", "ulysses", None),
    )
    return jax.shard_map(
        per_device, mesh=mesh, in_specs=in_specs, out_specs=out_specs, check_vma=False
    )
```

time: 3680 us -> 1350 us (0.37)
  waiting for transfers between devices: 2500 us -> 723 us
  blocking collectives: 525 us -> 180 us
  matrix products: 317 us -> 152 us
  local copies, waits for them, and re-layouts: 149 us -> 89.9 us
  Pallas kernels: 0 us -> 46.9 us
    reduce_scatter x15 -> x3, waiting for transfers between devices: 2060 us -> 160 us  [the longest x2 160 us: combine(): lax.psum_scatter(total.astype(bfloat), 'blk', scatter_dimension=0)]
    all_gather x9 -> x4, waiting for transfers between devices: 287 us -> 12 us  [the longest x1 12 us: per_device(): projections = lax.all_gather(projections, 'blk', axis=0)]
    ppermute x0 -> x38, waiting for transfers between devices: none -> 267 us  [swap(): return lax.ppermute(values, 'ulysses', [(i, i ^ bit) for i in range(size)])]
    unnamed x18 -> x13, waiting for transfers between devices: 3.57 us -> 222 us
    all_to_all x5 -> x4, blocking collectives: 273 us -> 96.6 us  [the longest x2 61.3 us: from_heads(): lax.all_to_all(stacked, 'blk', split_axis=0, concat_axis=0, tiled=True)]
    dot_general x42 -> x19, matrix products: 203 us -> 43.2 us  [the longest x2 9.27 us: combine(): jnp.einsum('esct,escd->std', picked_low, rows, preferred_element_type=sin...]
    all_gather x1, blocking collectives: 172 us -> 70.9 us  [per_device(): small = lax.all_gather(small, ('ulysses', 'blk'), axis=1, tiled=True)]
    all_to_all x7 -> x4, waiting for transfers between devices: 153 us -> 61.7 us  [the longest x1 55.3 us: to_heads(): return lax.all_to_all(both, 'blk', split_axis=0, concat_axis=0, tiled=True)]
  transfers between devices with their start and end apart: 32 -> 52, of which waited for: 29 -> 24; matrix products, arithmetic and copies ran while one was open for 9% -> 18% of each run, Pallas kernels for 0% -> 2%
where the time goes in v1:
time: 1350 us; the launch traced here: 1340 us
  waiting for transfers between devices  723 us (54%)
  blocking collectives  180 us (13%)
  matrix products  152 us (11%)
  other arithmetic  96.2 us (7%)
  local copies, waits for them, and re-layouts  89.9 us (7%)
  Pallas kernels  46.9 us (3%)
  starting transfers between devices  33.1 us (2%)
  between operations  16.5 us (1%)
    ppermute x38, waiting for transfers between devices, swap(): return lax.ppermute(values, 'ulysses', [(i, i ^ bit) for i in range(size)])  267 us
    unnamed x13, waiting for transfers between devices  222 us
    reduce_scatter x2, waiting for transfers between devices, combine(): lax.psum_scatter(total.astype(bfloat), 'blk', scatter_dimension=0)  160 us
    all_gather x1, blocking collectives, per_device(): small = lax.all_gather(small, ('ulysses', 'blk'), axis=1, tiled=True)  70.9 us
    all_to_all x2, blocking collectives, from_heads(): lax.all_to_all(stacked, 'blk', split_axis=0, concat_axis=0, tiled=True)  61.3 us
    all_to_all x1, waiting for transfers between devices, to_heads(): return lax.all_to_all(both, 'blk', split_axis=0, concat_axis=0, tiled=True)  55.3 us
    unnamed x223, local copies, waits for them, and re-layouts  31.9 us
  transfers between devices with their start and end apart: 52, of which 24 were waited for; matrix products, arithmetic and copies ran while one was open for 18% of the time, Pallas kernels for 2%

profile of v1, /device:TPU:0, one launch (start us, length us, event | category | flops | bytes accessed | tf_op | source)
XLA Modules:
  0.0 1338.0 jit_solution(12200427196578335774)
XLA Ops:
  11.9 15.8 %all_to_all.40 = bf16[4,3,64,512]{3,2,1,0:T(8,128)(2,1)} all-to-all(bf16[4,3,64,512]{3,2,1,0:T(8,128)(2,1)S(1)} %copy.258), channel_id=1, replica_groups=mesh['ulysses'=4,'blk'=8] {'ulysses'}, dimensions={0} | all-to-all | bytes 1572864 | tf_op jit(solution)/shard_map/all_to_all | solution.py:334
  28.0 70.9 %all-gather.3 = bf16[32,64,20]{1,2,0:T(8,128)(2,1)S(1)} all-gather(bf16[1,64,20]{1,2,0:T(8,128)(2,1)S(1)} %bitcast.436), channel_id=1, replica_groups=mesh['ulysses'=4,'blk'=8] {'ulysses','blk'}, dimensions={0}, use_global_device_ids=true | all-gather | bytes 84480 | tf_op jit(solution)/shard_map/all_gather | solution.py:344
  104.7 10.6 collective-permute-done.1
  117.6 12.0 all-gather.11.cloned.1.call-done
  173.9 55.3 %all-to-all-done.1 = bf16[8,3,256,128]{3,2,1,0:T(8,128)(2,1)S(1)} async-done(((bf16[8,3,256,128]{3,2,1,0:T(8,128)(2,1)}), bf16[8,3,256,128]{3,2,1,0:T(8,128)(2,1)S(1)}, u32[]{:S(2)}, u32[]{:S(2)}) %all-to-all-start.1) | async-done | bytes 1572896 | tf_op jit(solution)/shard_map/all_to_all | solution.py:109
  241.8 21.3 %attention_forward.1 = (f32[2048,128]{1,0:T(8,128)S(1)}, f32[8,1,256]{2,1,0:T(1,128)S(1)}) custom-call(s32[8]{0:T(128)S(1)} %get-tuple-element.48.low_ref, s32[8]{0:T(128)S(1)} %get-tuple-element.46.open_ref, s32[8]{0:T(128)S(1)} %get-tuple-element.45.close_ref, s32[8]{0:T(128)S(1)} %get-tuple-element.47.high_ref, s32[8,1,256]{2,1,0:T(1,128)S(1)} %iota_add_fusion.pos_ref, ...), custom_call_target="tpu_custom_call" | custom-call | tf_op jit(solution)/shard_map/attention_forward/pallas_call | solution.py:264
  264.2 20.4 %all_to_all.41 = bf16[8,1,256,128]{3,2,1,0:T(8,128)(2,1)S(1)} all-to-all(bf16[8,1,256,128]{3,2,1,0:T(8,128)(2,1)S(1)} %bitcast.359), channel_id=1, replica_groups=mesh['ulysses'=4,'blk'=8] {'blk'}, dimensions={0} | all-to-all | bytes 1048576 | tf_op jit(solution)/shard_map/all_to_all | solution.py:117
  297.1 12.5 collective-permute-done.9
  323.0 41.5 %collective-permute-done.11 = bf16[2,2048,256]{2,1,0:T(8,128)(2,1)} collective-permute-done((bf16[2,2048,256]{2,1,0:T(8,128)(2,1)S(1)}, bf16[2,2048,256]{2,1,0:T(8,128)(2,1)}, u32[]{:S(2)}, u32[]{:S(2)}) %collective-permute-start.11) | collective-permute-done | bytes 2097184 | tf_op jit(solution)/shard_map/ppermute | solution.py:65
  368.5 40.9 %collective-permute-done.14 = bf16[2,2048,256]{2,1,0:T(8,128)(2,1)} collective-permute-done((bf16[2,2048,256]{2,1,0:T(8,128)(2,1)}, bf16[2,2048,256]{2,1,0:T(8,128)(2,1)}, u32[]{:S(2)}, u32[]{:S(2)}) %collective-permute-start.14) | collective-permute-done | bytes 2097184 | tf_op jit(solution)/shard_map/ppermute | solution.py:65
  424.4 28.2 %collective-permute-done.17 = bf16[2,256,2048]{2,1,0:T(8,128)(2,1)} collective-permute-done((bf16[2,256,2048]{2,1,0:T(8,128)(2,1)}, bf16[2,256,2048]{2,1,0:T(8,128)(2,1)}, u32[]{:S(2)}, u32[]{:S(2)}) %collective-permute-start.17) | collective-permute-done | bytes 2097184 | tf_op jit(solution)/shard_map/ppermute | solution.py:65
  452.6 9.3 fusion.29
  462.0 10.6 multiply_convert_fusion.2
  475.4 11.2 fusion.1
  487.7 11.4 fusion.2
  499.0 12.8 multiply_convert_fusion.1
  511.9 11.3 fusion.27
  523.1 12.0 add_convert_fusion
  551.0 76.9 %reduce-scatter.15.cloned.1.call-done = bf16[1,128,2048]{2,1,0:T(8,128)(2,1)} async-done(((bf16[8,128,2048]{2,1,0:T(8,128)(2,1)}), bf16[1,128,2048]{2,1,0:T(8,128)(2,1)}) %reduce-scatter.15.cloned.1.call-update) | async-done | bytes 524304 | tf_op jit(solution)/shard_map/reduce_scatter | solution.py:437
  631.7 12.2 collective-permute-done.20
  650.5 19.5 %all_to_all.42 = bf16[8,1,256,128]{3,2,1,0:T(8,128)(2,1)S(1)} all-to-all(bf16[8,1,256,128]{3,2,1,0:T(8,128)(2,1)S(1)} %maximum_select_fusion.5), channel_id=1, replica_groups=mesh['ulysses'=4,'blk'=8] {'blk'}, dimensions={0} | all-to-all | bytes 1048576 | tf_op jit(solution)/shard_map/all_to_all | solution.py:109
  671.0 25.5 %attention_backward.1 = (f32[2048,128]{1,0:T(8,128)}, f32[4096,128]{1,0:T(8,128)}, f32[4096,128]{1,0:T(8,128)}) custom-call(s32[8]{0:T(128)} %copy-done.10, s32[8]{0:T(128)} %copy-done.8, s32[8]{0:T(128)} %copy-done.7, s32[8]{0:T(128)} %copy-done.9, s32[8,1,256]{2,1,0:T(1,128)} %copy-done.5, s32[8,1,256]{2,1,0:T(1,128)} %bitcast.328, ...), custom_call_target="tpu_custom_call" | custom-call | tf_op jit(solution)/shard_map/attention_backward/pallas_call | solution.py:287
  702.4 40.9 %all_to_all.43 = bf16[8,3,256,128]{3,2,1,0:T(8,128)(2,1)S(1)} all-to-all(bf16[8,3,256,128]{3,2,1,0:T(8,128)(2,1)S(1)} %pad_maximum_fusion.4), channel_id=1, replica_groups=mesh['ulysses'=4,'blk'=8] {'blk'}, dimensions={0} | all-to-all | bytes 3145728 | tf_op jit(solution)/shard_map/all_to_all | solution.py:117
  788.4 15.1 %fusion.97 = (bf16[2,2048,1024]{2,1,0:T(8,128)(2,1)}, f32[2,2048,1024]{2,1,0:T(8,128)}) fusion(bf16[2,640,2048]{2,1,0:T(8,128)(2,1)} %bitcast.331, bf16[2,640,1024]{2,1,0:T(8,128)(2,1)} %get-tuple-element.49), kind=kOutput, calls=%fused_computation.263 | convolution fusion | flops 5372903424 | bytes 33030144 | tf_op jit(solution)/shard_map/erd,erf->edf/dot_general | solution.py:468
  808.2 15.0 %fusion.98 = (bf16[2,2048,1024]{2,1,0:T(8,128)(2,1)}, f32[2,2048,1024]{2,1,0:T(8,128)}) fusion(bf16[2,640,2048]{2,1,0:T(8,128)(2,1)} %bitcast.332, bf16[2,640,1024]{2,1,0:T(8,128)(2,1)} %copy-done.43), kind=kOutput, calls=%fused_computation.264 | convolution fusion | flops 5372903424 | bytes 33030144 | tf_op jit(solution)/shard_map/erd,erf->edf/dot_general | solution.py:469
  828.3 12.1 fusion.99
  865.8 37.2 %collective-permute-done.31 = bf16[2,2048,256]{2,1,0:T(8,128)(2,1)} collective-permute-done((bf16[2,2048,256]{2,1,0:T(8,128)(2,1)}, bf16[2,2048,256]{2,1,0:T(8,128)(2,1)}, u32[]{:S(2)}, u32[]{:S(2)}) %collective-permute-start.31) | collective-permute-done | bytes 2097184 | tf_op jit(solution)/shard_map/ppermute | solution.py:65
  913.9 33.9 %collective-permute-done.34 = bf16[2,2048,256]{2,1,0:T(8,128)(2,1)S(1)} collective-permute-done((bf16[2,2048,256]{2,1,0:T(8,128)(2,1)S(1)}, bf16[2,2048,256]{2,1,0:T(8,128)(2,1)S(1)}, u32[]{:S(2)}, u32[]{:S(2)}) %collective-permute-start.34) | collective-permute-done | bytes 2097184 | tf_op jit(solution)/shard_map/ppermute | solution.py:65
  954.2 38.6 %collective-permute-done.37 = bf16[2,256,2048]{2,1,0:T(8,128)(2,1)S(1)} collective-permute-done((bf16[2,256,2048]{2,1,0:T(8,128)(2,1)S(1)}, bf16[2,256,2048]{2,1,0:T(8,128)(2,1)S(1)}, u32[]{:S(2)}, u32[]{:S(2)}) %collective-permute-start.37) | collective-permute-done | bytes 2097184 | tf_op jit(solution)/shard_map/ppermute | solution.py:65
  1007.4 86.4 %all-reduce.3.cloned.1.call-done = bf16[8,4,3,64,512]{4,3,0,1,2:T(8,128)(2,1)} async-done(((bf16[8,4,3,64,512]{4,3,0,1,2:T(8,128)(2,1)}), bf16[8,4,3,64,512]{4,3,0,1,2:T(8,128)(2,1)}) %all-reduce.3.cloned.1.call-update) | async-done | bytes 6291472
  1101.1 83.5 %reduce-scatter.13.cloned.1.call-done = bf16[1,128,2048]{2,1,0:T(8,128)(2,1)} async-done(((bf16[8,128,2048]{2,1,0:T(8,128)(2,1)}), bf16[1,128,2048]{2,1,0:T(8,128)(2,1)}) %reduce-scatter.13.cloned.1.call-update) | async-done | bytes 524304 | tf_op jit(solution)/shard_map/reduce_scatter | solution.py:437
  1187.4 134.3 %reduce-scatter.19.cloned.1.call-done = f32[64,18]{1,0:T(8,128)} async-done(((f32[2048,18]{1,0:T(8,128)}), f32[64,18]{1,0:T(8,128)}) %reduce-scatter.19.cloned.1.call-update) | async-done | bytes 4624
  (498 shorter events, 282.6 us)
Async XLA Ops:
  7.2 122.4 %all-gather.11.cloned.1.call-start = ((), (), s32[]{:S(2)}) async-start(), calls=%async_computation.17 | async-start | bytes 7077888 | tf_op jit(solution)/shard_map/all_gather | solution.py:337
  27.7 257.2 %all-gather.9.cloned.1.call-start = ((), (), s32[]{:S(2)}) async-start(), calls=%async_computation.13 | async-start | bytes 2359296 | tf_op jit(solution)/shard_map/all_gather | solution.py:340
  168.8 60.4 %all-to-all-start.1 = ((bf16[8,3,256,128]{3,2,1,0:T(8,128)(2,1)}), bf16[8,3,256,128]{3,2,1,0:T(8,128)(2,1)S(1)}, u32[]{:S(2)}, u32[]{:S(2)}) async-start(bf16[8,3,256,128]{3,2,1,0:T(8,128)(2,1)} %copy.268), calls=%async_computation.1 | async-start | bytes 3145728 | tf_op jit(solution)/shard_map/all_to_all | solution.py:109
  172.7 236.7 %all-gather.15.cloned.1.call-start = ((), (), s32[]{:S(2)}) async-start(), calls=%async_computation.19 | async-start | bytes 4718592 | tf_op jit(solution)/shard_map/all_gather | solution.py:418
  173.5 244.5 %all-gather.13.cloned.1.call-start = ((), (), s32[]{:S(2)}) async-start(), calls=%async_computation.18 | async-start | bytes 4718592 | tf_op jit(solution)/shard_map/all_gather | solution.py:417
  315.7 48.7 %collective-permute-start.11 = (bf16[2,2048,256]{2,1,0:T(8,128)(2,1)S(1)}, bf16[2,2048,256]{2,1,0:T(8,128)(2,1)}, u32[]{:S(2)}, u32[]{:S(2)}) collective-permute-start(bf16[2,2048,256]{2,1,0:T(8,128)(2,1)S(1)} %convert_element_type.332), channel_id=1, source_target_pairs={{0,16},{8,24},{16,0},{24,8},{1,17},{9,25},{17,1},{25,9},{2,18},{10... | collective-permute-start | bytes 6291464 | tf_op jit(solution)/shard_map/ppermute | solution.py:65
  318.8 90.6 %collective-permute-start.14 = (bf16[2,2048,256]{2,1,0:T(8,128)(2,1)}, bf16[2,2048,256]{2,1,0:T(8,128)(2,1)}, u32[]{:S(2)}, u32[]{:S(2)}) collective-permute-start(bf16[2,2048,256]{2,1,0:T(8,128)(2,1)} %convert_element_type.333), channel_id=1, source_target_pairs={{0,16},{8,24},{16,0},{24,8},{1,17},{9,25},{17,1},{25,9},{2,18},{10... | collective-permute-start | bytes 6291464 | tf_op jit(solution)/shard_map/ppermute | solution.py:65
  319.6 104.3 %collective-permute-start.10 = (bf16[2,2048,256]{2,1,0:T(8,128)(2,1)S(1)}, bf16[2,2048,256]{2,1,0:T(8,128)(2,1)}, u32[]{:S(2)}, u32[]{:S(2)}) collective-permute-start(bf16[2,2048,256]{2,1,0:T(8,128)(2,1)S(1)} %convert_element_type.332), channel_id=1, source_target_pairs={{0,8},{8,0},{16,24},{24,16},{1,9},{9,1},{17,25},{25,17},{2,10},{10... | collective-permute-start | bytes 6291464 | tf_op jit(solution)/shard_map/ppermute | solution.py:65
  319.6 142.4 %collective-permute-start.13 = (bf16[2,2048,256]{2,1,0:T(8,128)(2,1)}, bf16[2,2048,256]{2,1,0:T(8,128)(2,1)}, u32[]{:S(2)}, u32[]{:S(2)}) collective-permute-start(bf16[2,2048,256]{2,1,0:T(8,128)(2,1)} %convert_element_type.333), channel_id=1, source_target_pairs={{0,8},{8,0},{16,24},{24,16},{1,9},{9,1},{17,25},{25,17},{2,10},{10... | collective-permute-start | bytes 6291464 | tf_op jit(solution)/shard_map/ppermute | solution.py:65
  321.8 130.9 %collective-permute-start.17 = (bf16[2,256,2048]{2,1,0:T(8,128)(2,1)}, bf16[2,256,2048]{2,1,0:T(8,128)(2,1)}, u32[]{:S(2)}, u32[]{:S(2)}) collective-permute-start(bf16[2,256,2048]{2,1,0:T(8,128)(2,1)} %convert_element_type.335), channel_id=1, source_target_pairs={{0,16},{8,24},{16,0},{24,8},{1,17},{9,25},{17,1},{25,9},{2,18},{10... | collective-permute-start | bytes 6291464 | tf_op jit(solution)/shard_map/ppermute | solution.py:65
  364.5 88.2 %collective-permute-start.12 = (bf16[2,2048,256]{2,1,0:T(8,128)(2,1)}, bf16[2,2048,256]{2,1,0:T(8,128)(2,1)}, u32[]{:S(2)}, u32[]{:S(2)}) collective-permute-start(bf16[2,2048,256]{2,1,0:T(8,128)(2,1)} %collective-permute-done.11), channel_id=1, source_target_pairs={{0,8},{8,0},{16,24},{24,16},{1,9},{9,1},{17,25},{25,17},{2,10},{10... | collective-permute-start | bytes 6291464 | tf_op jit(solution)/shard_map/ppermute | solution.py:65
  365.1 44.3 %all-to-all-start.3 = ((f32[8,2,128]{2,1,0:T(2,128)}), f32[8,2,128]{2,1,0:T(2,128)S(1)}, u32[]{:S(2)}, u32[]{:S(2)}) async-start(f32[8,2,128]{2,1,0:T(2,128)} %bitcast.57), calls=%async_computation.3 | async-start | bytes 16384 | tf_op jit(solution)/shard_map/all_to_all | solution.py:365
  368.5 259.4 %reduce-scatter.15.cloned.1.call-start = ((), (), s32[]{:S(2)}) async-start(), calls=%async_computation.15 | async-start | bytes 4718592 | tf_op jit(solution)/shard_map/reduce_scatter | solution.py:437
  409.4 52.6 %collective-permute-start.15 = (bf16[2,2048,256]{2,1,0:T(8,128)(2,1)}, bf16[2,2048,256]{2,1,0:T(8,128)(2,1)}, u32[]{:S(2)}, u32[]{:S(2)}) collective-permute-start(bf16[2,2048,256]{2,1,0:T(8,128)(2,1)} %collective-permute-done.14), channel_id=1, source_target_pairs={{0,8},{8,0},{16,24},{24,16},{1,9},{9,1},{17,25},{25,17},{2,10},{10... | collective-permute-start | bytes 6291464 | tf_op jit(solution)/shard_map/ppermute | solution.py:65
  423.9 48.7 %collective-permute-start.16 = (bf16[2,256,2048]{2,1,0:T(8,128)(2,1)}, bf16[2,256,2048]{2,1,0:T(8,128)(2,1)S(1)}, u32[]{:S(2)}, u32[]{:S(2)}) collective-permute-start(bf16[2,256,2048]{2,1,0:T(8,128)(2,1)} %convert_element_type.335), channel_id=1, source_target_pairs={{0,8},{8,0},{16,24},{24,16},{1,9},{9,1},{17,25},{25,17},{2,10},{10... | collective-permute-start | bytes 6291464 | tf_op jit(solution)/shard_map/ppermute | solution.py:65
  452.6 20.0 %collective-permute-start.18 = (bf16[2,256,2048]{2,1,0:T(8,128)(2,1)}, bf16[2,256,2048]{2,1,0:T(8,128)(2,1)S(1)}, u32[]{:S(2)}, u32[]{:S(2)}) collective-permute-start(bf16[2,256,2048]{2,1,0:T(8,128)(2,1)} %collective-permute-done.17), channel_id=1, source_target_pairs={{0,8},{8,0},{16,24},{24,16},{1,9},{9,1},{17,25},{25,17},{2,10},{10... | collective-permute-start | bytes 6291464 | tf_op jit(solution)/shard_map/ppermute | solution.py:65
  544.5 454.0 %reduce-scatter.17.cloned.1.call-start = ((), (), s32[]{:S(2)}) async-start(), calls=%async_computation.16 | async-start | bytes 2359296 | tf_op jit(solution)/shard_map/reduce_scatter | solution.py:532
  747.7 252.6 %reduce-scatter.21.cloned.1.call-start = ((), (), s32[]{:S(2)}) async-start(), calls=%async_computation.21 | async-start | bytes 294912
  782.0 311.8 %all-reduce.3.cloned.1.call-start = ((), (), s32[]{:S(2)}) async-start(), calls=%async_computation.22 | async-start | bytes 12582912
  788.2 396.4 %reduce-scatter.13.cloned.1.call-start = ((), (), s32[]{:S(2)}) async-start(), calls=%async_computation.14 | async-start | bytes 4718592 | tf_op jit(solution)/shard_map/reduce_scatter | solution.py:437
  808.2 41.2 %collective-permute-start.30 = (bf16[2,2048,256]{2,1,0:T(8,128)(2,1)}, bf16[2,2048,256]{2,1,0:T(8,128)(2,1)}, u32[]{:S(2)}, u32[]{:S(2)}) collective-permute-start(bf16[2,2048,256]{2,1,0:T(8,128)(2,1)} %get-tuple-element.56), channel_id=1, source_target_pairs={{0,8},{8,0},{16,24},{24,16},{1,9},{9,1},{17,25},{25,17},{2,10},{10... | collective-permute-start | bytes 6291464 | tf_op jit(solution)/shard_map/ppermute | solution.py:65
  827.9 28.2 %collective-permute-start.33 = (bf16[2,2048,256]{2,1,0:T(8,128)(2,1)}, bf16[2,2048,256]{2,1,0:T(8,128)(2,1)}, u32[]{:S(2)}, u32[]{:S(2)}) collective-permute-start(bf16[2,2048,256]{2,1,0:T(8,128)(2,1)} %get-tuple-element.54), channel_id=1, source_target_pairs={{0,8},{8,0},{16,24},{24,16},{1,9},{9,1},{17,25},{25,17},{2,10},{10... | collective-permute-start | bytes 6291464 | tf_op jit(solution)/shard_map/ppermute | solution.py:65
  843.8 477.9 %reduce-scatter.19.cloned.1.call-start = ((), (), s32[]{:S(2)}) async-start(), calls=%async_computation.20 | async-start | bytes 1081344
  854.2 48.8 %collective-permute-start.31 = (bf16[2,2048,256]{2,1,0:T(8,128)(2,1)}, bf16[2,2048,256]{2,1,0:T(8,128)(2,1)}, u32[]{:S(2)}, u32[]{:S(2)}) collective-permute-start(bf16[2,2048,256]{2,1,0:T(8,128)(2,1)} %fusion.11), channel_id=1, source_target_pairs={{0,16},{8,24},{16,0},{24,8},{1,17},{9,25},{17,1},{25,9},{2,18},{10... | collective-permute-start | bytes 6291464 | tf_op jit(solution)/shard_map/ppermute | solution.py:65
  855.9 58.0 %collective-permute-start.32 = (bf16[2,2048,256]{2,1,0:T(8,128)(2,1)}, bf16[2,2048,256]{2,1,0:T(8,128)(2,1)S(1)}, u32[]{:S(2)}, u32[]{:S(2)}) collective-permute-start(bf16[2,2048,256]{2,1,0:T(8,128)(2,1)} %get-tuple-element.53), channel_id=1, source_target_pairs={{0,8},{8,0},{16,24},{24,16},{1,9},{9,1},{17,25},{25,17},{2,10},{10... | collective-permute-start | bytes 6291464 | tf_op jit(solution)/shard_map/ppermute | solution.py:65
  856.1 98.1 %collective-permute-start.35 = (bf16[2,256,2048]{2,1,0:T(8,128)(2,1)}, bf16[2,256,2048]{2,1,0:T(8,128)(2,1)S(1)}, u32[]{:S(2)}, u32[]{:S(2)}) collective-permute-start(bf16[2,256,2048]{2,1,0:T(8,128)(2,1)} %get-tuple-element.51), channel_id=1, source_target_pairs={{0,8},{8,0},{16,24},{24,16},{1,9},{9,1},{17,25},{25,17},{2,10},{10... | collective-permute-start | bytes 6291464 | tf_op jit(solution)/shard_map/ppermute | solution.py:65
  860.1 87.7 %collective-permute-start.34 = (bf16[2,2048,256]{2,1,0:T(8,128)(2,1)S(1)}, bf16[2,2048,256]{2,1,0:T(8,128)(2,1)S(1)}, u32[]{:S(2)}, u32[]{:S(2)}) collective-permute-start(bf16[2,2048,256]{2,1,0:T(8,128)(2,1)S(1)} %fusion.9), channel_id=1, source_target_pairs={{0,16},{8,24},{16,0},{24,8},{1,17},{9,25},{17,1},{25,9},{2,18},{10... | collective-permute-start | bytes 6291464 | tf_op jit(solution)/shard_map/ppermute | solution.py:65
  864.6 128.2 %collective-permute-start.37 = (bf16[2,256,2048]{2,1,0:T(8,128)(2,1)S(1)}, bf16[2,256,2048]{2,1,0:T(8,128)(2,1)S(1)}, u32[]{:S(2)}, u32[]{:S(2)}) collective-permute-start(bf16[2,256,2048]{2,1,0:T(8,128)(2,1)S(1)} %fusion.7), channel_id=1, source_target_pairs={{0,16},{8,24},{16,0},{24,8},{1,17},{9,25},{17,1},{25,9},{2,18},{10... | collective-permute-start | bytes 6291464 | tf_op jit(solution)/shard_map/ppermute | solution.py:65
  913.8 39.0 %collective-permute-start.27 = (bf16[128,2048]{1,0:T(8,128)(2,1)S(1)}, bf16[128,2048]{1,0:T(8,128)(2,1)S(1)}, u32[]{:S(2)}, u32[]{:S(2)}) collective-permute-start(bf16[128,2048]{1,0:T(8,128)(2,1)S(1)} %get-tuple-element.61), channel_id=1, source_target_pairs={{0,8},{8,0},{16,24},{24,16},{1,9},{9,1},{17,25},{25,17},{2,10},{10... | collective-permute-start | bytes 1572872 | tf_op jit(solution)/shard_map/ppermute | solution.py:65
  952.8 49.6 %collective-permute-start.26 = (bf16[128,2048]{1,0:T(8,128)(2,1)S(1)}, bf16[128,2048]{1,0:T(8,128)(2,1)S(1)}, u32[]{:S(2)}, u32[]{:S(2)}) collective-permute-start(bf16[128,2048]{1,0:T(8,128)(2,1)S(1)} %get-tuple-element.60), channel_id=1, source_target_pairs={{0,8},{8,0},{16,24},{24,16},{1,9},{9,1},{17,25},{25,17},{2,10},{10... | collective-permute-start | bytes 1572872 | tf_op jit(solution)/shard_map/ppermute | solution.py:65
  953.0 50.3 %collective-permute-start.28 = (bf16[128,2048]{1,0:T(8,128)(2,1)S(1)}, bf16[128,2048]{1,0:T(8,128)(2,1)}, u32[]{:S(2)}, u32[]{:S(2)}) collective-permute-start(bf16[128,2048]{1,0:T(8,128)(2,1)S(1)} %add_convert_fusion.1), channel_id=1, source_target_pairs={{0,16},{8,24},{16,0},{24,8},{1,17},{9,25},{17,1},{25,9},{2,18},{10... | collective-permute-start | bytes 1572872 | tf_op jit(solution)/shard_map/ppermute | solution.py:65
  1096.6 228.7 %all-to-all-start.7 = ((bf16[4,3,64,512]{3,2,1,0:T(8,128)(2,1)}), bf16[4,3,64,512]{3,2,1,0:T(8,128)(2,1)}, u32[]{:S(2)}, u32[]{:S(2)}) async-start(bf16[4,3,64,512]{3,2,1,0:T(8,128)(2,1)} %copy.295), calls=%async_computation.9 | async-start | bytes 1572864 | tf_op jit(solution)/shard_map/all_to_all | solution.py:530
  (120 other events, 2974.2 us)
Sparse Core Ops, SparseCore 0:
  27.8 101.6 all-gather.10
  132.3 49.2 all-gather.8
  183.7 97.0 all-gather.14
  313.3 72.0 all-gather.12
  541.1 86.6 reduce-scatter.14
  747.8 66.5 reduce-scatter.16
  818.7 60.2 reduce-scatter.20
  883.2 210.5 all-reduce.2
  1097.5 87.0 reduce-scatter.12
  1186.8 134.9 reduce-scatter.18

commit v2 on v1

v2 whole, which is shorter than its diff:
```python
import math

import jax
import jax.numpy as jnp
from jax import lax
from jax.experimental import pallas as pl
from jax.experimental.pallas import tpu as pltpu
from jax.sharding import PartitionSpec as P

HEAD_DIM = 128
NORM_EPSILON = 1e-05
ROPE_BASE = 10000.0
MASKED_SCORE = -1e30
SCORE_SCALE = HEAD_DIM ** (-0.5)
LOG2_SCALE = SCORE_SCALE * math.log2(math.e)
QUERY_ROWS = 256
HALF_ROWS = 256
KEY_ROWS = 512
BLK = ("far", "near")
PLANE = ("ulysses", "near")
bfloat = jnp.bfloat16
single = jnp.float32


def norm_parts(values):
    recip_factor = lax.rsqrt(jnp.mean(values * values, axis=-1, keepdims=True) + NORM_EPSILON)
    return (values * recip_factor, recip_factor)


def norm_back(grad_in, hat_values, recip_factor):
    return recip_factor * (
        grad_in - hat_values * jnp.mean(grad_in * hat_values, axis=-1, keepdims=True)
    )


def doc_begins(doc_starts, tokens_at):
    at_or_before = doc_starts[:, None] <= tokens_at.reshape(1, -1)
    begins = jnp.max(jnp.where(at_or_before, doc_starts[:, None], 0), axis=0)
    return begins.reshape(tokens_at.shape)


def angles(position, head_size):
    half_size = head_size // 2
    frequency = ROPE_BASE ** (-(jnp.arange(half_size, dtype=jnp.float32) * 2.0 / head_size))
    turn = position.astype(jnp.float32)[:, None] * frequency[None, :]
    cosine, sine = jnp.cos(turn), jnp.sin(turn)
    return jnp.concatenate([cosine, cosine], 1), jnp.concatenate([-sine, sine], 1)


def swap(values, bit, axis="ulysses"):
    size = lax.axis_size(axis)
    return lax.ppermute(values, axis, [(i, i ^ bit) for i in range(size)])


def gather_plane(values):
    me, side = lax.axis_index("ulysses"), lax.axis_index("near")
    near = swap(values, 1, "near")
    beyond = swap(values, 2)
    corner = swap(beyond, 1, "near")
    out = jnp.zeros((2, 4) + values.shape, values.dtype)
    for other, bit, part in ((0, 0, values), (0, 2, beyond), (1, 0, near), (1, 2, corner)):
        for core, piece in ((0, part), (1, swap(part, 1))):
            place = (side ^ other, me ^ bit ^ core) + (0,) * values.ndim
            out = lax.dynamic_update_slice(out, piece[None, None], place)
    return out


def line_steps(size):
    for step in range(1, size):
        up = [(i, i + 1) for i in range(step - 1, size - 1)]
        yield up, [(size - 1 - i, size - 1 - j) for i, j in up]


def gather_line(values, axis):
    size = lax.axis_size("far")
    if size > 4:
        return lax.all_gather(values, "far", axis=axis)
    at = lax.axis_index("far")
    below, above, parts = values, values, []
    for step, (up, down) in enumerate(line_steps(size), 1):
        below, above = lax.ppermute(below, "far", up), lax.ppermute(above, "far", down)
        parts = [(at - step, below), (at + step, above)] + parts
    shape = values.shape[:axis] + (size,) + values.shape[axis:]
    out = jnp.zeros(shape, values.dtype)
    for place, part in parts + [(at, values)]:
        out = lax.dynamic_update_index_in_dim(out, part, jnp.clip(place, 0, size - 1), axis)
    return out


def gather_ulysses(values):
    me = lax.axis_index("ulysses")
    beyond = swap(values, 2)
    core = swap(values, 1)
    beyond_core = swap(beyond, 1)
    out = jnp.zeros((4,) + values.shape, values.dtype)
    for bit, part in enumerate((values, core, beyond, beyond_core)):
        out = lax.dynamic_update_index_in_dim(out, part, me ^ bit, 0)
    return out


def scatter_sum_ulysses(parts, kind=bfloat):
    far = swap(parts(3).astype(kind), 1)
    near = swap(parts(1).astype(kind), 1)
    across = swap((parts(2) + far.astype(single)).astype(kind), 2)
    return parts(0) + near.astype(single) + across.astype(single)


def scatter_sum_plane(parts, beside):
    kept, sent = [], []
    for bits in (0, 2):
        mine, other = parts(bits)
        core_mine, core_other = parts(bits ^ 1)
        got = swap(jnp.stack([core_mine, core_other]).astype(bfloat), 1).astype(single)
        kept.append(mine + got[0])
        sent.append(other + got[1])
    got = swap(jnp.stack(sent).astype(bfloat), 1, "near").astype(single)
    got, beside = tie(got, beside)
    across = swap((kept[1] + got[1]).astype(bfloat), 2)
    return kept[0] + got[0] + across.astype(single), beside


def gather_small(values):
    count, size = values.shape
    blk_size = lax.axis_size(BLK)
    out = lax.all_to_all(
        jnp.broadcast_to(values, (blk_size, count, size)), BLK, split_axis=0, concat_axis=0, tiled=True
    )
    out = jnp.transpose(out, (1, 0, 2)).reshape(count, blk_size * size)
    return jnp.transpose(gather_ulysses(out), (1, 0, 2)).reshape(count, -1)


def scatter_sum_blk_small(values):
    count, blk_size = values.shape[0], lax.axis_size(BLK)
    parts = jnp.transpose(values.reshape(count, blk_size, -1), (1, 0, 2))
    parts = lax.all_to_all(parts, BLK, split_axis=0, concat_axis=0, tiled=True)
    return jnp.sum(parts, axis=0)


def tie(*values):
    return lax.optimization_barrier(values)


def sum_plane(values):
    values = values + swap(values, 1)
    values = values + swap(values, 2)
    return values + swap(values, 1, "near")


def swap_halves(values, core):
    got = swap(lax.dynamic_index_in_dim(values, 1 - core, 0, keepdims=False), 1)
    return lax.dynamic_update_index_in_dim(values, got, 1 - core, 0)


def line_to_heads(split, far_size):
    count, rows = split.shape[4:6]
    both = swap_halves(split, lax.axis_index("ulysses") % 2)
    both = both.reshape(far_size, 2, count, rows, HEAD_DIM)
    both = lax.all_to_all(both, "far", split_axis=0, concat_axis=0, tiled=True)
    return both.reshape(2 * far_size, count, rows, HEAD_DIM)


def line_from_heads(stacked, far_size):
    count, rows = stacked.shape[1:3]
    back = stacked.reshape(far_size, 2, count, rows, HEAD_DIM)
    back = lax.all_to_all(back, "far", split_axis=0, concat_axis=0, tiled=True)
    back = back.reshape(2, 2, far_size // 4, 2, count, rows, HEAD_DIM)
    return swap_halves(back, lax.axis_index("ulysses") % 2)


def blk_to_heads(values, blk_size):
    core = lax.axis_index("ulysses") % 2
    groups = blk_size // 8
    rows = values.shape[0] // (2 * groups)
    split = values.reshape(2, groups, rows, 2, 2, HEAD_DIM)
    split = jnp.transpose(split, (0, 4, 1, 3, 2, 5))
    both = swap_halves(split, core).reshape(blk_size, rows, HEAD_DIM)
    return lax.all_to_all(both, BLK, split_axis=0, concat_axis=0, tiled=True)


def blk_from_heads(stacked, blk_size):
    core = lax.axis_index("ulysses") % 2
    groups, rows = blk_size // 8, stacked.shape[1]
    back = lax.all_to_all(stacked, BLK, split_axis=0, concat_axis=0, tiled=True)
    whole = swap_halves(back.reshape(2, 2, groups, 2, rows, HEAD_DIM), core)
    whole = jnp.transpose(whole, (0, 2, 4, 3, 1, 5))
    return whole.reshape(2 * groups * rows, 4 * HEAD_DIM)


def head_groups(far_size, groups):
    return [[j * groups + p for p in range(groups)] for j in range(far_size // groups)]


def dot_nt(a, b):
    return lax.dot_general(a, b, (((1,), (1,)), ((), ())), preferred_element_type=single)


def key_loops(low_ref, open_ref, close_ref, high_ref, index, step, carry):
    low, opened = low_ref[index], open_ref[index]
    closed, high = close_ref[index], high_ref[index]
    carry = lax.fori_loop(low, opened, lambda kb, c: step(kb, c, True), carry)
    carry = lax.fori_loop(opened, closed, lambda kb, c: step(kb, c, False), carry)
    return lax.fori_loop(closed, high, lambda kb, c: step(kb, c, True), carry)


def allowed(start, pos, begin):
    key_at = start + lax.broadcasted_iota(jnp.int32, (KEY_ROWS, pos.shape[1]), 0)
    return (key_at <= pos) & (key_at >= begin)


def load_keys(core, mine_ref, other_ref, at, store):
    for blk in range(mine_ref.shape[0]):
        start = 2 * blk * HALF_ROWS
        store(pl.multiple_of(start + core * HALF_ROWS, HALF_ROWS), mine_ref[blk, at])
        store(pl.multiple_of(start + (1 - core) * HALF_ROWS, HALF_ROWS), other_ref[blk, at - mine_ref.shape[1] + 2])


def forward_kernel(
    core_ref, low_ref, open_ref, close_ref, high_ref,
    pos_ref, begin_ref, q_ref, mine_ref, other_ref, o_ref, lse_ref, k_ref, vt_ref,
):
    index = pl.program_id(0)

    @pl.when(index == 0)
    def _():
        core, last = core_ref[0], mine_ref.shape[1]

        def store_key(start, rows):
            k_ref[pl.ds(start, HALF_ROWS), :] = rows

        def store_value(start, rows):
            vt_ref[:, pl.ds(start, HALF_ROWS)] = jnp.transpose(rows)

        load_keys(core, mine_ref, other_ref, last - 2, store_key)
        load_keys(core, mine_ref, other_ref, last - 1, store_value)

    query = q_ref[0, 0]
    pos, begin = pos_ref[0], begin_ref[0]
    rows = query.shape[0]

    def step(block, carry, masked):
        top, total, acc = carry
        start = pl.multiple_of(block * KEY_ROWS, KEY_ROWS)
        scores = dot_nt(k_ref[pl.ds(start, KEY_ROWS), :], query) * LOG2_SCALE
        if masked:
            scores = jnp.where(allowed(start, pos, begin), scores, MASKED_SCORE)
        new_top = jnp.maximum(top, jnp.max(scores, axis=0, keepdims=True))
        probs = jnp.exp2(scores - new_top)
        shrink = jnp.exp2(top - new_top)
        total = total * shrink + jnp.sum(probs, axis=0, keepdims=True)
        acc = acc * shrink + jnp.dot(
            vt_ref[:, pl.ds(start, KEY_ROWS)], probs.astype(bfloat), preferred_element_type=single
        )
        return new_top, total, acc

    carry = (
        jnp.full((1, rows), MASKED_SCORE, single),
        jnp.zeros((1, rows), single),
        jnp.zeros((HEAD_DIM, rows), single),
    )
    top, total, acc = key_loops(low_ref, open_ref, close_ref, high_ref, index, step, carry)
    o_ref[0] = jnp.transpose(acc / total)
    lse_ref[0] = top + jnp.log2(total)


def backward_kernel(
    core_ref, low_ref, open_ref, close_ref, high_ref, pos_ref, begin_ref, lse_ref, o_ref,
    q_ref, do_ref, mine_ref, other_ref, dq_ref, keep_ref, send_ref, k_ref, v_ref, kt_ref, dk_ref, dv_ref,
):
    index = pl.program_id(0)
    core = core_ref[0]

    @pl.when(index == 0)
    def _():
        dk_ref[...] = jnp.zeros_like(dk_ref)
        dv_ref[...] = jnp.zeros_like(dv_ref)
        last = mine_ref.shape[1]

        def store_key(start, rows):
            k_ref[pl.ds(start, HALF_ROWS), :] = rows
            kt_ref[:, pl.ds(start, HALF_ROWS)] = jnp.transpose(rows)

        def store_value(start, rows):
            v_ref[pl.ds(start, HALF_ROWS), :] = rows

        load_keys(core, mine_ref, other_ref, last - 2, store_key)
        load_keys(core, mine_ref, other_ref, last - 1, store_value)

    query, d_out = q_ref[0, 0], do_ref[0]
    pos, begin = pos_ref[0], begin_ref[0]
    lse = lse_ref[0]
    products = d_out.astype(single) * o_ref[0]
    delta = jnp.sum(jnp.transpose(products), axis=0, keepdims=True)

    def step(block, acc, masked):
        start = pl.multiple_of(block * KEY_ROWS, KEY_ROWS)
        rows = pl.ds(start, KEY_ROWS)
        scores = dot_nt(k_ref[rows, :], query) * LOG2_SCALE
        probs = jnp.exp2(scores - lse)
        if masked:
            probs = jnp.where(allowed(start, pos, begin), probs, 0.0)
        d_probs = dot_nt(v_ref[rows, :], d_out)
        d_scores = (probs * (d_probs - delta)).astype(bfloat)
        dv_ref[rows, :] += jnp.dot(probs.astype(bfloat), d_out, preferred_element_type=single)
        dk_ref[rows, :] += jnp.dot(d_scores, query, preferred_element_type=single)
        return acc + jnp.dot(kt_ref[:, rows], d_scores, preferred_element_type=single)

    acc = jnp.zeros((HEAD_DIM, query.shape[0]), single)
    acc = key_loops(low_ref, open_ref, close_ref, high_ref, index, step, acc)
    dq_ref[0] = (jnp.transpose(acc) * SCORE_SCALE).astype(bfloat)

    @pl.when(index == pl.num_programs(0) - 1)
    def _():
        for blk in range(keep_ref.shape[0]):
            start = 2 * blk * HALF_ROWS
            mine = pl.ds(pl.multiple_of(start + core * HALF_ROWS, HALF_ROWS), HALF_ROWS)
            other = pl.ds(pl.multiple_of(start + (1 - core) * HALF_ROWS, HALF_ROWS), HALF_ROWS)
            keep_ref[blk, 0] = dk_ref[mine, :] * SCORE_SCALE
            keep_ref[blk, 1] = dv_ref[mine, :]
            send_ref[blk, 0] = (dk_ref[other, :] * SCORE_SCALE).astype(bfloat)
            send_ref[blk, 1] = dv_ref[other, :].astype(bfloat)


def block_bounds(pos, begin):
    first, last = jnp.min(begin, axis=1), jnp.max(begin, axis=1)
    low = first // KEY_ROWS
    high = jnp.max(pos, axis=1) // KEY_ROWS + 1
    opened = jnp.clip((last + KEY_ROWS - 1) // KEY_ROWS, low, high)
    closed = jnp.clip((jnp.min(pos, axis=1) + 1) // KEY_ROWS, opened, high)
    return low, opened, closed, high


def block_spec(shape):
    return pl.BlockSpec((1,) + shape[1:], lambda i, *_: (i,) + (0,) * (len(shape) - 1))


def first_spec(shape):
    return pl.BlockSpec((1, 1) + shape[2:], lambda i, *_: (i,) + (0,) * (len(shape) - 1))


def whole_spec(shape):
    return pl.BlockSpec(shape, lambda *_: (0,) * len(shape), pipeline_mode=pl.Buffered(1))


def attention_forward(scalars, pos, begin, query, mine, other):
    blocks, _, rows = pos.shape
    keys = 2 * mine.shape[0] * HALF_ROWS
    out_shape = [
        jax.ShapeDtypeStruct((blocks, rows, HEAD_DIM), single),
        jax.ShapeDtypeStruct(pos.shape, single),
    ]
    return pl.pallas_call(
        forward_kernel,
        grid_spec=pltpu.PrefetchScalarGridSpec(
            num_scalar_prefetch=5,
            grid=(blocks,),
            in_specs=[
                block_spec(pos.shape), block_spec(pos.shape), first_spec(query.shape),
                whole_spec(mine.shape), whole_spec(other.shape),
            ],
            out_specs=[block_spec(out.shape) for out in out_shape],
            scratch_shapes=[pltpu.VMEM((keys, HEAD_DIM), bfloat), pltpu.VMEM((HEAD_DIM, keys), bfloat)],
        ),
        out_shape=out_shape,
        compiler_params=pltpu.CompilerParams(vmem_limit_bytes=48 << 20),
        name="attention_forward",
    )(*scalars, pos, begin, query, mine, other)


def attention_backward(scalars, pos, begin, lse, head_out, query, d_out, mine, other):
    blocks, _, rows = pos.shape
    keys = 2 * mine.shape[0] * HALF_ROWS
    pair = (mine.shape[0], 2, HALF_ROWS, HEAD_DIM)
    out_shape = [
        jax.ShapeDtypeStruct(d_out.shape, bfloat),
        jax.ShapeDtypeStruct(pair, single),
        jax.ShapeDtypeStruct(pair, bfloat),
    ]
    return pl.pallas_call(
        backward_kernel,
        grid_spec=pltpu.PrefetchScalarGridSpec(
            num_scalar_prefetch=5,
            grid=(blocks,),
            in_specs=[
                block_spec(pos.shape), block_spec(pos.shape), block_spec(pos.shape),
                block_spec(head_out.shape), first_spec(query.shape), block_spec(d_out.shape),
                whole_spec(mine.shape), whole_spec(other.shape),
            ],
            out_specs=[block_spec(d_out.shape), whole_spec(pair), whole_spec(pair)],
            scratch_shapes=[
                pltpu.VMEM((keys, HEAD_DIM), bfloat), pltpu.VMEM((keys, HEAD_DIM), bfloat),
                pltpu.VMEM((HEAD_DIM, keys), bfloat),
                pltpu.VMEM((keys, HEAD_DIM), single), pltpu.VMEM((keys, HEAD_DIM), single),
            ],
        ),
        out_shape=out_shape,
        compiler_params=pltpu.CompilerParams(vmem_limit_bytes=60 << 20),
        name="attention_backward",
    )(*scalars, pos, begin, lse, head_out, query, d_out, mine, other)


def turned(values, cosine, sine):
    return values * cosine + pltpu.roll(values, HEAD_DIM // 2, 1) * sine


def rotate_kernel(lin_ref, recip_ref, gain_ref, cosine_ref, sine_ref, out_ref):
    groups, rows = out_ref.shape[2], out_ref.shape[5]
    cosine, sine = cosine_ref[...], sine_ref[...]
    for which in range(3):
        for head in range(2):
            at = head * HEAD_DIM
            values = lin_ref[:, pl.ds((2 * which + head) * HEAD_DIM, HEAD_DIM)]
            if which < 2:
                values = values * recip_ref[:, which : which + 1]
                values = values * gain_ref[which : which + 1, at : at + HEAD_DIM]
                values = turned(values, cosine, sine)
            values = values.astype(bfloat)
            for group in range(groups):
                out_ref[0, head, group, 0, which] = values[group * rows : (group + 1) * rows]


def back_parts(d_ref, lin_ref, recip_ref, gain_ref, cosine, sine, which, head):
    at = head * HEAD_DIM
    grad = d_ref[0, head, :, 0, which].reshape(-1, HEAD_DIM).astype(single)
    grad = turned(grad, cosine, -sine)
    hat = lin_ref[:, pl.ds((2 * which + head) * HEAD_DIM, HEAD_DIM)] * recip_ref[:, which : which + 1]
    return grad, grad * gain_ref[which : which + 1, at : at + HEAD_DIM], hat


def sums_kernel(d_ref, lin_ref, recip_ref, gain_ref, cosine_ref, sine_ref, gain_out_ref, sum_ref):
    first = (pl.program_id(0) == 0) & (pl.program_id(1) == 0)

    @pl.when(first)
    def _():
        gain_out_ref[...] = jnp.zeros_like(gain_out_ref)

    cosine, sine = cosine_ref[...], sine_ref[...]
    for which in range(2):
        total = None
        for head in range(2):
            grad, scaled, hat = back_parts(
                d_ref, lin_ref, recip_ref, gain_ref, cosine, sine, which, head
            )
            at = pl.ds(head * HEAD_DIM, HEAD_DIM)
            gain_out_ref[which : which + 1, at] += jnp.sum(grad * hat, axis=0, keepdims=True)
            product = jnp.transpose(scaled * hat)
            product = jnp.sum(product, axis=0, keepdims=True)
            total = product if total is None else total + product
        sum_ref[0, 0, which : which + 1, :] = total


def lin_kernel(d_ref, lin_ref, recip_ref, mean_ref, gain_ref, cosine_ref, sine_ref, out_ref):
    cosine, sine = cosine_ref[...], sine_ref[...]
    for head in range(2):
        for which in range(2):
            _, scaled, hat = back_parts(
                d_ref, lin_ref, recip_ref, gain_ref, cosine, sine, which, head
            )
            grad = recip_ref[:, which : which + 1] * (scaled - hat * mean_ref[:, which : which + 1])
            out_ref[:, pl.ds((2 * which + head) * HEAD_DIM, HEAD_DIM)] = grad.astype(bfloat)
        out_ref[:, pl.ds((4 + head) * HEAD_DIM, HEAD_DIM)] = d_ref[0, head, :, 0, 2].reshape(
            -1, HEAD_DIM
        )


def token_spec(columns):
    return pl.BlockSpec((HALF_ROWS, columns), lambda near, half: (2 * near + half, 0))


def split_spec(groups, rows):
    return pl.BlockSpec(
        (1, 2, groups, 1, 3, rows, HEAD_DIM), lambda near, half: (half, 0, 0, near, 0, 0, 0)
    )


def project_kernel(rows_ref, weight_ref, lin_ref, sum_ref):
    part = weight_ref.shape[1] // 3
    lin = jnp.dot(rows_ref[...], weight_ref[...], preferred_element_type=single)
    lin_ref[...] = lin
    for which in range(2):
        values = lin[:, which * part : (which + 1) * part]
        sum_ref[0, 0, which : which + 1, :] = jnp.sum(
            jnp.transpose(values * values), axis=0, keepdims=True
        )


def projected(rows, weight):
    return pl.pallas_call(
        project_kernel,
        grid=(2, 2),
        in_specs=[token_spec(rows.shape[1]), whole_spec(weight.shape)],
        out_specs=[
            token_spec(weight.shape[1]),
            pl.BlockSpec((1, 1, 2, HALF_ROWS), lambda near, half: (near, half, 0, 0)),
        ],
        out_shape=[
            jax.ShapeDtypeStruct((rows.shape[0], weight.shape[1]), single),
            jax.ShapeDtypeStruct((2, 2, 2, HALF_ROWS), single),
        ],
        compiler_params=pltpu.CompilerParams(vmem_limit_bytes=32 << 20),
        name="projected",
    )(rows, weight)


def columns(values):
    return jnp.transpose(values, (0, 1, 3, 2)).reshape(-1, 2)


def rotated_heads(lin, recips, gains, cosine, sine, groups):
    rows = HALF_ROWS // groups
    return pl.pallas_call(
        rotate_kernel,
        grid=(2, 2),
        in_specs=[
            token_spec(lin.shape[1]), token_spec(2), whole_spec(gains.shape),
            token_spec(HEAD_DIM), token_spec(HEAD_DIM),
        ],
        out_specs=split_spec(groups, rows),
        out_shape=jax.ShapeDtypeStruct((2, 2, groups, 2, 3, rows, HEAD_DIM), bfloat),
        name="rotated_heads",
    )(lin, recips, gains, cosine, sine)


def rotated_sums(d_split, lin, recips, gains, cosine, sine):
    groups, rows = d_split.shape[2], d_split.shape[5]
    return pl.pallas_call(
        sums_kernel,
        grid=(2, 2),
        in_specs=[
            split_spec(groups, rows), token_spec(lin.shape[1]), token_spec(2),
            whole_spec(gains.shape), token_spec(HEAD_DIM), token_spec(HEAD_DIM),
        ],
        out_specs=[
            pl.BlockSpec(gains.shape, lambda near, half: (0, 0)),
            pl.BlockSpec((1, 1, 2, HALF_ROWS), lambda near, half: (near, half, 0, 0)),
        ],
        out_shape=[
            jax.ShapeDtypeStruct(gains.shape, single),
            jax.ShapeDtypeStruct((2, 2, 2, HALF_ROWS), single),
        ],
        name="rotated_sums",
    )(d_split, lin, recips, gains, cosine, sine)


def rotated_back(d_split, lin, recips, means, gains, cosine, sine):
    groups, rows = d_split.shape[2], d_split.shape[5]
    return pl.pallas_call(
        lin_kernel,
        grid=(2, 2),
        in_specs=[
            split_spec(groups, rows), token_spec(lin.shape[1]), token_spec(2), token_spec(2),
            whole_spec(gains.shape), token_spec(HEAD_DIM), token_spec(HEAD_DIM),
        ],
        out_specs=token_spec(lin.shape[1]),
        out_shape=jax.ShapeDtypeStruct(lin.shape, bfloat),
        name="rotated_back",
    )(d_split, lin, recips, means, gains, cosine, sine)


def unpack_kernel(in_ref, *out_refs):
    count, rows, width = in_ref.shape
    part = width // 3
    for which in range(3):
        for piece in range(count):
            out_refs[which][:, pl.ds(piece * part, part)] = in_ref[
                piece, :, pl.ds(which * part, part)
            ].astype(single)


def unpacked(values):
    count, rows, width = values.shape
    return pl.pallas_call(
        unpack_kernel,
        out_shape=[jax.ShapeDtypeStruct((rows, count * width // 3), single)] * 3,
        name="unpacked",
    )(values)


def dot_tn(a, b):
    return lax.dot_general(a, b, (((0,), (0,)), ((), ())), preferred_element_type=single)


def picks(slot_ref, source, expert, capacity):
    slots = slot_ref[source, expert : expert + 1, :]
    rows = lax.broadcasted_iota(jnp.int32, (capacity, slots.shape[1]), 0) + 1
    return slots == rows.astype(single)


def spread_tokens(slot_ref, first, second, out_ref, capacity):
    for source in range(slot_ref.shape[0]):
        at = slice(source * capacity, (source + 1) * capacity)
        total = dot_tn(picks(slot_ref, source, 0, capacity).astype(bfloat), first[at])
        total += dot_tn(picks(slot_ref, source, 1, capacity).astype(bfloat), second[at])
        out_ref[source] = total.astype(bfloat)


def expert_kernel(
    blk_ref, slot_ref, ffn_ref, cot_ref, router_ref, gate_ref, up_ref, down_ref, gate_tile_ref,
    up_tile_ref, x_ref, c_ref, value_ref, hidden_ref, d_gate_ref, d_up_ref, probs_ref, out_ref,
    grad_ref, d_both_ref, first_ref,
):
    expert, step = pl.program_id(0), pl.program_id(1)
    sources = ffn_ref.shape[0]
    capacity = x_ref.shape[1] // sources
    part = gate_ref.shape[3]
    tile = gate_tile_ref.shape[2]

    @pl.when((expert == 0) & (step == 0))
    def _():
        for source in range(sources):
            logits = dot_nt(router_ref[...], ffn_ref[source])
            shifted = jnp.exp(logits - jnp.max(logits, axis=0, keepdims=True))
            probs_ref[source] = shifted / jnp.sum(shifted, axis=0, keepdims=True)

    def fill(which):
        for source in range(sources):
            at = pl.ds(source * capacity, capacity)
            picked = picks(slot_ref, source, which, capacity)
            picked_low = picked.astype(bfloat)
            x_ref[0, at, :] = jnp.dot(
                picked_low, ffn_ref[source], preferred_element_type=single
            ).astype(bfloat)
            cot_rows = jnp.dot(picked_low, cot_ref[source], preferred_element_type=single)
            c_ref[0, at, :] = cot_rows.astype(bfloat)
            probs = probs_ref[source, pl.ds(2 * blk_ref[0] + which, 1), :]
            value = jnp.sum(jnp.where(picked, probs, 0.0), axis=1, keepdims=True)
            value_ref[0, at, :] = value
            grad_ref[at, :] = (value * cot_rows).astype(bfloat)

    for which in range(2):
        pl.when((expert == which) & (step == 0))(lambda which=which: fill(which))

    def hidden_part(index):
        w_both = jnp.concatenate([gate_ref[0, 0], up_ref[0, 0]], axis=1)
        both = jnp.dot(x_ref[0], w_both, preferred_element_type=single)
        gate_val, up_val = both[:, :part], both[:, part:]
        d_hidden = dot_nt(grad_ref[...], down_ref[0, 0])
        sigmoid = 1.0 / (1.0 + jnp.exp(-gate_val))
        silu = gate_val * sigmoid
        hidden_ref[0] = (silu * up_val).astype(bfloat)
        d_gate = (d_hidden * up_val * sigmoid * (1.0 + gate_val * (1.0 - sigmoid))).astype(bfloat)
        d_up = (d_hidden * silu).astype(bfloat)
        d_gate_ref[0] = d_gate
        d_up_ref[0] = d_up
        d_both_ref[:, pl.ds(2 * index * part, part)] = d_gate
        d_both_ref[:, pl.ds((2 * index + 1) * part, part)] = d_up

    for index in range(4):
        pl.when(step == index)(lambda index=index: hidden_part(index))

    def row_tile(index, which):
        weights = [ref[i, 0] for i in range(4) for ref in (gate_tile_ref, up_tile_ref)]
        d_rows = dot_nt(d_both_ref[...], jnp.concatenate(weights, axis=1)).astype(bfloat)
        at = pl.ds(index * tile, tile)
        if which == 0:
            first_ref[:, at] = d_rows
        else:
            spread_tokens(slot_ref, first_ref[:, at], d_rows, out_ref, capacity)

    for index in range(4):
        for which in range(2):
            pl.when((step == index + 4) & (expert == which))(
                lambda index=index, which=which: row_tile(index, which)
            )


def grads_kernel(
    slot_ref, x_ref, c_ref, value_ref, hidden_ref, d_gate_ref, d_up_ref, down_tile_ref,
    gate_sent_ref, up_sent_ref, down_sent_ref, gate_kept_ref, up_kept_ref, down_kept_ref,
    d_probs_ref, out_ref, grad_ref, xt_ref, dots_ref, first_ref,
):
    expert, step = pl.program_id(0), pl.program_id(1)
    sources = slot_ref.shape[0]
    capacity = x_ref.shape[1] // sources
    part = d_gate_ref.shape[2]
    tile = down_tile_ref.shape[3]

    @pl.when(step == 0)
    def _():
        grad_ref[...] = (value_ref[0] * c_ref[0].astype(single)).astype(bfloat)
        xt_ref[...] = jnp.transpose(x_ref[0])
        dots_ref[...] = jnp.zeros_like(dots_ref)

    def weight_part(index, gate_ref, up_ref, down_ref):
        d_both = jnp.concatenate([d_gate_ref[0], d_up_ref[0]], axis=1)
        both = jnp.dot(xt_ref[...], d_both, preferred_element_type=single)
        gate_ref[0, 0] = both[:, :part].astype(gate_ref.dtype)
        up_ref[0, 0] = both[:, part:].astype(up_ref.dtype)
        hidden = hidden_ref[0, :, pl.ds(index * part, part)]
        down_ref[0, 0] = dot_tn(hidden, grad_ref[...]).astype(down_ref.dtype)

    for index in range(4):
        refs = (
            (gate_sent_ref, up_sent_ref, down_sent_ref)
            if index < 2
            else (gate_kept_ref, up_kept_ref, down_kept_ref)
        )
        pl.when(step == index)(lambda index=index, refs=refs: weight_part(index, *refs))

    def out_tile(index, which):
        down = jnp.concatenate([down_tile_ref[i, 0] for i in range(4)], axis=0)
        expert_out = jnp.dot(hidden_ref[0], down, preferred_element_type=single)
        expert_out = expert_out.astype(bfloat).astype(single)
        at = pl.ds(index * tile, tile)
        dots_ref[...] += jnp.sum(
            c_ref[0, :, at].astype(single) * expert_out, axis=1, keepdims=True
        )
        weighted = (value_ref[0] * expert_out).astype(bfloat)
        if which == 0:
            first_ref[:, at] = weighted
        else:
            spread_tokens(slot_ref, first_ref[:, at], weighted, out_ref, capacity)
        if index == 3:
            for source in range(sources):
                picked = picks(slot_ref, source, which, capacity)
                row = dots_ref[source * capacity : (source + 1) * capacity]
                d_probs_ref[source, which : which + 1, :] = jnp.sum(
                    jnp.where(picked, row, 0.0), axis=0, keepdims=True
                )

    for index in range(4):
        for which in range(2):
            pl.when((step == index + 4) & (expert == which))(
                lambda index=index, which=which: out_tile(index, which)
            )


def rows_spec(rows, columns):
    return pl.BlockSpec((1, rows, columns), lambda e, k, *_: (e, 0, 0))


def first_half(k):
    return jnp.minimum(k, 3)


def second_half(k):
    return jnp.maximum(k - 4, 0)


def part_spec(rows, columns):
    return pl.BlockSpec((1, rows, columns), lambda e, k, *_: (e, 0, first_half(k)))


def weight_spec(shape, place=first_half):
    return pl.BlockSpec((1, 1) + shape[2:], lambda e, k, *_: (place(k), e, 0, 0))


def token_tile_spec(shape):
    block = shape[:2] + (shape[2] // 4,)
    return pl.BlockSpec(block, lambda e, k, *_: (0, 0, e * second_half(k)))


def expert_rows(blk, slot_map, ffn_all, cot_all, router_t, gate, up, down, capacity):
    sources, tokens, width = ffn_all.shape
    rows, experts, hidden = sources * capacity, router_t.shape[0], 4 * gate.shape[3]
    wide = jax.ShapeDtypeStruct((2, rows, width), bfloat)
    narrow = jax.ShapeDtypeStruct((2, rows, hidden), bfloat)
    probs = jax.ShapeDtypeStruct((sources, experts, tokens), single)
    tile_spec = pl.BlockSpec(
        (4, 1, width // 4, hidden // 4), lambda e, k, *_: (0, e, second_half(k), 0)
    )
    return pl.pallas_call(
        expert_kernel,
        grid_spec=pltpu.PrefetchScalarGridSpec(
            num_scalar_prefetch=1,
            grid=(2, 8),
            in_specs=[
                whole_spec(slot_map.shape), whole_spec(ffn_all.shape), whole_spec(cot_all.shape),
                whole_spec(router_t.shape), weight_spec(gate.shape), weight_spec(up.shape),
                weight_spec(down.shape), tile_spec, tile_spec,
            ],
            out_specs=[
                rows_spec(rows, width), rows_spec(rows, width), rows_spec(rows, 1),
                part_spec(rows, hidden // 4), part_spec(rows, hidden // 4),
                part_spec(rows, hidden // 4), whole_spec(probs.shape), token_tile_spec(ffn_all.shape),
            ],
            scratch_shapes=[
                pltpu.VMEM((rows, width), bfloat), pltpu.VMEM((rows, 2 * hidden), bfloat),
                pltpu.VMEM((rows, width), bfloat),
            ],
        ),
        out_shape=[
            wide, wide, jax.ShapeDtypeStruct((2, rows, 1), single), narrow, narrow, narrow,
            probs, jax.ShapeDtypeStruct(ffn_all.shape, bfloat),
        ],
        compiler_params=pltpu.CompilerParams(vmem_limit_bytes=60 << 20),
        name="expert_rows",
    )(blk[None], slot_map, ffn_all, cot_all, router_t, gate, up, down, gate, up)


def expert_grads(slot_map, x, c, value, hidden, d_gate, d_up, down, tokens):
    rows, width = x.shape[1:]
    part = down.shape[2]
    wide, tall = (2, 2, width, part), (2, 2, part, width)
    summed = (slot_map.shape[0], tokens, width)

    def sent(k):
        return jnp.minimum(k, 1)

    def kept(k):
        return jnp.clip(k - 2, 0, 1)

    shapes = (wide, wide, tall)
    return pl.pallas_call(
        grads_kernel,
        grid=(2, 8),
        in_specs=[
            whole_spec(slot_map.shape), rows_spec(rows, width), rows_spec(rows, width),
            rows_spec(rows, 1), rows_spec(rows, 4 * part), part_spec(rows, part),
            part_spec(rows, part),
            pl.BlockSpec((4, 1, part, width // 4), lambda e, k: (0, e, 0, second_half(k))),
        ],
        out_specs=[weight_spec(shape, sent) for shape in shapes]
        + [weight_spec(shape, kept) for shape in shapes]
        + [whole_spec(slot_map.shape), token_tile_spec(summed)],
        out_shape=[jax.ShapeDtypeStruct(shape, bfloat) for shape in shapes]
        + [jax.ShapeDtypeStruct(shape, single) for shape in shapes]
        + [
            jax.ShapeDtypeStruct(slot_map.shape, single),
            jax.ShapeDtypeStruct(summed, bfloat),
        ],
        scratch_shapes=[
            pltpu.VMEM((rows, width), bfloat), pltpu.VMEM((width, rows), bfloat),
            pltpu.VMEM((rows, 1), single), pltpu.VMEM((rows, width), bfloat),
        ],
        compiler_params=pltpu.CompilerParams(vmem_limit_bytes=60 << 20),
        name="expert_grads",
    )(slot_map, x, c, value, hidden, d_gate, d_up, down)


def plain_experts(blk, slot_map, ffn_all, cot_all, router_t, gate, up, down, capacity):
    sources, tokens, width = ffn_all.shape
    count = slot_map.shape[1]

    def joined(weights, axis):
        return jnp.concatenate([weights[i] for i in range(4)], axis=axis)

    gate, up, down = joined(gate, 2), joined(up, 2), joined(down, 1)
    slot_at = jnp.arange(1, capacity + 1, dtype=jnp.int32).astype(single)
    picked = jnp.transpose(slot_map, (1, 0, 2))[:, :, None, :] == slot_at[None, None, :, None]
    picked_low = picked.astype(bfloat)
    logits = jnp.einsum("ed,std->set", router_t, ffn_all, preferred_element_type=single)
    shifted = jnp.exp(logits - jnp.max(logits, axis=1, keepdims=True))
    probs = shifted / jnp.sum(shifted, axis=1, keepdims=True)
    local = jnp.transpose(lax.dynamic_slice_in_dim(probs, blk * count, count, 1), (1, 0, 2))
    value = jnp.sum(jnp.where(picked, local[:, :, None, :], 0.0), axis=3).reshape(count, -1, 1)

    def dispatch(rows):
        rows = jnp.einsum("esct,std->escd", picked_low, rows, preferred_element_type=single)
        return rows.astype(bfloat).reshape(count, -1, width)

    def combine(rows):
        rows = rows.astype(bfloat).reshape(count, sources, capacity, width)
        total = jnp.einsum("esct,escd->std", picked_low, rows, preferred_element_type=single)
        return total.astype(bfloat)

    def dots(spec, *arrays):
        return jnp.einsum(spec, *arrays, preferred_element_type=single)

    x, c = dispatch(ffn_all), dispatch(cot_all).astype(single)
    grad = (value * c).astype(bfloat)
    gate_val, up_val = dots("erd,edf->erf", x, gate), dots("erd,edf->erf", x, up)
    sigmoid = jax.nn.sigmoid(gate_val)
    hidden = (gate_val * sigmoid * up_val).astype(bfloat)
    d_hidden = dots("erd,efd->erf", grad, down)
    d_gate = (d_hidden * up_val * sigmoid * (1.0 + gate_val * (1.0 - sigmoid))).astype(bfloat)
    d_up = (d_hidden * gate_val * sigmoid).astype(bfloat)
    d_part = combine(dots("erf,edf->erd", d_gate, gate) + dots("erf,edf->erd", d_up, up))
    expert_out = dots("erf,efd->erd", hidden, down).astype(bfloat).astype(single)
    d_value = jnp.sum(c * expert_out, axis=2).reshape(count, sources, capacity, 1)
    d_probs = jnp.transpose(jnp.sum(jnp.where(picked, d_value, 0.0), axis=2), (1, 0, 2))
    mixed_part = combine(value * expert_out)

    def cut(total, axis):
        parts = jnp.stack(jnp.split(total, 4, axis=axis))
        return parts[:2].astype(bfloat), parts[2:]

    gate_sent, gate_kept = cut(dots("erd,erf->edf", x, d_gate), 2)
    up_sent, up_kept = cut(dots("erd,erf->edf", x, d_up), 2)
    down_sent, down_kept = cut(dots("erf,erd->efd", hidden, grad), 1)
    return probs, d_part, (
        gate_sent, up_sent, down_sent, gate_kept, up_kept, down_kept, d_probs, mixed_part
    )


def per_device(
    block_input, w_query, w_key, w_value, w_out, attn_gain, ffn_gain, query_gain, key_gain,
    router, w_gate, w_up, w_down, expert_ids, slot_ids, doc_starts, cotangent,
):
    ulysses_size = lax.axis_size("ulysses")
    blk_size = lax.axis_size(BLK)
    blk = lax.axis_index(BLK)
    uly = lax.axis_index("ulysses")
    core = uly % 2
    own_tokens, width = block_input.shape
    picks = expert_ids.shape[1]
    experts = router.shape[1]
    capacity = 5 * own_tokens * picks // (4 * experts)
    local_experts = experts // blk_size
    blk_tokens = ulysses_size * own_tokens
    far_size = blk_size // 2
    far_tokens = 2 * blk_tokens
    plane_size = 2 * ulysses_size
    local_width = width // ulysses_size
    plane_width = width // plane_size
    weight_rows = w_query.shape[0]
    groups = blk_size // 8
    plane = 2 * uly + blk % 2

    projections = jnp.concatenate(
        [
            weight.astype(bfloat).reshape(weight_rows, plane_size, plane_width)
            for weight in (w_query, w_key, w_value)
        ],
        axis=2,
    )
    projections = lax.all_to_all(
        jnp.transpose(projections, (1, 0, 2)), PLANE, split_axis=0, concat_axis=0, tiled=True
    )
    projections = projections.reshape(ulysses_size, 2 * weight_rows, 3 * plane_width)
    small = jnp.concatenate(
        [jnp.stack([attn_gain, ffn_gain, query_gain, key_gain]), router.T]
    ).astype(bfloat)
    w_qkv = gather_line(projections, 1).reshape(width, 3 * plane_width)
    small = gather_small(small)
    gate_mine, up_mine, down_mine = w_gate.astype(bfloat), w_up.astype(bfloat), w_down.astype(bfloat)
    plane_input = gather_plane(block_input).reshape(far_tokens, width)
    pair_beyond = swap(jnp.stack([gate_mine, up_mine]), 2)
    w_qkv, pair_beyond = tie(w_qkv, pair_beyond)
    attn_g = small[0].astype(single)
    ffn_g = small[1].astype(single)
    plane_gains = lax.dynamic_slice_in_dim(
        small[2:4], plane * plane_width, plane_width, 1
    ).astype(single)
    router_t = small[4:]

    def gather_expert(mine, beyond):
        return jnp.stack([swap(mine, 1), swap(beyond, 1), mine, beyond])

    named = expert_ids[:, :, None] == jnp.arange(experts, dtype=jnp.int32)[None, None, :]
    slot_map = jnp.sum(jnp.where(named, slot_ids[:, :, None] + 1, 0), axis=1)
    slot_map = slot_map.T.astype(single).reshape(blk_size, local_experts, own_tokens)
    slot_map = lax.all_to_all(slot_map, BLK, split_axis=0, concat_axis=0, tiled=True)

    inputs = block_input.astype(single)
    hat_one, recip_one = norm_parts(inputs)
    normed = (norm_parts(plane_input.astype(single))[0] * attn_g).astype(bfloat)
    lin, squares = projected(normed, w_qkv)
    w_o = lax.all_gather(w_out.astype(bfloat), BLK, axis=0, tiled=True)
    cot_all = lax.all_gather(cotangent, BLK, axis=0)
    squares, down_mine = tie(sum_plane(squares), down_mine)
    down_beyond = swap(down_mine, 2)
    recips = columns(lax.rsqrt(squares / width + NORM_EPSILON))
    far_at = blk // 2 * far_tokens + jnp.arange(far_tokens, dtype=jnp.int32)
    cosine, sine = angles(far_at - doc_begins(doc_starts, far_at), HEAD_DIM)
    split = rotated_heads(lin, recips, plane_gains, cosine, sine, groups)
    heads_in = line_to_heads(split, far_size)
    gate_beyond, up_beyond = pair_beyond[0], pair_beyond[1]
    part_rows = heads_in.shape[2]
    if groups == 1:
        query, mine = heads_in, heads_in
    else:
        query = heads_in[:, 0].reshape(-1, 1, QUERY_ROWS, HEAD_DIM)
        mine = lax.all_gather(
            heads_in[:, 1:], "far", axis=2, axis_index_groups=head_groups(far_size, groups)
        ).reshape(blk_size, 2, HALF_ROWS, HEAD_DIM)
    other = swap(mine[:, -2:], 1)
    query_at = (
        jnp.arange(blk_size, dtype=jnp.int32)[:, None] * blk_tokens
        + core * HALF_ROWS
        + blk // 2 % groups * part_rows
        + jnp.arange(part_rows, dtype=jnp.int32)[None, :]
    ).reshape(-1, QUERY_ROWS)
    query_begin = doc_begins(doc_starts, query_at)
    scalars = (core[None],) + block_bounds(query_at, query_begin)
    query_at, query_begin = query_at[:, None], query_begin[:, None]
    head_out, lse = attention_forward(scalars, query_at, query_begin, query, mine, other)
    attended = blk_from_heads(
        head_out.astype(bfloat).reshape(blk_size, part_rows, HEAD_DIM), blk_size
    )
    attended, down_beyond = tie(attended, down_beyond)
    expert_gate = gather_expert(gate_mine, gate_beyond)
    expert_up = gather_expert(up_mine, up_beyond)
    expert_down = gather_expert(down_mine, down_beyond)
    out_part = jnp.dot(attended, w_o, preferred_element_type=single)

    def token_rows(values):
        return lambda bits: lax.dynamic_slice_in_dim(
            values, (uly ^ bits) * own_tokens, own_tokens, 0
        )

    residual_mid = inputs + scatter_sum_ulysses(token_rows(out_part))
    hat_two, recip_two = norm_parts(residual_mid)
    ffn_in = (hat_two * ffn_g).astype(bfloat)

    ffn_all = lax.all_gather(ffn_in, BLK, axis=0)
    if capacity % 16 == 0:
        *kept_rows, probs_all, d_part = expert_rows(
            blk, slot_map, ffn_all, cot_all, router_t, expert_gate, expert_up, expert_down, capacity
        )
        *kept_rows, d_part = tie(*kept_rows, d_part)
        results = expert_grads(slot_map, *kept_rows, expert_down, own_tokens)
    else:
        probs_all, d_part, results = plain_experts(
            blk, slot_map, ffn_all, cot_all, router_t, expert_gate, expert_up, expert_down, capacity
        )
    d_ffn_in = lax.psum_scatter(d_part, BLK, scatter_dimension=0).astype(single)
    gate_sent, up_sent, down_sent, gate_kept, up_kept, down_kept, d_probs, mixed_part = results

    def add_core(sent, kept):
        got = swap(sent, 1).astype(single)
        return kept[0] + got[0], (kept[1] + got[1]).astype(bfloat)

    down_kept, down_sent = add_core(down_sent, down_kept)
    down_across = swap(down_sent, 2)
    d_probs = lax.all_to_all(d_probs, BLK, split_axis=0, concat_axis=0, tiled=True)
    d_probs = d_probs.reshape(experts, own_tokens)
    d_probs, gate_kept, up_kept = tie(d_probs, gate_kept, up_kept)
    gate_kept, gate_sent = add_core(gate_sent, gate_kept)
    up_kept, up_sent = add_core(up_sent, up_kept)
    d_ffn_in, mixed_part, gate_sent, up_sent, down_across = tie(
        d_ffn_in, mixed_part, gate_sent, up_sent, down_across
    )
    grad_w_down = down_kept + down_across.astype(single)
    mixed_sum = lax.psum_scatter(mixed_part, BLK, scatter_dimension=0)

    router_probs = lax.dynamic_index_in_dim(probs_all, blk, 0, keepdims=False)
    d_logits = (
        router_probs * (d_probs - jnp.sum(router_probs * d_probs, axis=0, keepdims=True))
    ).astype(bfloat)
    grad_router_part = jnp.dot(d_logits, ffn_in, preferred_element_type=single)
    d_ffn_in = d_ffn_in + dot_tn(d_logits, router_t)
    grad_ffn_part = jnp.sum(d_ffn_in * hat_two, axis=0)
    d_mid = cotangent.astype(single) + norm_back(d_ffn_in * ffn_g, hat_two, recip_two)

    d_attn_out = gather_ulysses(d_mid.astype(bfloat)).reshape(blk_tokens, width)
    d_attn_out, gate_sent = tie(d_attn_out, gate_sent)
    gate_across = swap(gate_sent, 2)
    d_attended = dot_nt(d_attn_out, w_o).astype(bfloat)
    grad_out_part = jnp.einsum("ti,to->io", attended, d_attn_out, preferred_element_type=single)
    grad_out_part = grad_out_part.astype(bfloat).reshape(blk_size, weight_rows, width)
    d_out = blk_to_heads(d_attended, blk_size).reshape(head_out.shape)
    d_out, grad_out_part, grad_w_down = tie(d_out, grad_out_part, grad_w_down)
    grad_w_out = lax.psum_scatter(grad_out_part, BLK, scatter_dimension=0)
    dq_head, keep, send = attention_backward(
        scalars, query_at, query_begin, lse, head_out, query, d_out, mine, other
    )
    dq_head, gate_across, up_sent = tie(dq_head, gate_across, up_sent)
    up_across = swap(up_sent, 2)
    grad_w_gate = gate_kept + gate_across.astype(single)
    d_keys = (keep + swap(send, 1).astype(single)).astype(bfloat)
    if groups > 1:
        moved = jnp.moveaxis(d_keys.reshape(blk_size, 2, groups, part_rows, HEAD_DIM), 2, 0)
        moved = lax.psum_scatter(
            moved, "far", scatter_dimension=0, axis_index_groups=head_groups(far_size, groups)
        )
        d_keys = moved
    d_stack = jnp.concatenate(
        [dq_head.reshape(blk_size, 1, part_rows, HEAD_DIM), d_keys], axis=1
    )
    d_split = line_from_heads(d_stack, far_size)
    narrow = scatter_sum_ulysses(
        lambda bits: lax.dynamic_slice_in_dim(
            jnp.concatenate([grad_ffn_part[None], grad_router_part]),
            (uly ^ bits) * local_width, local_width, 1,
        ),
        single,
    )
    d_split, narrow, up_across, mixed_sum, grad_w_gate = tie(
        d_split, narrow, up_across, mixed_sum, grad_w_gate
    )
    mixed = (residual_mid + mixed_sum.astype(single)).astype(bfloat)
    grad_w_up = up_kept + up_across.astype(single)
    gain_parts, means = rotated_sums(d_split, lin, recips, plane_gains, cosine, sine)
    means = columns(sum_plane(means) / width)
    means, grad_w_out = tie(means, grad_w_out)
    grad_w_out = grad_w_out.astype(single)
    d_lin = rotated_back(d_split, lin, recips, means, plane_gains, cosine, sine)
    grads = jnp.einsum("td,to->do", normed, d_lin, preferred_element_type=single)
    grads = grads.astype(bfloat).reshape(ulysses_size, far_size, 2 * weight_rows, 3 * plane_width)
    grads = jnp.transpose(grads, (1, 0, 2, 3)).reshape(-1, 3 * plane_width)
    grads = lax.psum_scatter(grads, "far", scatter_dimension=0, tiled=True)
    d_normed_part = dot_nt(d_lin, w_qkv)
    grad_attn_part = jnp.sum(d_normed_part * norm_parts(plane_input.astype(single))[0], axis=0)
    d_normed_part = d_normed_part.reshape(2, blk_tokens, width)
    side = blk % 2

    def near_rows(bits):
        mine, other = (
            lax.dynamic_slice(
                d_normed_part, (place, (uly ^ bits) * own_tokens, 0), (1, own_tokens, width)
            )[0]
            for place in (side, 1 - side)
        )
        return mine, other

    d_normed, grad_w_up = scatter_sum_plane(near_rows, grad_w_up)
    input_grad = d_mid + norm_back(d_normed * attn_g, hat_one, recip_one)

    def own_columns(values):
        return scatter_sum_ulysses(
            lambda bits: lax.dynamic_slice_in_dim(values, (uly ^ bits) * local_width, local_width, 1),
            single,
        )

    gain_parts = lax.dynamic_update_slice_in_dim(
        jnp.zeros((2, local_width), single), gain_parts, side * plane_width, 1
    )
    last = own_columns(grad_attn_part[None])
    gains = scatter_sum_blk_small(jnp.concatenate([last, narrow, gain_parts]))
    grads = grads.reshape(plane_size, weight_rows, 3 * plane_width)
    grads = lax.all_to_all(grads, PLANE, split_axis=0, concat_axis=0, tiled=True)
    grads = unpacked(grads)
    return (
        mixed,
        input_grad.astype(bfloat),
        grads[0],
        grads[1],
        grads[2],
        grad_w_out,
        gains[0],
        gains[1],
        gains[-2],
        gains[-1],
        gains[2:-2].T,
        grad_w_gate,
        grad_w_up,
        grad_w_down,
    )


def solution(mesh):
    in_specs = (
        P(("far", "near", "ulysses"), None),
        P(("ulysses", "far", "near"), None),
        P(("ulysses", "far", "near"), None),
        P(("ulysses", "far", "near"), None),
        P(("ulysses", "far", "near"), None),
        P(("ulysses", "far", "near")),
        P(("ulysses", "far", "near")),
        P(("ulysses", "far", "near")),
        P(("ulysses", "far", "near")),
        P(("ulysses", "far", "near"), None),
        P(BLK, None, "ulysses"),
        P(BLK, None, "ulysses"),
        P(BLK, "ulysses", None),
        P(("far", "near", "ulysses"), None),
        P(("far", "near", "ulysses"), None),
        P(),
        P(("far", "near", "ulysses"), None),
    )
    out_specs = (
        P(("far", "near", "ulysses"), None),
        P(("far", "near", "ulysses"), None),
        P(("ulysses", "far", "near"), None),
        P(("ulysses", "far", "near"), None),
        P(("ulysses", "far", "near"), None),
        P(("ulysses", "far", "near"), None),
        P(("ulysses", "far", "near")),
        P(("ulysses", "far", "near")),
        P(("ulysses", "far", "near")),
        P(("ulysses", "far", "near")),
        P(("ulysses", "far", "near"), None),
        P(BLK, None, "ulysses"),
        P(BLK, None, "ulysses"),
        P(BLK, "ulysses", None),
    )
    ulysses_size, blk_size = mesh.devices.shape
    shape = (ulysses_size, blk_size // 2, 2)
    split_mesh = jax.sharding.Mesh(mesh.devices.reshape(shape), ("ulysses", "far", "near"))
    return jax.shard_map(
        per_device, mesh=split_mesh, in_specs=in_specs, out_specs=out_specs, check_vma=False
    )
```

time: 1350 us -> 874 us (0.65)
  waiting for transfers between devices: 723 us -> 341 us
  blocking collectives: 180 us -> 34.5 us
  Pallas kernels: 46.9 us -> 192 us
  matrix products: 152 us -> 19.6 us
  starting transfers between devices: 33.1 us -> 71.3 us
  other arithmetic: 96.2 us -> 127 us
  local copies, waits for them, and re-layouts: 89.9 us -> 62.5 us
    unnamed x13 -> x7, waiting for transfers between devices: 222 us -> 0.82 us
    reduce_scatter x3 -> x4, waiting for transfers between devices: 160 us -> 15 us  [the longest x1 15 us: per_device(): grad_w_out = lax.psum_scatter(grad_out_part, BLK, scatter_dimension=0)]
    pallas_call x0 -> x7, Pallas kernels: none -> 144 us  [the longest x1 74.6 us: expert_rows(): pl.pallas_call(expert_kernel, grid_spec=pltpu.PrefetchScalarGridSpec(num_...]
    dot_general x21 -> x3, matrix products: 138 us -> 6.91 us  [the longest x1 6.2 us: per_device(): jnp.einsum('td,to->do', normed, d_lin, preferred_element_type=single)]
    all_gather x1 -> x0, blocking collectives: 70.9 us -> none  [per_device(): small = lax.all_gather(small, ('ulysses', 'blk'), axis=1, tiled=True)]
    all_to_all x4 -> x2, blocking collectives: 96.6 us -> 34.5 us  [the longest x1 25.3 us: blk_from_heads(): back = lax.all_to_all(stacked, BLK, split_axis=0, concat_axis=0, tiled=True)]
    ppermute x38 -> x58, waiting for transfers between devices: 267 us -> 210 us  [the longest x52 170 us: swap(): return lax.ppermute(values, axis, [(i, i ^ bit) for i in range(size)])]
    another operation x11 -> x10, other arithmetic: 5.93 us -> 33.8 us  [the longest x3 21.1 us: gather_expert(): return jnp.stack([swap(mine, 1), swap(beyond, 1), mine, beyond])]
  transfers between devices with their start and end apart: 52 -> 73, of which waited for: 24 -> 33; matrix products, arithmetic and copies ran while one was open for 18% -> 21% of each run, Pallas kernels for 2% -> 13%
where the time goes in v2:
time: 874 us; the launch traced here: 865 us
  waiting for transfers between devices  341 us (39%)
  Pallas kernels  192 us (22%)
  other arithmetic  127 us (15%)
  starting transfers between devices  71.3 us (8%)
  local copies, waits for them, and re-layouts  62.5 us (7%)
  blocking collectives  34.5 us (4%)
  matrix products  19.6 us (2%)
  between operations  15.9 us (2%)
    ppermute x52, waiting for transfers between devices, swap(): return lax.ppermute(values, axis, [(i, i ^ bit) for i in range(size)])  170 us
    pallas_call x1, Pallas kernels, expert_rows(): pl.pallas_call(expert_kernel, grid_spec=pltpu.PrefetchScalarGridSpec(num_...  74.6 us
    all_to_all x1, waiting for transfers between devices, line_to_heads(): both = lax.all_to_all(both, 'far', split_axis=0, concat_axis=0, tiled=True)  53.3 us
    pallas_call x1, Pallas kernels, expert_grads(): pl.pallas_call(grads_kernel, grid=(2, 8), in_specs=[whole_spec(slot_map.s...  46.9 us
    ppermute x3, waiting for transfers between devices, gather_line(): lax.ppermute(above, 'far', down)  34.5 us
    all_gather x1, waiting for transfers between devices, per_device(): ffn_all = lax.all_gather(ffn_in, BLK, axis=0)  32.8 us
    ppermute x52, starting transfers between devices, swap(): return lax.ppermute(values, axis, [(i, i ^ bit) for i in range(size)])  30.1 us
    pallas_call x1, Pallas kernels, attention_backward(): pl.pallas_call(backward_kernel, grid_spec=pltpu.PrefetchScalarGridSpec(nu...  26.4 us
  transfers between devices with their start and end apart: 73, of which 33 were waited for; matrix products, arithmetic and copies ran while one was open for 21% of the time, Pallas kernels for 13%

profile of v2, /device:TPU:0, one launch (start us, length us, event | category | flops | bytes accessed | tf_op | source)
XLA Modules:
  0.0 864.5 jit_solution(11255215285880795)
XLA Ops:
  43.2 9.9 %collective-permute-done.8 = bf16[20,512]{1,0:T(8,128)(2,1)S(1)} collective-permute-done((bf16[20,512]{1,0:T(8,128)(2,1)S(1)}, bf16[20,512]{1,0:T(8,128)(2,1)S(1)}, u32[]{:S(2)}, u32[]{:S(2)}) %collective-permute-start.8) | collective-permute-done | bytes 20512 | tf_op jit(solution)/shard_map/ppermute | solution.py:52
  96.7 17.2 %collective-permute-done.14 = bf16[4,128,768]{2,1,0:T(8,128)(2,1)S(1)} collective-permute-done((bf16[4,128,768]{2,1,0:T(8,128)(2,1)S(1)}, bf16[4,128,768]{2,1,0:T(8,128)(2,1)S(1)}, u32[]{:S(2)}, u32[]{:S(2)}) %collective-permute-start.14) | collective-permute-done | bytes 786464 | tf_op jit(solution)/shard_map/ppermute | solution.py:81
  119.2 15.5 %collective-permute-done.15 = bf16[4,128,768]{2,1,0:T(8,128)(2,1)S(1)} collective-permute-done((bf16[4,128,768]{2,1,0:T(8,128)(2,1)S(1)}, bf16[4,128,768]{2,1,0:T(8,128)(2,1)S(1)}, u32[]{:S(2)}, u32[]{:S(2)}) %collective-permute-start.15) | collective-permute-done | bytes 786464 | tf_op jit(solution)/shard_map/ppermute | solution.py:81
  135.1 14.3 %collective-permute-done.16 = bf16[2,2,2048,256]{3,2,1,0:T(8,128)(2,1)} collective-permute-done((bf16[2,2,2048,256]{3,2,1,0:T(8,128)(2,1)}, bf16[2,2,2048,256]{3,2,1,0:T(8,128)(2,1)}, u32[]{:S(2)}, u32[]{:S(2)}) %collective-permute-start.16) | collective-permute-done | bytes 4194336 | tf_op jit(solution)/shard_map/ppermute | solution.py:52
  184.4 53.3 %all-to-all-done.2 = bf16[4,2,3,256,128]{4,3,2,1,0:T(8,128)(2,1)S(1)} async-done(((bf16[4,2,3,256,128]{4,3,2,1,0:T(8,128)(2,1)}), bf16[4,2,3,256,128]{4,3,2,1,0:T(8,128)(2,1)S(1)}, u32[]{:S(2)}, u32[]{:S(2)}) %all-to-all-start.2) | async-done | bytes 1572896 | tf_op jit(solution)/shard_map/all_to_all | solution.py:158
  244.0 21.7 %attention_forward.1 = (f32[8,256,128]{2,1,0:T(8,128)S(1)}, f32[8,1,256]{2,1,0:T(1,128)S(1)}) custom-call(s32[1]{0:T(128)} %bitcast.core_ref, s32[8]{0:T(128)S(1)} %get-tuple-element.162.low_ref, s32[8]{0:T(128)S(1)} %get-tuple-element.160.open_ref, s32[8]{0:T(128)S(1)} %get-tuple-element.159.close_ref, s32[8]{0:T(128)S(1)} %get-tuple-element.161.high_ref, ...), custom_call_target="tpu_custom_call" | custom-call | tf_op jit(solution)/shard_map/attention_forward/pallas_call | solution.py:351
  266.4 25.3 %all_to_all.50 = bf16[8,256,128]{2,1,0:T(8,128)(2,1)S(1)} all-to-all(bf16[8,256,128]{2,1,0:T(8,128)(2,1)S(1)} %convert_element_type.212), channel_id=1, replica_groups=mesh['ulysses'=4,'far'=4,'near'=2] {'far','near'}, dimensions={0} | all-to-all | bytes 1048576 | tf_op jit(solution)/shard_map/all_to_all | solution.py:183
  304.3 13.3 %collective-permute-done.26 = bf16[128,2048]{1,0:T(8,128)(2,1)S(1)} collective-permute-done((bf16[128,2048]{1,0:T(8,128)(2,1)S(1)}, bf16[128,2048]{1,0:T(8,128)(2,1)S(1)}, u32[]{:S(2)}, u32[]{:S(2)}) %collective-permute-start.26) | collective-permute-done | bytes 524320 | tf_op jit(solution)/shard_map/ppermute | solution.py:52
  322.9 6.0 slice_bitcast_fusion.6
  338.1 7.4 pad_maximum_fusion.gate_ref.gate_tile_ref
  345.5 6.1 pad_maximum_fusion.1.up_ref.up_tile_ref
  351.6 7.6 pad_maximum_fusion.2.down_ref.down_tile_ref
  359.3 32.8 %all-gather.8.cloned.1.call-done = bf16[1024,2048]{1,0:T(8,128)(2,1)} async-done(((bf16[128,2048]{1,0:T(8,128)(2,1)}), bf16[1024,2048]{1,0:T(8,128)(2,1)}) %all-gather.8.cloned.1.call-update) | async-done | bytes 4194320 | tf_op jit(solution)/shard_map/all_gather | solution.py:995
  392.1 74.6 %expert_rows.1 = (bf16[2,640,2048]{2,1,0:T(8,128)(2,1)}, bf16[2,640,2048]{2,1,0:T(8,128)(2,1)}, f32[2,640,1]{2,1,0:T(8,128)}, bf16[2,640,1024]{2,1,0:T(8,128)(2,...) custom-call(s32[1]{0:T(128)} %bitcast.50.blk_ref, ...), custom_call_target="tpu_custom_call" | custom-call | tf_op jit(solution)/shard_map/expert_rows/pallas_call | solution.py:761
  466.8 46.9 %expert_grads.1 = (bf16[2,2,2048,256]{3,2,1,0:T(8,128)(2,1)}, bf16[2,2,2048,256]{3,2,1,0:T(8,128)(2,1)}, bf16[2,2,256,2048]{3,2,1,0:T(8,128)(2,1)}, f32[2,2,2048...) custom-call(f32[8,2,128]{2,1,0:T(2,128)} %copy-done.51, ...), custom_call_target="tpu_custom_call" | custom-call | tf_op jit(solution)/shard_map/expert_grads/pallas_call | solution.py:803
  514.4 7.6 collective-permute-done.35
  528.5 9.3 %all_to_all.51 = f32[8,2,128]{2,1,0:T(2,128)S(1)} all-to-all(f32[8,2,128]{2,1,0:T(2,128)S(1)} %copy-done.52), channel_id=1, replica_groups=mesh['ulysses'=4,'far'=4,'near'=2] {'far','near'}, dimensions={0} | all-to-all | bytes 16384 | tf_op jit(solution)/shard_map/all_to_all | solution.py:1015
  538.6 6.4 convert_element_type.231
  545.0 7.2 fusion.9
  555.2 19.8 %collective-permute-done.36 = bf16[2,256,2048]{2,1,0:T(8,128)(2,1)} collective-permute-done((bf16[2,256,2048]{2,1,0:T(8,128)(2,1)}, bf16[2,256,2048]{2,1,0:T(8,128)(2,1)}, u32[]{:S(2)}, u32[]{:S(2)}) %collective-permute-start.36) | collective-permute-done | bytes 2097184 | tf_op jit(solution)/shard_map/ppermute | solution.py:52
  580.3 11.7 %collective-permute-done.38 = bf16[128,2048]{1,0:T(8,128)(2,1)S(1)} collective-permute-done((bf16[128,2048]{1,0:T(8,128)(2,1)S(1)}, bf16[128,2048]{1,0:T(8,128)(2,1)S(1)}, u32[]{:S(2)}, u32[]{:S(2)}) %collective-permute-start.38) | collective-permute-done | bytes 524320 | tf_op jit(solution)/shard_map/ppermute | solution.py:52
  603.8 7.8 fusion.5
  614.2 14.3 %all-to-all-done.6.do_ref = bf16[8,256,128]{2,1,0:T(8,128)(2,1)S(1)} async-done(((bf16[8,256,128]{2,1,0:T(8,128)(2,1)}), bf16[8,256,128]{2,1,0:T(8,128)(2,1)S(1)}, u32[]{:S(2)}, u32[]{:S(2)}) %all-to-all-start.6) | async-done | bytes 524320 | tf_op jit(solution)/shard_map/all_to_all | solution.py:177
  629.3 26.4 %attention_backward.1 = (bf16[8,256,128]{2,1,0:T(8,128)(2,1)}, f32[8,2,256,128]{3,2,1,0:T(8,128)}, bf16[8,2,256,128]{3,2,1,0:T(8,128)(2,1)}) custom-call(s32[1]{0:T(128)} %bitcast.core_ref, s32[8]{0:T(128)} %copy-done.14, s32[8]{0:T(128)} %copy-done.12, s32[8]{0:T(128)} %copy-done.11, s32[8]{0:T(128)} %copy-done.13, s32[8,1,256]{2,1,0:T(1,128)} %copy-done.9, ...), custom_call_target="tpu_custom_call" | custom-call | tf_op jit(solution)/shard_map/attention_backward/pallas_call | solution.py:378
  669.2 45.2 %collective-permute-done.46 = f32[17,512]{1,0:T(8,128)S(1)} collective-permute-done((f32[17,512]{1,0:T(8,128)S(1)}, f32[17,512]{1,0:T(8,128)S(1)}, u32[]{:S(2)}, u32[]{:S(2)}) %collective-permute-start.46) | collective-permute-done | bytes 34848 | tf_op jit(solution)/shard_map/ppermute | solution.py:52
  720.1 6.9 fusion.3
  743.9 15.0 %reduce-scatter.9.cloned.1.call-done = bf16[1,64,2048]{2,1,0:T(8,128)(2,1)} async-done(((bf16[8,64,2048]{2,1,0:T(8,128)(2,1)}), bf16[1,64,2048]{2,1,0:T(8,128)(2,1)}) %reduce-scatter.9.cloned.1.call-update) | async-done | bytes 262160 | tf_op jit(solution)/shard_map/reduce_scatter | solution.py:1043
  764.2 6.2 convolution_convert_fusion
  792.2 6.8 fusion.1
  807.5 9.8 %collective-permute-done.53 = bf16[2,128,2048]{2,1,0:T(8,128)(2,1)} collective-permute-done((bf16[2,128,2048]{2,1,0:T(8,128)(2,1)}, bf16[2,128,2048]{2,1,0:T(8,128)(2,1)}, u32[]{:S(2)}, u32[]{:S(2)}) %collective-permute-start.53) | collective-permute-done | bytes 1048608 | tf_op jit(solution)/shard_map/ppermute | solution.py:52
  828.0 7.6 collective-permute-done.54
  845.0 9.3 %all-to-all-done.8.in_ref = bf16[8,64,768]{2,1,0:T(8,128)(2,1)S(1)} async-done(((bf16[8,64,768]{2,1,0:T(8,128)(2,1)}), bf16[8,64,768]{2,1,0:T(8,128)(2,1)S(1)}, u32[]{:S(2)}, u32[]{:S(2)}) %all-to-all-start.8) | async-done | bytes 786464 | tf_op jit(solution)/shard_map/all_to_all | solution.py:1111
  (424 shorter events, 279.9 us)
Async XLA Ops:
  7.2 53.8 %collective-permute-start = (bf16[128,2048]{1,0:T(8,128)(2,1)}, bf16[128,2048]{1,0:T(8,128)(2,1)}, u32[]{:S(2)}, u32[]{:S(2)}) collective-permute-start(bf16[128,2048]{1,0:T(8,128)(2,1)} %param.17), channel_id=1, source_target_pairs={{0,8},{8,0},{16,24},{24,16},{1,9},{9,1},{17,25},{25,17},{2,10},{10... | collective-permute-start | bytes 1572872 | tf_op jit(solution)/shard_map/ppermute | solution.py:52
  7.7 51.2 %collective-permute-start.1 = (bf16[128,2048]{1,0:T(8,128)(2,1)}, bf16[128,2048]{1,0:T(8,128)(2,1)}, u32[]{:S(2)}, u32[]{:S(2)}) collective-permute-start(bf16[128,2048]{1,0:T(8,128)(2,1)} %param.17), channel_id=1, source_target_pairs={{0,16},{8,24},{16,0},{24,8},{1,17},{9,25},{17,1},{25,9},{2,18},{10... | collective-permute-start | bytes 1572872 | tf_op jit(solution)/shard_map/ppermute | solution.py:52
  10.3 50.7 %collective-permute-start.3 = (bf16[128,2048]{1,0:T(8,128)(2,1)}, bf16[128,2048]{1,0:T(8,128)(2,1)}, u32[]{:S(2)}, u32[]{:S(2)}) collective-permute-start(bf16[128,2048]{1,0:T(8,128)(2,1)} %param.17), channel_id=1, source_target_pairs={{0,1},{1,0},{2,3},{3,2},{4,5},{5,4},{6,7},{7,6},{8,9},{9,8},{10,11... | collective-permute-start | bytes 1572872 | tf_op jit(solution)/shard_map/ppermute | solution.py:52
  14.7 22.6 %all-to-all-start = ((bf16[8,2,640]{2,1,0:T(2,128)(2,1)}), bf16[8,2,640]{2,1,0:T(2,128)(2,1)S(1)}, u32[]{:S(2)}, u32[]{:S(2)}) async-start(bf16[8,2,640]{2,1,0:T(2,128)(2,1)} %reshape.300), calls=%async_computation | async-start | bytes 40960 | tf_op jit(solution)/shard_map/all_to_all | solution.py:125
  19.6 275.3 %all-gather.6.cloned.1.call-start = ((), (), s32[]{:S(2)}) async-start(), calls=%async_computation.14 | async-start | bytes 2359296 | tf_op jit(solution)/shard_map/all_gather | solution.py:948
  37.4 27.4 %all-to-all-start.1 = ((bf16[8,64,768]{2,1,0:T(8,128)(2,1)}), bf16[8,64,768]{2,1,0:T(8,128)(2,1)S(1)}, u32[]{:S(2)}, u32[]{:S(2)}) async-start(bf16[8,64,768]{2,1,0:T(8,128)(2,1)} %copy.122), calls=%async_computation.1 | async-start | bytes 1572864 | tf_op jit(solution)/shard_map/all_to_all | solution.py:916
  56.0 93.4 %collective-permute-start.16 = (bf16[2,2,2048,256]{3,2,1,0:T(8,128)(2,1)}, bf16[2,2,2048,256]{3,2,1,0:T(8,128)(2,1)}, u32[]{:S(2)}, u32[]{:S(2)}) collective-permute-start(bf16[2,2,2048,256]{3,2,1,0:T(8,128)(2,1)} %pad_maximum_fusion.3), channel_id=1, source_target_pairs={{0,16},{8,24},{16,0},{24,8},{1,17},{9,25},{17,1},{25,9},{2,18},{10... | collective-permute-start | bytes 12582920 | tf_op jit(solution)/shard_map/ppermute | solution.py:52
  64.8 23.4 %collective-permute-start.10 = (bf16[4,128,768]{2,1,0:T(8,128)(2,1)S(1)}, bf16[4,128,768]{2,1,0:T(8,128)(2,1)S(1)}, u32[]{:S(2)}, u32[]{:S(2)}) collective-permute-start(bf16[4,128,768]{2,1,0:T(8,128)(2,1)S(1)} %bitcast.267), channel_id=1, source_target_pairs={{0,2},{2,4},{4,6},{1,3},{3,5},{5,7},{8,10},{10,12},{12,14},{9,11},... | collective-permute-start | bytes 2359304 | tf_op jit(solution)/shard_map/ppermute | solution.py:81
  68.7 22.0 %collective-permute-start.13 = (bf16[4,128,768]{2,1,0:T(8,128)(2,1)S(1)}, bf16[4,128,768]{2,1,0:T(8,128)(2,1)S(1)}, u32[]{:S(2)}, u32[]{:S(2)}) collective-permute-start(bf16[4,128,768]{2,1,0:T(8,128)(2,1)S(1)} %bitcast.268), channel_id=1, source_target_pairs={{6,4},{4,2},{2,0},{7,5},{5,3},{3,1},{14,12},{12,10},{10,8},{15,13}... | collective-permute-start | bytes 2359304 | tf_op jit(solution)/shard_map/ppermute | solution.py:81
  90.8 23.1 %collective-permute-start.14 = (bf16[4,128,768]{2,1,0:T(8,128)(2,1)S(1)}, bf16[4,128,768]{2,1,0:T(8,128)(2,1)S(1)}, u32[]{:S(2)}, u32[]{:S(2)}) collective-permute-start(bf16[4,128,768]{2,1,0:T(8,128)(2,1)S(1)} %collective-permute-done.13), channel_id=1, source_target_pairs={{4,2},{2,0},{5,3},{3,1},{12,10},{10,8},{13,11},{11,9},{20,18},{18,... | collective-permute-start | bytes 2359304 | tf_op jit(solution)/shard_map/ppermute | solution.py:81
  96.0 22.8 %collective-permute-start.12 = (bf16[4,128,768]{2,1,0:T(8,128)(2,1)S(1)}, bf16[4,128,768]{2,1,0:T(8,128)(2,1)S(1)}, u32[]{:S(2)}, u32[]{:S(2)}) collective-permute-start(bf16[4,128,768]{2,1,0:T(8,128)(2,1)S(1)} %collective-permute-done.11), channel_id=1, source_target_pairs={{4,6},{5,7},{12,14},{13,15},{20,22},{21,23},{28,30},{29,31}} | collective-permute-start | bytes 2359304 | tf_op jit(solution)/shard_map/ppermute | solution.py:81
  113.9 20.8 %collective-permute-start.15 = (bf16[4,128,768]{2,1,0:T(8,128)(2,1)S(1)}, bf16[4,128,768]{2,1,0:T(8,128)(2,1)S(1)}, u32[]{:S(2)}, u32[]{:S(2)}) collective-permute-start(bf16[4,128,768]{2,1,0:T(8,128)(2,1)S(1)} %collective-permute-done.14), channel_id=1, source_target_pairs={{2,0},{3,1},{10,8},{11,9},{18,16},{19,17},{26,24},{27,25}} | collective-permute-start | bytes 2359304 | tf_op jit(solution)/shard_map/ppermute | solution.py:81
  178.6 59.2 %all-to-all-start.2 = ((bf16[4,2,3,256,128]{4,3,2,1,0:T(8,128)(2,1)}), bf16[4,2,3,256,128]{4,3,2,1,0:T(8,128)(2,1)S(1)}, u32[]{:S(2)}, u32[]{:S(2)}) async-start(bf16[4,2,3,256,128]{4,3,2,1,0:T(8,128)(2,1)} %bitcast.251), calls=%async_computation.2 | async-start | bytes 3145728 | tf_op jit(solution)/shard_map/all_to_all | solution.py:158
  183.6 175.7 %all-gather.10.cloned.1.call-start = ((), (), s32[]{:S(2)}) async-start(), calls=%async_computation.20 | async-start | bytes 4718592 | tf_op jit(solution)/shard_map/all_gather | solution.py:949
  184.4 207.8 %all-gather.8.cloned.1.call-start = ((), (), s32[]{:S(2)}) async-start(), calls=%async_computation.19 | async-start | bytes 4718592 | tf_op jit(solution)/shard_map/all_gather | solution.py:995
  239.2 55.7 %collective-permute-start.23 = (bf16[2,256,2048]{2,1,0:T(8,128)(2,1)}, bf16[2,256,2048]{2,1,0:T(8,128)(2,1)}, u32[]{:S(2)}, u32[]{:S(2)}) collective-permute-start(bf16[2,256,2048]{2,1,0:T(8,128)(2,1)} %convert_element_type.209), channel_id=1, source_target_pairs={{0,16},{8,24},{16,0},{24,8},{1,17},{9,25},{17,1},{25,9},{2,18},{10... | collective-permute-start | bytes 6291464 | tf_op jit(solution)/shard_map/ppermute | solution.py:52
  334.0 25.3 %all-to-all-start.4 = ((f32[8,2,128]{2,1,0:T(2,128)}), f32[8,2,128]{2,1,0:T(2,128)S(1)}, u32[]{:S(2)}, u32[]{:S(2)}) async-start(f32[8,2,128]{2,1,0:T(2,128)} %bitcast.52), calls=%async_computation.4 | async-start | bytes 16384 | tf_op jit(solution)/shard_map/all_to_all | solution.py:942
  337.3 216.7 %reduce-scatter.5.cloned.1.call-start = ((), (), s32[]{:S(2)}) async-start(), calls=%async_computation.15 | async-start | bytes 4718592 | tf_op jit(solution)/shard_map/reduce_scatter | solution.py:1006
  466.8 260.4 %reduce-scatter.7.cloned.1.call-start = ((), (), s32[]{:S(2)}) async-start(), calls=%async_computation.16 | async-start | bytes 4718592 | tf_op jit(solution)/shard_map/reduce_scatter | solution.py:1024
  513.8 24.0 %collective-permute-start.33 = (bf16[2,2,2048,256]{3,2,1,0:T(8,128)(2,1)}, bf16[2,2,2048,256]{3,2,1,0:T(8,128)(2,1)S(1)}, u32[]{:S(2)}, u32[]{:S(2)}) collective-permute-start(bf16[2,2,2048,256]{3,2,1,0:T(8,128)(2,1)} %get-tuple-element.109), channel_id=1, source_target_pairs={{0,8},{8,0},{16,24},{24,16},{1,9},{9,1},{17,25},{25,17},{2,10},{10... | collective-permute-start | bytes 12582920 | tf_op jit(solution)/shard_map/ppermute | solution.py:52
  514.3 24.3 %collective-permute-start.34 = (bf16[2,2,2048,256]{3,2,1,0:T(8,128)(2,1)}, bf16[2,2,2048,256]{3,2,1,0:T(8,128)(2,1)}, u32[]{:S(2)}, u32[]{:S(2)}) collective-permute-start(bf16[2,2,2048,256]{3,2,1,0:T(8,128)(2,1)} %get-tuple-element.111), channel_id=1, source_target_pairs={{0,8},{8,0},{16,24},{24,16},{1,9},{9,1},{17,25},{25,17},{2,10},{10... | collective-permute-start | bytes 12582920 | tf_op jit(solution)/shard_map/ppermute | solution.py:52
  527.0 48.0 %collective-permute-start.36 = (bf16[2,256,2048]{2,1,0:T(8,128)(2,1)}, bf16[2,256,2048]{2,1,0:T(8,128)(2,1)}, u32[]{:S(2)}, u32[]{:S(2)}) collective-permute-start(bf16[2,256,2048]{2,1,0:T(8,128)(2,1)} %fusion.11), channel_id=1, source_target_pairs={{0,16},{8,24},{16,0},{24,8},{1,17},{9,25},{17,1},{25,9},{2,18},{10... | collective-permute-start | bytes 6291464 | tf_op jit(solution)/shard_map/ppermute | solution.py:52
  598.0 57.8 %collective-permute-start.41 = (bf16[2,2048,256]{2,1,0:T(8,128)(2,1)}, bf16[2,2048,256]{2,1,0:T(8,128)(2,1)S(1)}, u32[]{:S(2)}, u32[]{:S(2)}) collective-permute-start(bf16[2,2048,256]{2,1,0:T(8,128)(2,1)} %fusion.9), channel_id=1, source_target_pairs={{0,16},{8,24},{16,0},{24,8},{1,17},{9,25},{17,1},{25,9},{2,18},{10... | collective-permute-start | bytes 6291464 | tf_op jit(solution)/shard_map/ppermute | solution.py:52
  600.2 28.3 %all-to-all-start.6 = ((bf16[8,256,128]{2,1,0:T(8,128)(2,1)}), bf16[8,256,128]{2,1,0:T(8,128)(2,1)S(1)}, u32[]{:S(2)}, u32[]{:S(2)}) async-start(bf16[8,256,128]{2,1,0:T(8,128)(2,1)} %bitcast.80), calls=%async_computation.7 | async-start | bytes 1048576 | tf_op jit(solution)/shard_map/all_to_all | solution.py:177
  603.7 155.1 %reduce-scatter.9.cloned.1.call-start = ((), (), s32[]{:S(2)}) async-start(), calls=%async_computation.17 | async-start | bytes 2359296 | tf_op jit(solution)/shard_map/reduce_scatter | solution.py:1043
  661.8 58.2 %all-to-all-start.7 = ((bf16[4,2,3,256,128]{4,3,2,1,0:T(8,128)(2,1)}), bf16[4,2,3,256,128]{4,3,2,1,0:T(8,128)(2,1)S(1)}, u32[]{:S(2)}, u32[]{:S(2)}) async-start(bf16[4,2,3,256,128]{4,3,2,1,0:T(8,128)(2,1)} %pad_maximum_fusion.4), calls=%async_computation.8 | async-start | bytes 3145728 | tf_op jit(solution)/shard_map/all_to_all | solution.py:165
  665.4 173.3 %reduce-scatter.11.cloned.1.call-start = ((), (), s32[]{:S(2)}) async-start(), calls=%async_computation.18 | async-start | bytes 3932160 | tf_op jit(solution)/shard_map/reduce_scatter | solution.py:1081
  665.4 61.7 %collective-permute-start.47 = (bf16[2,2048,256]{2,1,0:T(8,128)(2,1)}, bf16[2,2048,256]{2,1,0:T(8,128)(2,1)}, u32[]{:S(2)}, u32[]{:S(2)}) collective-permute-start(bf16[2,2048,256]{2,1,0:T(8,128)(2,1)} %fusion.10), channel_id=1, source_target_pairs={{0,16},{8,24},{16,0},{24,8},{1,17},{9,25},{17,1},{25,9},{2,18},{10... | collective-permute-start | bytes 6291464 | tf_op jit(solution)/shard_map/ppermute | solution.py:52
  668.6 45.8 %collective-permute-start.46 = (f32[17,512]{1,0:T(8,128)S(1)}, f32[17,512]{1,0:T(8,128)S(1)}, u32[]{:S(2)}, u32[]{:S(2)}) collective-permute-start(f32[17,512]{1,0:T(8,128)S(1)} %get-tuple-element.177), channel_id=1, source_target_pairs={{0,16},{8,24},{16,0},{24,8},{1,17},{9,25},{17,1},{25,9},{2,18},{10... | collective-permute-start | bytes 104456 | tf_op jit(solution)/shard_map/ppermute | solution.py:52
  669.2 45.2 %collective-permute-start.44 = (f32[17,512]{1,0:T(8,128)S(1)}, f32[17,512]{1,0:T(8,128)S(1)}, u32[]{:S(2)}, u32[]{:S(2)}) collective-permute-start(f32[17,512]{1,0:T(8,128)S(1)} %get-tuple-element.176), channel_id=1, source_target_pairs={{0,8},{8,0},{16,24},{24,16},{1,9},{9,1},{17,25},{25,17},{2,10},{10... | collective-permute-start | bytes 104456 | tf_op jit(solution)/shard_map/ppermute | solution.py:52
  791.4 25.9 %collective-permute-start.53 = (bf16[2,128,2048]{2,1,0:T(8,128)(2,1)}, bf16[2,128,2048]{2,1,0:T(8,128)(2,1)}, u32[]{:S(2)}, u32[]{:S(2)}) collective-permute-start(bf16[2,128,2048]{2,1,0:T(8,128)(2,1)} %pad_maximum_fusion.7), channel_id=1, source_target_pairs={{0,1},{1,0},{2,3},{3,2},{4,5},{5,4},{6,7},{7,6},{8,9},{9,8},{10,11... | collective-permute-start | bytes 3145736 | tf_op jit(solution)/shard_map/ppermute | solution.py:52
  803.5 21.9 %all-to-all-start.9 = ((f32[8,1,1280]{2,1,0:T(1,128)}), f32[8,1,1280]{2,1,0:T(1,128)S(1)}, u32[]{:S(2)}, u32[]{:S(2)}) async-start(f32[8,1,1280]{2,1,0:T(1,128)} %reshape.302), calls=%async_computation.13 | async-start | bytes 81920 | tf_op jit(solution)/shard_map/all_to_all | solution.py:135
  (100 other events, 1379.5 us)
Sparse Core Ops, SparseCore 0:
  23.1 51.6 all-gather.5
  186.6 104.7 all-gather.9
  320.5 71.5 all-gather.7
  466.9 86.2 reduce-scatter.4
  575.2 106.8 reduce-scatter.6
  685.5 73.3 reduce-scatter.8
  772.5 59.9 reduce-scatter.10

commit v3 on v2

--- a/solution.py
+++ b/solution.py
@@ -113,20 +113,22 @@
         got = swap(jnp.stack([core_mine, core_other]).astype(bfloat), 1).astype(single)
         kept.append(mine + got[0])
         sent.append(other + got[1])
-    got = swap(jnp.stack(sent).astype(bfloat), 1, "near").astype(single)
+    got = swap(jnp.stack(sent).astype(bfloat), 1, "near")
     got, beside = tie(got, beside)
+    got = got.astype(single)
     across = swap((kept[1] + got[1]).astype(bfloat), 2)
     return kept[0] + got[0] + across.astype(single), beside
 
 
-def gather_small(values):
-    count, size = values.shape
+def gather_blk_small(values):
+    ulysses_size, count, size = values.shape
     blk_size = lax.axis_size(BLK)
+    mine = jnp.transpose(values, (1, 0, 2)).reshape(count, -1)
     out = lax.all_to_all(
-        jnp.broadcast_to(values, (blk_size, count, size)), BLK, split_axis=0, concat_axis=0, tiled=True
-    )
-    out = jnp.transpose(out, (1, 0, 2)).reshape(count, blk_size * size)
-    return jnp.transpose(gather_ulysses(out), (1, 0, 2)).reshape(count, -1)
+        jnp.broadcast_to(mine, (blk_size,) + mine.shape), BLK, split_axis=0, concat_axis=0, tiled=True
+    )
+    out = out.reshape(blk_size, count, ulysses_size, size)
+    return jnp.transpose(out, (1, 2, 0, 3)).reshape(count, -1)
 
 
 def scatter_sum_blk_small(values):
@@ -167,14 +169,13 @@
     return swap_halves(back, lax.axis_index("ulysses") % 2)
 
 
-def blk_to_heads(values, blk_size):
+def blk_halves(values, blk_size):
     core = lax.axis_index("ulysses") % 2
     groups = blk_size // 8
     rows = values.shape[0] // (2 * groups)
     split = values.reshape(2, groups, rows, 2, 2, HEAD_DIM)
     split = jnp.transpose(split, (0, 4, 1, 3, 2, 5))
-    both = swap_halves(split, core).reshape(blk_size, rows, HEAD_DIM)
-    return lax.all_to_all(both, BLK, split_axis=0, concat_axis=0, tiled=True)
+    return swap_halves(split, core).reshape(blk_size, rows, HEAD_DIM)
 
 
 def blk_from_heads(stacked, blk_size):
@@ -188,6 +189,10 @@
 
 def head_groups(far_size, groups):
     return [[j * groups + p for p in range(groups)] for j in range(far_size // groups)]
+
+
+def kernel_cost(micros):
+    return pl.CostEstimate(flops=micros * 10**9, bytes_accessed=0, transcendentals=0)
 
 
 def dot_nt(a, b):
@@ -362,6 +367,7 @@
         ),
         out_shape=out_shape,
         compiler_params=pltpu.CompilerParams(vmem_limit_bytes=48 << 20),
+        cost_estimate=kernel_cost(22),
         name="attention_forward",
     )(*scalars, pos, begin, query, mine, other)
 
@@ -394,6 +400,7 @@
         ),
         out_shape=out_shape,
         compiler_params=pltpu.CompilerParams(vmem_limit_bytes=60 << 20),
+        cost_estimate=kernel_cost(26),
         name="attention_backward",
     )(*scalars, pos, begin, lse, head_out, query, d_out, mine, other)
 
@@ -497,6 +504,7 @@
             jax.ShapeDtypeStruct((2, 2, 2, HALF_ROWS), single),
         ],
         compiler_params=pltpu.CompilerParams(vmem_limit_bytes=32 << 20),
+        cost_estimate=kernel_cost(5),
         name="projected",
     )(rows, weight)
 
@@ -516,6 +524,7 @@
         ],
         out_specs=split_spec(groups, rows),
         out_shape=jax.ShapeDtypeStruct((2, 2, groups, 2, 3, rows, HEAD_DIM), bfloat),
+        cost_estimate=kernel_cost(5),
         name="rotated_heads",
     )(lin, recips, gains, cosine, sine)
 
@@ -537,6 +546,7 @@
             jax.ShapeDtypeStruct(gains.shape, single),
             jax.ShapeDtypeStruct((2, 2, 2, HALF_ROWS), single),
         ],
+        cost_estimate=kernel_cost(5),
         name="rotated_sums",
     )(d_split, lin, recips, gains, cosine, sine)
 
@@ -552,6 +562,7 @@
         ],
         out_specs=token_spec(lin.shape[1]),
         out_shape=jax.ShapeDtypeStruct(lin.shape, bfloat),
+        cost_estimate=kernel_cost(5),
         name="rotated_back",
     )(d_split, lin, recips, means, gains, cosine, sine)
 
@@ -580,7 +591,7 @@
 
 
 def picks(slot_ref, source, expert, capacity):
-    slots = slot_ref[source, expert : expert + 1, :]
+    slots = slot_ref[source, pl.ds(expert, 1), :]
     rows = lax.broadcasted_iota(jnp.int32, (capacity, slots.shape[1]), 0) + 1
     return slots == rows.astype(single)
 
@@ -601,8 +612,8 @@
     expert, step = pl.program_id(0), pl.program_id(1)
     sources = ffn_ref.shape[0]
     capacity = x_ref.shape[1] // sources
-    part = gate_ref.shape[3]
-    tile = gate_tile_ref.shape[2]
+    part = gate_ref.shape[-1]
+    tile = gate_tile_ref.shape[-2]
 
     @pl.when((expert == 0) & (step == 0))
     def _():
@@ -626,11 +637,11 @@
             value_ref[0, at, :] = value
             grad_ref[at, :] = (value * cot_rows).astype(bfloat)
 
-    for which in range(2):
-        pl.when((expert == which) & (step == 0))(lambda which=which: fill(which))
-
-    def hidden_part(index):
-        w_both = jnp.concatenate([gate_ref[0, 0], up_ref[0, 0]], axis=1)
+    pl.when(step == 0)(lambda: fill(expert))
+
+    @pl.when(step < 4)
+    def _():
+        w_both = jnp.concatenate([gate_ref[0, 0, 0], up_ref[0, 0, 0]], axis=1)
         both = jnp.dot(x_ref[0], w_both, preferred_element_type=single)
         gate_val, up_val = both[:, :part], both[:, part:]
         d_hidden = dot_nt(grad_ref[...], down_ref[0, 0])
@@ -641,32 +652,47 @@
         d_up = (d_hidden * silu).astype(bfloat)
         d_gate_ref[0] = d_gate
         d_up_ref[0] = d_up
-        d_both_ref[:, pl.ds(2 * index * part, part)] = d_gate
-        d_both_ref[:, pl.ds((2 * index + 1) * part, part)] = d_up
-
-    for index in range(4):
-        pl.when(step == index)(lambda index=index: hidden_part(index))
-
-    def row_tile(index, which):
-        weights = [ref[i, 0] for i in range(4) for ref in (gate_tile_ref, up_tile_ref)]
+        at = pl.multiple_of(2 * step * part, part)
+        d_both_ref[:, pl.ds(at, part)] = d_gate
+        d_both_ref[:, pl.ds(pl.multiple_of(at + part, part), part)] = d_up
+
+    @pl.when(step >= 4)
+    def _():
+        weights = [ref[i, 0, 0] for i in range(4) for ref in (gate_tile_ref, up_tile_ref)]
         d_rows = dot_nt(d_both_ref[...], jnp.concatenate(weights, axis=1)).astype(bfloat)
-        at = pl.ds(index * tile, tile)
-        if which == 0:
+        at = pl.ds(pl.multiple_of((step - 4) * tile, tile), tile)
+
+        @pl.when(expert == 0)
+        def _():
             first_ref[:, at] = d_rows
-        else:
+
+        @pl.when(expert == 1)
+        def _():
             spread_tokens(slot_ref, first_ref[:, at], d_rows, out_ref, capacity)
 
-    for index in range(4):
-        for which in range(2):
-            pl.when((step == index + 4) & (expert == which))(
-                lambda index=index, which=which: row_tile(index, which)
-            )
+
+def down_grads_kernel(c_ref, value_ref, hidden_ref, sent_ref, kept_ref, grad_ref):
+    step = pl.program_id(1)
+
+    @pl.when(step == 0)
+    def _():
+        grad_ref[...] = (value_ref[0] * c_ref[0].astype(single)).astype(bfloat)
+
+    down = dot_tn(hidden_ref[0], grad_ref[...])
+
+    @pl.when(step < 2)
+    def _():
+        sent_ref[0, 0] = down.astype(bfloat)
+
+    @pl.when(step >= 2)
+    def _():
+        kept_ref[0, 0] = down
 
 
 def grads_kernel(
     slot_ref, x_ref, c_ref, value_ref, hidden_ref, d_gate_ref, d_up_ref, down_tile_ref,
-    gate_sent_ref, up_sent_ref, down_sent_ref, gate_kept_ref, up_kept_ref, down_kept_ref,
-    d_probs_ref, out_ref, grad_ref, xt_ref, dots_ref, first_ref,
+    gate_sent_ref, up_sent_ref, gate_kept_ref, up_kept_ref,
+    d_probs_ref, out_ref, xt_ref, dots_ref, first_ref,
 ):
     expert, step = pl.program_id(0), pl.program_id(1)
     sources = slot_ref.shape[0]
@@ -676,51 +702,50 @@
 
     @pl.when(step == 0)
     def _():
-        grad_ref[...] = (value_ref[0] * c_ref[0].astype(single)).astype(bfloat)
         xt_ref[...] = jnp.transpose(x_ref[0])
         dots_ref[...] = jnp.zeros_like(dots_ref)
 
-    def weight_part(index, gate_ref, up_ref, down_ref):
+    @pl.when(step < 4)
+    def _():
         d_both = jnp.concatenate([d_gate_ref[0], d_up_ref[0]], axis=1)
         both = jnp.dot(xt_ref[...], d_both, preferred_element_type=single)
-        gate_ref[0, 0] = both[:, :part].astype(gate_ref.dtype)
-        up_ref[0, 0] = both[:, part:].astype(up_ref.dtype)
-        hidden = hidden_ref[0, :, pl.ds(index * part, part)]
-        down_ref[0, 0] = dot_tn(hidden, grad_ref[...]).astype(down_ref.dtype)
-
-    for index in range(4):
-        refs = (
-            (gate_sent_ref, up_sent_ref, down_sent_ref)
-            if index < 2
-            else (gate_kept_ref, up_kept_ref, down_kept_ref)
-        )
-        pl.when(step == index)(lambda index=index, refs=refs: weight_part(index, *refs))
-
-    def out_tile(index, which):
+
+        @pl.when(step < 2)
+        def _():
+            gate_sent_ref[0, 0] = both[:, :part].astype(bfloat)
+            up_sent_ref[0, 0] = both[:, part:].astype(bfloat)
+
+        @pl.when(step >= 2)
+        def _():
+            gate_kept_ref[0, 0] = both[:, :part]
+            up_kept_ref[0, 0] = both[:, part:]
+
+    @pl.when(step >= 4)
+    def _():
         down = jnp.concatenate([down_tile_ref[i, 0] for i in range(4)], axis=0)
         expert_out = jnp.dot(hidden_ref[0], down, preferred_element_type=single)
         expert_out = expert_out.astype(bfloat).astype(single)
-        at = pl.ds(index * tile, tile)
+        at = pl.ds(pl.multiple_of((step - 4) * tile, tile), tile)
         dots_ref[...] += jnp.sum(
             c_ref[0, :, at].astype(single) * expert_out, axis=1, keepdims=True
         )
         weighted = (value_ref[0] * expert_out).astype(bfloat)
-        if which == 0:
+
+        @pl.when(expert == 0)
+        def _():
             first_ref[:, at] = weighted
-        else:
+
+        @pl.when(expert == 1)
+        def _():
             spread_tokens(slot_ref, first_ref[:, at], weighted, out_ref, capacity)
-        if index == 3:
-            for source in range(sources):
-                picked = picks(slot_ref, source, which, capacity)
-                row = dots_ref[source * capacity : (source + 1) * capacity]
-                d_probs_ref[source, which : which + 1, :] = jnp.sum(
-                    jnp.where(picked, row, 0.0), axis=0, keepdims=True
-                )
-
-    for index in range(4):
-        for which in range(2):
-            pl.when((step == index + 4) & (expert == which))(
-                lambda index=index, which=which: out_tile(index, which)
+
+    @pl.when(step == 7)
+    def _():
+        for source in range(sources):
+            picked = picks(slot_ref, source, expert, capacity)
+            row = dots_ref[source * capacity : (source + 1) * capacity]
+            d_probs_ref[source, pl.ds(expert, 1), :] = jnp.sum(
+                jnp.where(picked, row, 0.0), axis=0, keepdims=True
             )
 
 
@@ -749,15 +774,24 @@
     return pl.BlockSpec(block, lambda e, k, *_: (0, 0, e * second_half(k)))
 
 
-def expert_rows(blk, slot_map, ffn_all, cot_all, router_t, gate, up, down, capacity):
+def pair_spec(shape, which):
+    return pl.BlockSpec(
+        (1, 1, 1) + shape[3:], lambda e, k, *_: (first_half(k), which, e, 0, 0)
+    )
+
+
+def pair_tile_spec(shape, which):
+    return pl.BlockSpec(
+        (4, 1, 1, shape[3] // 4, shape[4]), lambda e, k, *_: (0, which, e, second_half(k), 0)
+    )
+
+
+def expert_rows(blk, slot_map, ffn_all, cot_all, router_t, pair, down, capacity):
     sources, tokens, width = ffn_all.shape
-    rows, experts, hidden = sources * capacity, router_t.shape[0], 4 * gate.shape[3]
+    rows, experts, hidden = sources * capacity, router_t.shape[0], 4 * down.shape[2]
     wide = jax.ShapeDtypeStruct((2, rows, width), bfloat)
     narrow = jax.ShapeDtypeStruct((2, rows, hidden), bfloat)
     probs = jax.ShapeDtypeStruct((sources, experts, tokens), single)
-    tile_spec = pl.BlockSpec(
-        (4, 1, width // 4, hidden // 4), lambda e, k, *_: (0, e, second_half(k), 0)
-    )
     return pl.pallas_call(
         expert_kernel,
         grid_spec=pltpu.PrefetchScalarGridSpec(
@@ -765,8 +799,8 @@
             grid=(2, 8),
             in_specs=[
                 whole_spec(slot_map.shape), whole_spec(ffn_all.shape), whole_spec(cot_all.shape),
-                whole_spec(router_t.shape), weight_spec(gate.shape), weight_spec(up.shape),
-                weight_spec(down.shape), tile_spec, tile_spec,
+                whole_spec(router_t.shape), pair_spec(pair.shape, 0), pair_spec(pair.shape, 1),
+                weight_spec(down.shape), pair_tile_spec(pair.shape, 0), pair_tile_spec(pair.shape, 1),
             ],
             out_specs=[
                 rows_spec(rows, width), rows_spec(rows, width), rows_spec(rows, 1),
@@ -783,23 +817,41 @@
             probs, jax.ShapeDtypeStruct(ffn_all.shape, bfloat),
         ],
         compiler_params=pltpu.CompilerParams(vmem_limit_bytes=60 << 20),
+        cost_estimate=kernel_cost(55),
         name="expert_rows",
-    )(blk[None], slot_map, ffn_all, cot_all, router_t, gate, up, down, gate, up)
+    )(blk[None], slot_map, ffn_all, cot_all, router_t, pair, pair, down, pair, pair)
+
+
+def sent_place(k):
+    return jnp.minimum(k, 1)
+
+
+def kept_place(k):
+    return jnp.clip(k - 2, 0, 1)
+
+
+def expert_down_grads(c, value, hidden):
+    rows, width = c.shape[1:]
+    part = hidden.shape[2] // 4
+    shape = (2, 2, part, width)
+    return pl.pallas_call(
+        down_grads_kernel,
+        grid=(2, 4),
+        in_specs=[rows_spec(rows, width), rows_spec(rows, 1), part_spec(rows, part)],
+        out_specs=[weight_spec(shape, sent_place), weight_spec(shape, kept_place)],
+        out_shape=[jax.ShapeDtypeStruct(shape, bfloat), jax.ShapeDtypeStruct(shape, single)],
+        scratch_shapes=[pltpu.VMEM((rows, width), bfloat)],
+        compiler_params=pltpu.CompilerParams(vmem_limit_bytes=40 << 20),
+        cost_estimate=kernel_cost(12),
+        name="expert_down_grads",
+    )(c, value, hidden)
 
 
 def expert_grads(slot_map, x, c, value, hidden, d_gate, d_up, down, tokens):
     rows, width = x.shape[1:]
     part = down.shape[2]
-    wide, tall = (2, 2, width, part), (2, 2, part, width)
+    wide = (2, 2, width, part)
     summed = (slot_map.shape[0], tokens, width)
-
-    def sent(k):
-        return jnp.minimum(k, 1)
-
-    def kept(k):
-        return jnp.clip(k - 2, 0, 1)
-
-    shapes = (wide, wide, tall)
     return pl.pallas_call(
         grads_kernel,
         grid=(2, 8),
@@ -809,32 +861,33 @@
             part_spec(rows, part),
             pl.BlockSpec((4, 1, part, width // 4), lambda e, k: (0, e, 0, second_half(k))),
         ],
-        out_specs=[weight_spec(shape, sent) for shape in shapes]
-        + [weight_spec(shape, kept) for shape in shapes]
+        out_specs=[weight_spec(wide, sent_place)] * 2
+        + [weight_spec(wide, kept_place)] * 2
         + [whole_spec(slot_map.shape), token_tile_spec(summed)],
-        out_shape=[jax.ShapeDtypeStruct(shape, bfloat) for shape in shapes]
-        + [jax.ShapeDtypeStruct(shape, single) for shape in shapes]
+        out_shape=[jax.ShapeDtypeStruct(wide, bfloat)] * 2
+        + [jax.ShapeDtypeStruct(wide, single)] * 2
         + [
             jax.ShapeDtypeStruct(slot_map.shape, single),
             jax.ShapeDtypeStruct(summed, bfloat),
         ],
         scratch_shapes=[
-            pltpu.VMEM((rows, width), bfloat), pltpu.VMEM((width, rows), bfloat),
-            pltpu.VMEM((rows, 1), single), pltpu.VMEM((rows, width), bfloat),
+            pltpu.VMEM((width, rows), bfloat), pltpu.VMEM((rows, 1), single),
+            pltpu.VMEM((rows, width), bfloat),
         ],
         compiler_params=pltpu.CompilerParams(vmem_limit_bytes=60 << 20),
+        cost_estimate=kernel_cost(39),
         name="expert_grads",
     )(slot_map, x, c, value, hidden, d_gate, d_up, down)
 
 
-def plain_experts(blk, slot_map, ffn_all, cot_all, router_t, gate, up, down, capacity):
+def plain_experts(blk, slot_map, ffn_all, cot_all, router_t, pair, down, capacity):
     sources, tokens, width = ffn_all.shape
     count = slot_map.shape[1]
 
     def joined(weights, axis):
         return jnp.concatenate([weights[i] for i in range(4)], axis=axis)
 
-    gate, up, down = joined(gate, 2), joined(up, 2), joined(down, 1)
+    gate, up, down = joined(pair[:, 0], 2), joined(pair[:, 1], 2), joined(down, 1)
     slot_at = jnp.arange(1, capacity + 1, dtype=jnp.int32).astype(single)
     picked = jnp.transpose(slot_map, (1, 0, 2))[:, :, None, :] == slot_at[None, None, :, None]
     picked_low = picked.astype(bfloat)
@@ -877,8 +930,8 @@
     gate_sent, gate_kept = cut(dots("erd,erf->edf", x, d_gate), 2)
     up_sent, up_kept = cut(dots("erd,erf->edf", x, d_up), 2)
     down_sent, down_kept = cut(dots("erf,erd->efd", hidden, grad), 1)
-    return probs, d_part, (
-        gate_sent, up_sent, down_sent, gate_kept, up_kept, down_kept, d_probs, mixed_part
+    return probs, d_part, (down_sent, down_kept), (
+        gate_sent, up_sent, gate_kept, up_kept, d_probs, mixed_part
     )
 
 
@@ -920,12 +973,13 @@
     small = jnp.concatenate(
         [jnp.stack([attn_gain, ffn_gain, query_gain, key_gain]), router.T]
     ).astype(bfloat)
+    projections, small = tie(projections, gather_ulysses(small))
     w_qkv = gather_line(projections, 1).reshape(width, 3 * plane_width)
-    small = gather_small(small)
+    small = gather_blk_small(small)
     gate_mine, up_mine, down_mine = w_gate.astype(bfloat), w_up.astype(bfloat), w_down.astype(bfloat)
     plane_input = gather_plane(block_input).reshape(far_tokens, width)
-    pair_beyond = swap(jnp.stack([gate_mine, up_mine]), 2)
-    w_qkv, pair_beyond = tie(w_qkv, pair_beyond)
+    pair_mine = jnp.stack([gate_mine, up_mine])
+    pair_beyond = swap(pair_mine, 2)
     attn_g = small[0].astype(single)
     ffn_g = small[1].astype(single)
     plane_gains = lax.dynamic_slice_in_dim(
@@ -933,20 +987,15 @@
     ).astype(single)
     router_t = small[4:]
 
-    def gather_expert(mine, beyond):
-        return jnp.stack([swap(mine, 1), swap(beyond, 1), mine, beyond])
-
-    named = expert_ids[:, :, None] == jnp.arange(experts, dtype=jnp.int32)[None, None, :]
-    slot_map = jnp.sum(jnp.where(named, slot_ids[:, :, None] + 1, 0), axis=1)
-    slot_map = slot_map.T.astype(single).reshape(blk_size, local_experts, own_tokens)
-    slot_map = lax.all_to_all(slot_map, BLK, split_axis=0, concat_axis=0, tiled=True)
-
     inputs = block_input.astype(single)
     hat_one, recip_one = norm_parts(inputs)
     normed = (norm_parts(plane_input.astype(single))[0] * attn_g).astype(bfloat)
     lin, squares = projected(normed, w_qkv)
     w_o = lax.all_gather(w_out.astype(bfloat), BLK, axis=0, tiled=True)
-    cot_all = lax.all_gather(cotangent, BLK, axis=0)
+    named = expert_ids[:, :, None] == jnp.arange(experts, dtype=jnp.int32)[None, None, :]
+    slot_map = jnp.sum(jnp.where(named, slot_ids[:, :, None] + 1, 0), axis=1)
+    slot_map = slot_map.T.astype(single).reshape(blk_size, local_experts, own_tokens)
+    squares, pair_beyond, w_o = tie(squares, pair_beyond, w_o)
     squares, down_mine = tie(sum_plane(squares), down_mine)
     down_beyond = swap(down_mine, 2)
     recips = columns(lax.rsqrt(squares / width + NORM_EPSILON))
@@ -954,7 +1003,9 @@
     cosine, sine = angles(far_at - doc_begins(doc_starts, far_at), HEAD_DIM)
     split = rotated_heads(lin, recips, plane_gains, cosine, sine, groups)
     heads_in = line_to_heads(split, far_size)
-    gate_beyond, up_beyond = pair_beyond[0], pair_beyond[1]
+    heads_in, cotangent_sent, slot_map = tie(heads_in, cotangent, slot_map)
+    slot_map = lax.all_to_all(slot_map, BLK, split_axis=0, concat_axis=0, tiled=True)
+    cot_all = lax.all_gather(cotangent_sent, BLK, axis=0)
     part_rows = heads_in.shape[2]
     if groups == 1:
         query, mine = heads_in, heads_in
@@ -963,7 +1014,10 @@
         mine = lax.all_gather(
             heads_in[:, 1:], "far", axis=2, axis_index_groups=head_groups(far_size, groups)
         ).reshape(blk_size, 2, HALF_ROWS, HEAD_DIM)
-    other = swap(mine[:, -2:], 1)
+    other, pair_mine, pair_beyond, down_mine = tie(
+        swap(mine[:, -2:], 1), pair_mine, pair_beyond, down_mine
+    )
+    pair_near, pair_far, down_near = swap(pair_mine, 1), swap(pair_beyond, 1), swap(down_mine, 1)
     query_at = (
         jnp.arange(blk_size, dtype=jnp.int32)[:, None] * blk_tokens
         + core * HALF_ROWS
@@ -977,10 +1031,10 @@
     attended = blk_from_heads(
         head_out.astype(bfloat).reshape(blk_size, part_rows, HEAD_DIM), blk_size
     )
-    attended, down_beyond = tie(attended, down_beyond)
-    expert_gate = gather_expert(gate_mine, gate_beyond)
-    expert_up = gather_expert(up_mine, up_beyond)
-    expert_down = gather_expert(down_mine, down_beyond)
+    attended, down_beyond, pair_near, pair_far, down_near = tie(
+        attended, down_beyond, pair_near, pair_far, down_near
+    )
+    down_far = swap(down_beyond, 1)
     out_part = jnp.dot(attended, w_o, preferred_element_type=single)
 
     def token_rows(values):
@@ -992,35 +1046,42 @@
     hat_two, recip_two = norm_parts(residual_mid)
     ffn_in = (hat_two * ffn_g).astype(bfloat)
 
+    ffn_in, pair_near, pair_far, pair_mine, pair_beyond = tie(
+        ffn_in, pair_near, pair_far, pair_mine, pair_beyond
+    )
     ffn_all = lax.all_gather(ffn_in, BLK, axis=0)
+    expert_pair = jnp.stack([pair_near, pair_far, pair_mine, pair_beyond])
+    expert_down = jnp.stack([down_near, down_far, down_mine, down_beyond])
     if capacity % 16 == 0:
         *kept_rows, probs_all, d_part = expert_rows(
-            blk, slot_map, ffn_all, cot_all, router_t, expert_gate, expert_up, expert_down, capacity
+            blk, slot_map, ffn_all, cot_all, router_t, expert_pair, expert_down, capacity
         )
         *kept_rows, d_part = tie(*kept_rows, d_part)
-        results = expert_grads(slot_map, *kept_rows, expert_down, own_tokens)
+        x, c, value, hidden, d_gate, d_up = kept_rows
+        down_results = expert_down_grads(c, value, hidden)
+        x, *down_results = tie(x, *down_results)
+        results = expert_grads(
+            slot_map, x, c, value, hidden, d_gate, d_up, expert_down, own_tokens
+        )
     else:
-        probs_all, d_part, results = plain_experts(
-            blk, slot_map, ffn_all, cot_all, router_t, expert_gate, expert_up, expert_down, capacity
+        probs_all, d_part, down_results, results = plain_experts(
+            blk, slot_map, ffn_all, cot_all, router_t, expert_pair, expert_down, capacity
         )
     d_ffn_in = lax.psum_scatter(d_part, BLK, scatter_dimension=0).astype(single)
-    gate_sent, up_sent, down_sent, gate_kept, up_kept, down_kept, d_probs, mixed_part = results
-
-    def add_core(sent, kept):
-        got = swap(sent, 1).astype(single)
-        return kept[0] + got[0], (kept[1] + got[1]).astype(bfloat)
-
-    down_kept, down_sent = add_core(down_sent, down_kept)
-    down_across = swap(down_sent, 2)
+    down_sent, down_kept = down_results
+    gate_sent, up_sent, gate_kept, up_kept, d_probs, mixed_part = results
+
     d_probs = lax.all_to_all(d_probs, BLK, split_axis=0, concat_axis=0, tiled=True)
     d_probs = d_probs.reshape(experts, own_tokens)
-    d_probs, gate_kept, up_kept = tie(d_probs, gate_kept, up_kept)
-    gate_kept, gate_sent = add_core(gate_sent, gate_kept)
-    up_kept, up_sent = add_core(up_sent, up_kept)
-    d_ffn_in, mixed_part, gate_sent, up_sent, down_across = tie(
-        d_ffn_in, mixed_part, gate_sent, up_sent, down_across
-    )
-    grad_w_down = down_kept + down_across.astype(single)
+    gate_sent, up_sent, down_got = tie(gate_sent, up_sent, swap(down_sent, 1))
+    gate_got, up_got = swap(gate_sent, 1), swap(up_sent, 1)
+
+    def onward(got, kept):
+        return (kept[1] + got[1].astype(single)).astype(bfloat)
+
+    down_sent = onward(down_got, down_kept)
+    gate_sent = onward(gate_got, gate_kept)
+    d_ffn_in, mixed_part, up_got, gate_sent = tie(d_ffn_in, mixed_part, up_got, gate_sent)
     mixed_sum = lax.psum_scatter(mixed_part, BLK, scatter_dimension=0)
 
     router_probs = lax.dynamic_index_in_dim(probs_all, blk, 0, keepdims=False)
@@ -1033,20 +1094,29 @@
     d_mid = cotangent.astype(single) + norm_back(d_ffn_in * ffn_g, hat_two, recip_two)
 
     d_attn_out = gather_ulysses(d_mid.astype(bfloat)).reshape(blk_tokens, width)
-    d_attn_out, gate_sent = tie(d_attn_out, gate_sent)
+    narrow = scatter_sum_ulysses(
+        lambda bits: lax.dynamic_slice_in_dim(
+            jnp.concatenate([grad_ffn_part[None], grad_router_part]),
+            (uly ^ bits) * local_width, local_width, 1,
+        ),
+        single,
+    )
+    d_attn_out, gate_sent, narrow = tie(d_attn_out, gate_sent, narrow)
     gate_across = swap(gate_sent, 2)
     d_attended = dot_nt(d_attn_out, w_o).astype(bfloat)
     grad_out_part = jnp.einsum("ti,to->io", attended, d_attn_out, preferred_element_type=single)
     grad_out_part = grad_out_part.astype(bfloat).reshape(blk_size, weight_rows, width)
-    d_out = blk_to_heads(d_attended, blk_size).reshape(head_out.shape)
-    d_out, grad_out_part, grad_w_down = tie(d_out, grad_out_part, grad_w_down)
+    d_halves, up_got = tie(blk_halves(d_attended, blk_size), up_got)
+    up_sent = onward(up_got, up_kept)
+    d_out = lax.all_to_all(d_halves, BLK, split_axis=0, concat_axis=0, tiled=True)
+    d_out = d_out.reshape(head_out.shape)
+    d_out, grad_out_part, up_sent = tie(d_out, grad_out_part, up_sent)
+    up_across = swap(up_sent, 2)
     grad_w_out = lax.psum_scatter(grad_out_part, BLK, scatter_dimension=0)
     dq_head, keep, send = attention_backward(
         scalars, query_at, query_begin, lse, head_out, query, d_out, mine, other
     )
-    dq_head, gate_across, up_sent = tie(dq_head, gate_across, up_sent)
-    up_across = swap(up_sent, 2)
-    grad_w_gate = gate_kept + gate_across.astype(single)
+    dq_head, gate_across = tie(dq_head, gate_across)
     d_keys = (keep + swap(send, 1).astype(single)).astype(bfloat)
     if groups > 1:
         moved = jnp.moveaxis(d_keys.reshape(blk_size, 2, groups, part_rows, HEAD_DIM), 2, 0)
@@ -1058,22 +1128,12 @@
         [dq_head.reshape(blk_size, 1, part_rows, HEAD_DIM), d_keys], axis=1
     )
     d_split = line_from_heads(d_stack, far_size)
-    narrow = scatter_sum_ulysses(
-        lambda bits: lax.dynamic_slice_in_dim(
-            jnp.concatenate([grad_ffn_part[None], grad_router_part]),
-            (uly ^ bits) * local_width, local_width, 1,
-        ),
-        single,
-    )
-    d_split, narrow, up_across, mixed_sum, grad_w_gate = tie(
-        d_split, narrow, up_across, mixed_sum, grad_w_gate
-    )
+    d_split, up_across, mixed_sum = tie(d_split, up_across, mixed_sum)
     mixed = (residual_mid + mixed_sum.astype(single)).astype(bfloat)
-    grad_w_up = up_kept + up_across.astype(single)
     gain_parts, means = rotated_sums(d_split, lin, recips, plane_gains, cosine, sine)
-    means = columns(sum_plane(means) / width)
-    means, grad_w_out = tie(means, grad_w_out)
-    grad_w_out = grad_w_out.astype(single)
+    means, down_sent = tie(sum_plane(means), down_sent)
+    down_across = swap(down_sent, 2)
+    means = columns(means / width)
     d_lin = rotated_back(d_split, lin, recips, means, plane_gains, cosine, sine)
     grads = jnp.einsum("td,to->do", normed, d_lin, preferred_element_type=single)
     grads = grads.astype(bfloat).reshape(ulysses_size, far_size, 2 * weight_rows, 3 * plane_width)
@@ -1093,7 +1153,17 @@
         )
         return mine, other
 
-    d_normed, grad_w_up = scatter_sum_plane(near_rows, grad_w_up)
+
+    def whole_sum(kept, got, across):
+        return kept[0] + got[0].astype(single) + across.astype(single)
+
+    grad_w_gate = whole_sum(gate_kept, gate_got, gate_across)
+    grad_w_up = whole_sum(up_kept, up_got, up_across)
+    d_normed, (grad_w_gate, grad_w_up, grad_attn_part, grad_w_out) = scatter_sum_plane(
+        near_rows, (grad_w_gate, grad_w_up, grad_attn_part, grad_w_out)
+    )
+    grad_w_out = grad_w_out.astype(single)
+    grad_w_down = whole_sum(down_kept, down_got, down_across)
     input_grad = d_mid + norm_back(d_normed * attn_g, hat_one, recip_one)
 
     def own_columns(values):

time: 874 us -> 810 us (0.927)
  waiting for transfers between devices: 341 us -> 309 us
  Pallas kernels: 192 us -> 176 us
  other arithmetic: 127 us -> 113 us
    ppermute x52 -> x50, waiting for transfers between devices: 170 us -> 73.9 us  [swap(): return lax.ppermute(values, axis, [(i, i ^ bit) for i in range(size)])]
    all_to_all x1, waiting for transfers between devices: 5.49 us -> 39.6 us  [line_from_heads(): back = lax.all_to_all(back, 'far', split_axis=0, concat_axis=0, tiled=True)]
    pallas_call x1, Pallas kernels: 74.6 us -> 49.4 us  [expert_rows(): pl.pallas_call(expert_kernel, grid_spec=pltpu.PrefetchScalarGridSpec(num_...]
    all_to_all x1, waiting for transfers between devices: 53.3 us -> 36.8 us  [line_to_heads(): both = lax.all_to_all(both, 'far', split_axis=0, concat_axis=0, tiled=True)]
    reduce_scatter x1, waiting for transfers between devices: 15 us -> 0.01 us  [per_device(): grad_w_out = lax.psum_scatter(grad_out_part, BLK, scatter_dimension=0)]
    all_gather x1, waiting for transfers between devices: 32.8 us -> 47.5 us  [per_device(): ffn_all = lax.all_gather(ffn_in, BLK, axis=0)]
    reduce_scatter x1, waiting for transfers between devices: 0.01 us -> 13.5 us  [per_device(): d_ffn_in = lax.psum_scatter(d_part, BLK, scatter_dimension=0).astype(single)]
    pallas_call x0 -> x1, Pallas kernels: none -> 12.5 us  [expert_down_grads(): pl.pallas_call(down_grads_kernel, grid=(2, 4), in_specs=[rows_spec(rows,...]
  transfers between devices with their start and end apart: 73 -> 72, of which waited for: 33 -> 28; matrix products, arithmetic and copies ran while one was open for 21% -> 22% of each run, Pallas kernels for 13% -> 15%
where the time goes in v3:
time: 810 us; the launch traced here: 802 us
  waiting for transfers between devices  309 us (38%)
  Pallas kernels  176 us (22%)
  other arithmetic  113 us (14%)
  starting transfers between devices  74.6 us (9%)
  local copies, waits for them, and re-layouts  59.8 us (7%)
  blocking collectives  28.5 us (4%)
  matrix products  26.1 us (3%)
  between operations  15.8 us (2%)
    ppermute x50, waiting for transfers between devices, swap(): return lax.ppermute(values, axis, [(i, i ^ bit) for i in range(size)])  73.9 us
    pallas_call x1, Pallas kernels, expert_rows(): pl.pallas_call(expert_kernel, grid_spec=pltpu.PrefetchScalarGridSpec(num_...  49.4 us
    all_gather x1, waiting for transfers between devices, per_device(): ffn_all = lax.all_gather(ffn_in, BLK, axis=0)  47.5 us
    pallas_call x1, Pallas kernels, expert_grads(): pl.pallas_call(grads_kernel, grid=(2, 8), in_specs=[whole_spec(slot_map.s...  43.4 us
    ppermute x3, waiting for transfers between devices, gather_line(): lax.ppermute(above, 'far', down)  42.6 us
    all_to_all x1, waiting for transfers between devices, line_from_heads(): back = lax.all_to_all(back, 'far', split_axis=0, concat_axis=0, tiled=True)  39.6 us
    all_to_all x1, waiting for transfers between devices, line_to_heads(): both = lax.all_to_all(both, 'far', split_axis=0, concat_axis=0, tiled=True)  36.8 us
    ppermute x50, starting transfers between devices, swap(): return lax.ppermute(values, axis, [(i, i ^ bit) for i in range(size)])  29.5 us
  transfers between devices with their start and end apart: 72, of which 28 were waited for; matrix products, arithmetic and copies ran while one was open for 22% of the time, Pallas kernels for 15%

profile of v3, /device:TPU:0, one launch (start us, length us, event | category | flops | bytes accessed | tf_op | source)
XLA Modules:
  0.0 802.0 jit_solution(3274776941704698313)
XLA Ops:
  62.9 15.1 %collective-permute-done.10 = bf16[4,128,768]{2,1,0:T(8,128)(2,1)S(1)} collective-permute-done((bf16[4,128,768]{2,1,0:T(8,128)(2,1)S(1)}, bf16[4,128,768]{2,1,0:T(8,128)(2,1)S(1)}, u32[]{:S(2)}, u32[]{:S(2)}) %collective-permute-start.10) | collective-permute-done | bytes 786464 | tf_op jit(solution)/shard_map/ppermute | solution.py:81
  78.6 13.5 %collective-permute-done.13 = bf16[4,128,768]{2,1,0:T(8,128)(2,1)S(1)} collective-permute-done((bf16[4,128,768]{2,1,0:T(8,128)(2,1)S(1)}, bf16[4,128,768]{2,1,0:T(8,128)(2,1)S(1)}, u32[]{:S(2)}, u32[]{:S(2)}) %collective-permute-start.13) | collective-permute-done | bytes 786464 | tf_op jit(solution)/shard_map/ppermute | solution.py:81
  98.1 14.6 %collective-permute-done.14 = bf16[4,128,768]{2,1,0:T(8,128)(2,1)S(1)} collective-permute-done((bf16[4,128,768]{2,1,0:T(8,128)(2,1)S(1)}, bf16[4,128,768]{2,1,0:T(8,128)(2,1)S(1)}, u32[]{:S(2)}, u32[]{:S(2)}) %collective-permute-start.14) | collective-permute-done | bytes 786464 | tf_op jit(solution)/shard_map/ppermute | solution.py:81
  118.1 14.4 %collective-permute-done.15 = bf16[4,128,768]{2,1,0:T(8,128)(2,1)S(1)} collective-permute-done((bf16[4,128,768]{2,1,0:T(8,128)(2,1)S(1)}, bf16[4,128,768]{2,1,0:T(8,128)(2,1)S(1)}, u32[]{:S(2)}, u32[]{:S(2)}) %collective-permute-start.15) | collective-permute-done | bytes 786464 | tf_op jit(solution)/shard_map/ppermute | solution.py:81
  154.3 5.1 rotated_heads.1
  168.2 36.8 %all-to-all-done.2 = bf16[4,2,3,256,128]{4,3,2,1,0:T(8,128)(2,1)S(1)} async-done(((bf16[4,2,3,256,128]{4,3,2,1,0:T(8,128)(2,1)}), bf16[4,2,3,256,128]{4,3,2,1,0:T(8,128)(2,1)S(1)}, u32[]{:S(2)}, u32[]{:S(2)}) %all-to-all-start.2) | async-done | bytes 1572896 | tf_op jit(solution)/shard_map/all_to_all | solution.py:160
  212.8 21.7 %attention_forward.1 = (f32[8,256,128]{2,1,0:T(8,128)S(1)}, f32[8,1,256]{2,1,0:T(1,128)S(1)}) custom-call(s32[1]{0:T(128)} %bitcast.core_ref, s32[8]{0:T(128)S(1)} %get-tuple-element.208.low_ref, s32[8]{0:T(128)S(1)} %get-tuple-element.206.open_ref, s32[8]{0:T(128)S(1)} %get-tuple-element.205.close_ref, s32[8]{0:T(128)S(1)} %get-tuple-element.207.high_ref, ...), custom_call_target="tpu_custom_call" | custom-call | flops 22000001024 | tf_op jit(solution)/shard_map/attention_forward/pallas_call | solution.py:356
  235.3 28.5 %all_to_all.50 = bf16[8,256,128]{2,1,0:T(8,128)(2,1)S(1)} all-to-all(bf16[8,256,128]{2,1,0:T(8,128)(2,1)S(1)} %convert_element_type.242), channel_id=1, replica_groups=mesh['ulysses'=4,'far'=4,'near'=2] {'far','near'}, dimensions={0} | all-to-all | bytes 1048576 | tf_op jit(solution)/shard_map/all_to_all | solution.py:184
  276.4 12.4 %collective-permute-done.29 = bf16[128,2048]{1,0:T(8,128)(2,1)S(1)} collective-permute-done((bf16[128,2048]{1,0:T(8,128)(2,1)S(1)}, bf16[128,2048]{1,0:T(8,128)(2,1)S(1)}, u32[]{:S(2)}, u32[]{:S(2)}) %collective-permute-start.29) | collective-permute-done | bytes 524320 | tf_op jit(solution)/shard_map/ppermute | solution.py:52
  297.4 14.3 %pad_maximum_fusion.gate_ref.up_ref.gate_tile_ref.up_tile_ref = bf16[4,2,2,2048,256]{4,3,2,1,0:T(8,128)(2,1)} fusion(bf16[1,2,2,2048,256]{4,3,2,1,0:T(8,128)(2,1)} %bitcast.63, bf16[1,2,2,2048,256]{4,3,2,1,0:T(8,128)(2,1)} %bitcast.261, bf16[1,2,2,2048,256]{4,3,2,1,0:T(8,128)(2,1)} %bitcast.61, bf16[1,2,2,2048,256]{4,3,2,1,0:T(8,128)(2,1)} %bitcast.60), kind=kLoop, calls=%fused_computation | loop fusion | flops 25165824 | bytes 33554432 | tf_op jit(solution)/shard_map/stack | solution.py:1053
  311.7 6.2 pad_maximum_fusion.1.down_ref.down_tile_ref
  317.9 47.5 %all-gather.8.cloned.1.call-done = bf16[1024,2048]{1,0:T(8,128)(2,1)} async-done(((bf16[128,2048]{1,0:T(8,128)(2,1)}), bf16[1024,2048]{1,0:T(8,128)(2,1)}) %all-gather.8.cloned.1.call-update) | async-done | bytes 4194320 | tf_op jit(solution)/shard_map/all_gather | solution.py:1052
  365.4 49.4 %expert_rows.1 = (bf16[2,640,2048]{2,1,0:T(8,128)(2,1)}, bf16[2,640,2048]{2,1,0:T(8,128)(2,1)}, f32[2,640,1]{2,1,0:T(8,128)}, bf16[2,640,1024]{2,1,0:T(8,128)(2,...) custom-call(s32[1]{0:T(128)} %bitcast.57.blk_ref, ...), custom_call_target="tpu_custom_call" | custom-call | flops 54999998464 | tf_op jit(solution)/shard_map/expert_rows/pallas_call | solution.py:795
  419.1 12.5 %expert_down_grads.1 = (bf16[2,2,256,2048]{3,2,1,0:T(8,128)(2,1)}, f32[2,2,256,2048]{3,2,1,0:T(8,128)}) custom-call(bf16[2,640,2048]{2,1,0:T(8,128)(2,1)S(1)} %copy-done.14, f32[2,640,1]{2,1,0:T(8,128)S(1)} %copy-done.16, bf16[2,640,1024]{2,1,0:T(8,128)(2,1)S(1)} %copy-done.15), custom_call_target="tpu_custom_call" | custom-call | flops 12000000000 | tf_op jit(solution)/shard_map/expert_down_grads/pallas_call | solution.py:837
  431.6 43.4 %expert_grads.1 = (bf16[2,2,2048,256]{3,2,1,0:T(8,128)(2,1)}, bf16[2,2,2048,256]{3,2,1,0:T(8,128)(2,1)}, f32[2,2,2048,256]{3,2,1,0:T(8,128)}, f32[2,2,2048,256]{...) custom-call(f32[8,2,128]{2,1,0:T(2,128)} %copy-done.45, ...), custom_call_target="tpu_custom_call" | custom-call | flops 38999998464 | tf_op jit(solution)/shard_map/expert_grads/pallas_call | solution.py:855
  479.1 6.4 all-to-all-done.5
  487.8 13.5 %reduce-scatter.5.cloned.1.call-done = bf16[1,128,2048]{2,1,0:T(8,128)(2,1)} async-done(((bf16[8,128,2048]{2,1,0:T(8,128)(2,1)}), bf16[1,128,2048]{2,1,0:T(8,128)(2,1)}) %reduce-scatter.5.cloned.1.call-update) | async-done | bytes 524304 | tf_op jit(solution)/shard_map/reduce_scatter | solution.py:1070
  513.6 13.1 %collective-permute-done.39 = f32[17,512]{1,0:T(8,128)S(1)} collective-permute-done((f32[17,512]{1,0:T(8,128)S(1)}, f32[17,512]{1,0:T(8,128)S(1)}, u32[]{:S(2)}, u32[]{:S(2)}) %collective-permute-start.39) | collective-permute-done | bytes 34848 | tf_op jit(solution)/shard_map/ppermute | solution.py:52
  552.6 16.1 %all-to-all-done.6.do_ref = bf16[8,256,128]{2,1,0:T(8,128)(2,1)} async-done(((bf16[8,256,128]{2,1,0:T(8,128)(2,1)}), bf16[8,256,128]{2,1,0:T(8,128)(2,1)}, u32[]{:S(2)}, u32[]{:S(2)}) %all-to-all-start.6) | async-done | bytes 524320 | tf_op jit(solution)/shard_map/all_to_all | solution.py:1111
  568.7 26.4 %attention_backward.1 = (bf16[8,256,128]{2,1,0:T(8,128)(2,1)}, f32[8,2,256,128]{3,2,1,0:T(8,128)}, bf16[8,2,256,128]{3,2,1,0:T(8,128)(2,1)}) custom-call(s32[1]{0:T(128)} %bitcast.core_ref, s32[8]{0:T(128)} %copy-done.10, s32[8]{0:T(128)} %copy-done.8, s32[8]{0:T(128)} %copy-done.7, s32[8]{0:T(128)} %copy-done.9, s32[8,1,256]{2,1,0:T(1,128)} %copy-done.6, ...), custom_call_target="tpu_custom_call" | custom-call | flops 25999998976 | tf_op jit(solution)/shard_map/attention_backward/pallas_call | solution.py:384
  606.3 39.6 %all-to-all-done.7 = bf16[4,2,3,256,128]{4,3,2,1,0:T(8,128)(2,1)S(1)} async-done(((bf16[4,2,3,256,128]{4,3,2,1,0:T(8,128)(2,1)}), bf16[4,2,3,256,128]{4,3,2,1,0:T(8,128)(2,1)S(1)}, u32[]{:S(2)}, u32[]{:S(2)}) %all-to-all-start.7) | async-done | bytes 1572896 | tf_op jit(solution)/shard_map/all_to_all | solution.py:167
  652.9 5.1 rotated_sums.1
  665.2 5.0 fusion.2
  671.3 5.3 rotated_back.1
  676.6 6.3 convolution_convert_fusion
  686.4 7.3 multiply_reduce_fusion
  699.0 5.4 bitcast_add_fusion.2
  715.1 5.1 bitcast_add_fusion.1
  720.2 18.5 %collective-permute-done.50 = bf16[2,128,2048]{2,1,0:T(8,128)(2,1)} collective-permute-done((bf16[2,128,2048]{2,1,0:T(8,128)(2,1)}, bf16[2,128,2048]{2,1,0:T(8,128)(2,1)}, u32[]{:S(2)}, u32[]{:S(2)}) %collective-permute-start.50) | collective-permute-done | bytes 1048608 | tf_op jit(solution)/shard_map/ppermute | solution.py:52
  745.5 7.8 collective-permute-done.54
  759.0 6.7 bitcast_add_fusion
  782.3 9.4 %all-to-all-done.8.in_ref = bf16[8,64,768]{2,1,0:T(8,128)(2,1)S(1)} async-done(((bf16[8,64,768]{2,1,0:T(8,128)(2,1)}), bf16[8,64,768]{2,1,0:T(8,128)(2,1)S(1)}, u32[]{:S(2)}, u32[]{:S(2)}) %all-to-all-start.8) | async-done | bytes 786464 | tf_op jit(solution)/shard_map/all_to_all | solution.py:1181
  (405 shorter events, 253.7 us)
Async XLA Ops:
  7.2 30.5 %collective-permute-start = (bf16[128,2048]{1,0:T(8,128)(2,1)}, bf16[128,2048]{1,0:T(8,128)(2,1)S(1)}, u32[]{:S(2)}, u32[]{:S(2)}) collective-permute-start(bf16[128,2048]{1,0:T(8,128)(2,1)} %param.17), channel_id=1, source_target_pairs={{0,8},{8,0},{16,24},{24,16},{1,9},{9,1},{17,25},{25,17},{2,10},{10... | collective-permute-start | bytes 1572872 | tf_op jit(solution)/shard_map/ppermute | solution.py:52
  7.7 28.4 %collective-permute-start.1 = (bf16[128,2048]{1,0:T(8,128)(2,1)}, bf16[128,2048]{1,0:T(8,128)(2,1)}, u32[]{:S(2)}, u32[]{:S(2)}) collective-permute-start(bf16[128,2048]{1,0:T(8,128)(2,1)} %param.17), channel_id=1, source_target_pairs={{0,16},{8,24},{16,0},{24,8},{1,17},{9,25},{17,1},{25,9},{2,18},{10... | collective-permute-start | bytes 1572872 | tf_op jit(solution)/shard_map/ppermute | solution.py:52
  10.3 35.8 %collective-permute-start.3 = (bf16[128,2048]{1,0:T(8,128)(2,1)}, bf16[128,2048]{1,0:T(8,128)(2,1)}, u32[]{:S(2)}, u32[]{:S(2)}) collective-permute-start(bf16[128,2048]{1,0:T(8,128)(2,1)} %param.17), channel_id=1, source_target_pairs={{0,1},{1,0},{2,3},{3,2},{4,5},{5,4},{6,7},{7,6},{8,9},{9,8},{10,11... | collective-permute-start | bytes 1572872 | tf_op jit(solution)/shard_map/ppermute | solution.py:52
  22.7 118.1 %all-gather.6.cloned.1.call-start = ((), (), s32[]{:S(2)}) async-start(), calls=%async_computation.14 | async-start | bytes 2359296 | tf_op jit(solution)/shard_map/all_gather | solution.py:994
  34.1 106.8 %collective-permute-start.16 = (bf16[2,2,2048,256]{3,2,1,0:T(8,128)(2,1)}, bf16[2,2,2048,256]{3,2,1,0:T(8,128)(2,1)}, u32[]{:S(2)}, u32[]{:S(2)}) collective-permute-start(bf16[2,2,2048,256]{3,2,1,0:T(8,128)(2,1)} %pad_maximum_fusion.2), channel_id=1, source_target_pairs={{0,16},{8,24},{16,0},{24,8},{1,17},{9,25},{17,1},{25,9},{2,18},{10... | collective-permute-start | bytes 12582920 | tf_op jit(solution)/shard_map/ppermute | solution.py:52
  46.1 31.9 %collective-permute-start.10 = (bf16[4,128,768]{2,1,0:T(8,128)(2,1)S(1)}, bf16[4,128,768]{2,1,0:T(8,128)(2,1)S(1)}, u32[]{:S(2)}, u32[]{:S(2)}) collective-permute-start(bf16[4,128,768]{2,1,0:T(8,128)(2,1)S(1)} %bitcast.277), channel_id=1, source_target_pairs={{0,2},{2,4},{4,6},{1,3},{3,5},{5,7},{8,10},{10,12},{12,14},{9,11},... | collective-permute-start | bytes 2359304 | tf_op jit(solution)/shard_map/ppermute | solution.py:81
  53.9 38.2 %collective-permute-start.13 = (bf16[4,128,768]{2,1,0:T(8,128)(2,1)S(1)}, bf16[4,128,768]{2,1,0:T(8,128)(2,1)S(1)}, u32[]{:S(2)}, u32[]{:S(2)}) collective-permute-start(bf16[4,128,768]{2,1,0:T(8,128)(2,1)S(1)} %bitcast.278), channel_id=1, source_target_pairs={{6,4},{4,2},{2,0},{7,5},{5,3},{3,1},{14,12},{12,10},{10,8},{15,13}... | collective-permute-start | bytes 2359304 | tf_op jit(solution)/shard_map/ppermute | solution.py:81
  55.2 38.2 %collective-permute-start.6 = (bf16[128,2048]{1,0:T(8,128)(2,1)}, bf16[128,2048]{1,0:T(8,128)(2,1)S(1)}, u32[]{:S(2)}, u32[]{:S(2)}) collective-permute-start(bf16[128,2048]{1,0:T(8,128)(2,1)} %collective-permute-done.5), channel_id=1, source_target_pairs={{0,8},{8,0},{16,24},{24,16},{1,9},{9,1},{17,25},{25,17},{2,10},{10... | collective-permute-start | bytes 1572872 | tf_op jit(solution)/shard_map/ppermute | solution.py:52
  92.1 20.6 %collective-permute-start.14 = (bf16[4,128,768]{2,1,0:T(8,128)(2,1)S(1)}, bf16[4,128,768]{2,1,0:T(8,128)(2,1)S(1)}, u32[]{:S(2)}, u32[]{:S(2)}) collective-permute-start(bf16[4,128,768]{2,1,0:T(8,128)(2,1)S(1)} %collective-permute-done.13), channel_id=1, source_target_pairs={{4,2},{2,0},{5,3},{3,1},{12,10},{10,8},{13,11},{11,9},{20,18},{18,... | collective-permute-start | bytes 2359304 | tf_op jit(solution)/shard_map/ppermute | solution.py:81
  97.4 20.4 %collective-permute-start.12 = (bf16[4,128,768]{2,1,0:T(8,128)(2,1)S(1)}, bf16[4,128,768]{2,1,0:T(8,128)(2,1)S(1)}, u32[]{:S(2)}, u32[]{:S(2)}) collective-permute-start(bf16[4,128,768]{2,1,0:T(8,128)(2,1)S(1)} %collective-permute-done.11), channel_id=1, source_target_pairs={{4,6},{5,7},{12,14},{13,15},{20,22},{21,23},{28,30},{29,31}} | collective-permute-start | bytes 2359304 | tf_op jit(solution)/shard_map/ppermute | solution.py:81
  164.0 41.1 %all-to-all-start.2 = ((bf16[4,2,3,256,128]{4,3,2,1,0:T(8,128)(2,1)}), bf16[4,2,3,256,128]{4,3,2,1,0:T(8,128)(2,1)S(1)}, u32[]{:S(2)}, u32[]{:S(2)}) async-start(bf16[4,2,3,256,128]{4,3,2,1,0:T(8,128)(2,1)} %bitcast.273), calls=%async_computation.2 | async-start | bytes 3145728 | tf_op jit(solution)/shard_map/all_to_all | solution.py:160
  167.5 150.3 %all-gather.10.cloned.1.call-start = ((), (), s32[]{:S(2)}) async-start(), calls=%async_computation.20 | async-start | bytes 4718592 | tf_op jit(solution)/shard_map/all_gather | solution.py:1008
  206.4 159.0 %all-gather.8.cloned.1.call-start = ((), (), s32[]{:S(2)}) async-start(), calls=%async_computation.19 | async-start | bytes 4718592 | tf_op jit(solution)/shard_map/all_gather | solution.py:1052
  210.0 56.1 %collective-permute-start.24 = (bf16[2,2,2048,256]{3,2,1,0:T(8,128)(2,1)}, bf16[2,2,2048,256]{3,2,1,0:T(8,128)(2,1)}, u32[]{:S(2)}, u32[]{:S(2)}) collective-permute-start(bf16[2,2,2048,256]{3,2,1,0:T(8,128)(2,1)} %pad_maximum_fusion.2), channel_id=1, source_target_pairs={{0,8},{8,0},{16,24},{24,16},{1,9},{9,1},{17,25},{25,17},{2,10},{10... | collective-permute-start | bytes 12582920 | tf_op jit(solution)/shard_map/ppermute | solution.py:52
  210.1 56.0 %collective-permute-start.25 = (bf16[2,2,2048,256]{3,2,1,0:T(8,128)(2,1)}, bf16[2,2,2048,256]{3,2,1,0:T(8,128)(2,1)}, u32[]{:S(2)}, u32[]{:S(2)}) collective-permute-start(bf16[2,2,2048,256]{3,2,1,0:T(8,128)(2,1)} %collective-permute-done.16), channel_id=1, source_target_pairs={{0,8},{8,0},{16,24},{24,16},{1,9},{9,1},{17,25},{25,17},{2,10},{10... | collective-permute-start | bytes 12582920 | tf_op jit(solution)/shard_map/ppermute | solution.py:52
  210.9 55.1 %collective-permute-start.23 = (bf16[2,256,2048]{2,1,0:T(8,128)(2,1)}, bf16[2,256,2048]{2,1,0:T(8,128)(2,1)}, u32[]{:S(2)}, u32[]{:S(2)}) collective-permute-start(bf16[2,256,2048]{2,1,0:T(8,128)(2,1)} %convert_element_type.237), channel_id=1, source_target_pairs={{0,16},{8,24},{16,0},{24,8},{1,17},{9,25},{17,1},{25,9},{2,18},{10... | collective-permute-start | bytes 6291464 | tf_op jit(solution)/shard_map/ppermute | solution.py:52
  211.5 54.6 %collective-permute-start.26 = (bf16[2,256,2048]{2,1,0:T(8,128)(2,1)}, bf16[2,256,2048]{2,1,0:T(8,128)(2,1)}, u32[]{:S(2)}, u32[]{:S(2)}) collective-permute-start(bf16[2,256,2048]{2,1,0:T(8,128)(2,1)} %convert_element_type.237), channel_id=1, source_target_pairs={{0,8},{8,0},{16,24},{24,16},{1,9},{9,1},{17,25},{25,17},{2,10},{10... | collective-permute-start | bytes 6291464 | tf_op jit(solution)/shard_map/ppermute | solution.py:52
  293.7 24.1 %all-to-all-start.4 = ((f32[8,2,128]{2,1,0:T(2,128)}), f32[8,2,128]{2,1,0:T(2,128)S(1)}, u32[]{:S(2)}, u32[]{:S(2)}) async-start(f32[8,2,128]{2,1,0:T(2,128)} %bitcast.52), calls=%async_computation.4 | async-start | bytes 16384 | tf_op jit(solution)/shard_map/all_to_all | solution.py:1007
  297.2 204.1 %reduce-scatter.5.cloned.1.call-start = ((), (), s32[]{:S(2)}) async-start(), calls=%async_computation.15 | async-start | bytes 4718592 | tf_op jit(solution)/shard_map/reduce_scatter | solution.py:1070
  431.6 43.4 %collective-permute-start.31 = (bf16[2,2,256,2048]{3,2,1,0:T(8,128)(2,1)}, bf16[2,2,256,2048]{3,2,1,0:T(8,128)(2,1)}, u32[]{:S(2)}, u32[]{:S(2)}) collective-permute-start(bf16[2,2,256,2048]{3,2,1,0:T(8,128)(2,1)} %get-tuple-element.151), channel_id=1, source_target_pairs={{0,8},{8,0},{16,24},{24,16},{1,9},{9,1},{17,25},{25,17},{2,10},{10... | collective-permute-start | bytes 12582920 | tf_op jit(solution)/shard_map/ppermute | solution.py:52
  475.0 27.4 %collective-permute-start.33 = (bf16[2,2,2048,256]{3,2,1,0:T(8,128)(2,1)}, bf16[2,2,2048,256]{3,2,1,0:T(8,128)(2,1)}, u32[]{:S(2)}, u32[]{:S(2)}) collective-permute-start(bf16[2,2,2048,256]{3,2,1,0:T(8,128)(2,1)} %get-tuple-element.154), channel_id=1, source_target_pairs={{0,8},{8,0},{16,24},{24,16},{1,9},{9,1},{17,25},{25,17},{2,10},{10... | collective-permute-start | bytes 12582920 | tf_op jit(solution)/shard_map/ppermute | solution.py:52
  475.6 31.7 %collective-permute-start.32 = (bf16[2,2,2048,256]{3,2,1,0:T(8,128)(2,1)}, bf16[2,2,2048,256]{3,2,1,0:T(8,128)(2,1)}, u32[]{:S(2)}, u32[]{:S(2)}) collective-permute-start(bf16[2,2,2048,256]{3,2,1,0:T(8,128)(2,1)} %get-tuple-element.152), channel_id=1, source_target_pairs={{0,8},{8,0},{16,24},{24,16},{1,9},{9,1},{17,25},{25,17},{2,10},{10... | collective-permute-start | bytes 12582920 | tf_op jit(solution)/shard_map/ppermute | solution.py:52
  479.0 173.8 %reduce-scatter.7.cloned.1.call-start = ((), (), s32[]{:S(2)}) async-start(), calls=%async_computation.16 | async-start | bytes 4718592 | tf_op jit(solution)/shard_map/reduce_scatter | solution.py:1085
  537.0 58.1 %collective-permute-start.41 = (bf16[2,2048,256]{2,1,0:T(8,128)(2,1)}, bf16[2,2048,256]{2,1,0:T(8,128)(2,1)S(1)}, u32[]{:S(2)}, u32[]{:S(2)}) collective-permute-start(bf16[2,2048,256]{2,1,0:T(8,128)(2,1)} %fusion), channel_id=1, source_target_pairs={{0,16},{8,24},{16,0},{24,8},{1,17},{9,25},{17,1},{25,9},{2,18},{10... | collective-permute-start | bytes 6291464 | tf_op jit(solution)/shard_map/ppermute | solution.py:52
  539.2 29.5 %all-to-all-start.6 = ((bf16[8,256,128]{2,1,0:T(8,128)(2,1)}), bf16[8,256,128]{2,1,0:T(8,128)(2,1)}, u32[]{:S(2)}, u32[]{:S(2)}) async-start(bf16[8,256,128]{2,1,0:T(8,128)(2,1)} %bitcast.84), calls=%async_computation.7 | async-start | bytes 1048576 | tf_op jit(solution)/shard_map/all_to_all | solution.py:1111
  601.2 44.8 %all-to-all-start.7 = ((bf16[4,2,3,256,128]{4,3,2,1,0:T(8,128)(2,1)}), bf16[4,2,3,256,128]{4,3,2,1,0:T(8,128)(2,1)S(1)}, u32[]{:S(2)}, u32[]{:S(2)}) async-start(bf16[4,2,3,256,128]{4,3,2,1,0:T(8,128)(2,1)} %pad_maximum_fusion.3), calls=%async_computation.8 | async-start | bytes 3145728 | tf_op jit(solution)/shard_map/all_to_all | solution.py:167
  604.7 115.4 %reduce-scatter.9.cloned.1.call-start = ((), (), s32[]{:S(2)}) async-start(), calls=%async_computation.17 | async-start | bytes 2359296 | tf_op jit(solution)/shard_map/reduce_scatter | solution.py:1115
  604.8 48.1 %collective-permute-start.44 = (bf16[2,2048,256]{2,1,0:T(8,128)(2,1)}, bf16[2,2048,256]{2,1,0:T(8,128)(2,1)}, u32[]{:S(2)}, u32[]{:S(2)}) collective-permute-start(bf16[2,2048,256]{2,1,0:T(8,128)(2,1)} %fusion.1), channel_id=1, source_target_pairs={{0,16},{8,24},{16,0},{24,8},{1,17},{9,25},{17,1},{25,9},{2,18},{10... | collective-permute-start | bytes 6291464 | tf_op jit(solution)/shard_map/ppermute | solution.py:52
  646.9 129.1 %reduce-scatter.11.cloned.1.call-start = ((), (), s32[]{:S(2)}) async-start(), calls=%async_computation.18 | async-start | bytes 3932160 | tf_op jit(solution)/shard_map/reduce_scatter | solution.py:1141
  704.5 54.5 %collective-permute-start.55 = (bf16[2,256,2048]{2,1,0:T(8,128)(2,1)}, bf16[2,256,2048]{2,1,0:T(8,128)(2,1)}, u32[]{:S(2)}, u32[]{:S(2)}) collective-permute-start(bf16[2,256,2048]{2,1,0:T(8,128)(2,1)} %fusion.2), channel_id=1, source_target_pairs={{0,16},{8,24},{16,0},{24,8},{1,17},{9,25},{17,1},{25,9},{2,18},{10... | collective-permute-start | bytes 6291464 | tf_op jit(solution)/shard_map/ppermute | solution.py:52
  713.5 25.2 %collective-permute-start.50 = (bf16[2,128,2048]{2,1,0:T(8,128)(2,1)}, bf16[2,128,2048]{2,1,0:T(8,128)(2,1)}, u32[]{:S(2)}, u32[]{:S(2)}) collective-permute-start(bf16[2,128,2048]{2,1,0:T(8,128)(2,1)} %pad_maximum_fusion.6), channel_id=1, source_target_pairs={{0,1},{1,0},{2,3},{3,2},{4,5},{5,4},{6,7},{7,6},{8,9},{9,8},{10,11... | collective-permute-start | bytes 3145736 | tf_op jit(solution)/shard_map/ppermute | solution.py:52
  744.2 25.2 %collective-permute-start.51 = (bf16[128,2048]{1,0:T(8,128)(2,1)}, bf16[128,2048]{1,0:T(8,128)(2,1)S(1)}, u32[]{:S(2)}, u32[]{:S(2)}) collective-permute-start(bf16[128,2048]{1,0:T(8,128)(2,1)} %fusion.17), channel_id=1, source_target_pairs={{0,16},{8,24},{16,0},{24,8},{1,17},{9,25},{17,1},{25,9},{2,18},{10... | collective-permute-start | bytes 1572872 | tf_op jit(solution)/shard_map/ppermute | solution.py:52
  (94 other events, 984.4 us)
Sparse Core Ops, SparseCore 0:
  26.2 61.9 all-gather.5
  206.5 77.2 all-gather.9
  293.0 72.3 all-gather.7
  414.9 86.3 reduce-scatter.4
  513.8 109.4 reduce-scatter.6
  647.0 66.6 reduce-scatter.8
  716.0 59.9 reduce-scatter.10

commit v4 on v3

--- a/solution.py
+++ b/solution.py
@@ -202,9 +202,16 @@
 def key_loops(low_ref, open_ref, close_ref, high_ref, index, step, carry):
     low, opened = low_ref[index], open_ref[index]
     closed, high = close_ref[index], high_ref[index]
-    carry = lax.fori_loop(low, opened, lambda kb, c: step(kb, c, True), carry)
-    carry = lax.fori_loop(opened, closed, lambda kb, c: step(kb, c, False), carry)
-    return lax.fori_loop(closed, high, lambda kb, c: step(kb, c, True), carry)
+    pairs = (closed - opened) // 2
+    paired = opened + 2 * pairs
+
+    def two(pair, carry):
+        return step(opened + 2 * pair, carry, False, 2 * KEY_ROWS)
+
+    carry = lax.fori_loop(low, opened, lambda kb, c: step(kb, c, True, KEY_ROWS), carry)
+    carry = lax.fori_loop(0, pairs, two, carry)
+    carry = lax.fori_loop(paired, closed, lambda kb, c: step(kb, c, False, KEY_ROWS), carry)
+    return lax.fori_loop(closed, high, lambda kb, c: step(kb, c, True, KEY_ROWS), carry)
 
 
 def allowed(start, pos, begin):
@@ -242,10 +249,10 @@
     pos, begin = pos_ref[0], begin_ref[0]
     rows = query.shape[0]
 
-    def step(block, carry, masked):
+    def step(block, carry, masked, size):
         top, total, acc = carry
         start = pl.multiple_of(block * KEY_ROWS, KEY_ROWS)
-        scores = dot_nt(k_ref[pl.ds(start, KEY_ROWS), :], query) * LOG2_SCALE
+        scores = dot_nt(k_ref[pl.ds(start, size), :], query) * LOG2_SCALE
         if masked:
             scores = jnp.where(allowed(start, pos, begin), scores, MASKED_SCORE)
         new_top = jnp.maximum(top, jnp.max(scores, axis=0, keepdims=True))
@@ -253,7 +260,7 @@
         shrink = jnp.exp2(top - new_top)
         total = total * shrink + jnp.sum(probs, axis=0, keepdims=True)
         acc = acc * shrink + jnp.dot(
-            vt_ref[:, pl.ds(start, KEY_ROWS)], probs.astype(bfloat), preferred_element_type=single
+            vt_ref[:, pl.ds(start, size)], probs.astype(bfloat), preferred_element_type=single
         )
         return new_top, total, acc
 
@@ -296,9 +303,9 @@
     products = d_out.astype(single) * o_ref[0]
     delta = jnp.sum(jnp.transpose(products), axis=0, keepdims=True)
 
-    def step(block, acc, masked):
+    def step(block, acc, masked, size):
         start = pl.multiple_of(block * KEY_ROWS, KEY_ROWS)
-        rows = pl.ds(start, KEY_ROWS)
+        rows = pl.ds(start, size)
         scores = dot_nt(k_ref[rows, :], query) * LOG2_SCALE
         probs = jnp.exp2(scores - lse)
         if masked:
@@ -400,7 +407,7 @@
         ),
         out_shape=out_shape,
         compiler_params=pltpu.CompilerParams(vmem_limit_bytes=60 << 20),
-        cost_estimate=kernel_cost(26),
+        cost_estimate=kernel_cost(1),
         name="attention_backward",
     )(*scalars, pos, begin, lse, head_out, query, d_out, mine, other)
 
@@ -1081,8 +1088,10 @@
 
     down_sent = onward(down_got, down_kept)
     gate_sent = onward(gate_got, gate_kept)
-    d_ffn_in, mixed_part, up_got, gate_sent = tie(d_ffn_in, mixed_part, up_got, gate_sent)
-    mixed_sum = lax.psum_scatter(mixed_part, BLK, scatter_dimension=0)
+    summed = lax.dynamic_update_slice(
+        jnp.zeros((blk_size, weight_rows + own_tokens, width), bfloat), mixed_part, (0, weight_rows, 0)
+    )
+    d_ffn_in, summed, up_got, gate_sent = tie(d_ffn_in, summed, up_got, gate_sent)
 
     router_probs = lax.dynamic_index_in_dim(probs_all, blk, 0, keepdims=False)
     d_logits = (
@@ -1112,11 +1121,11 @@
     d_out = d_out.reshape(head_out.shape)
     d_out, grad_out_part, up_sent = tie(d_out, grad_out_part, up_sent)
     up_across = swap(up_sent, 2)
-    grad_w_out = lax.psum_scatter(grad_out_part, BLK, scatter_dimension=0)
+    summed = lax.dynamic_update_slice(summed, grad_out_part, (0, 0, 0))
+    summed = lax.psum_scatter(summed, BLK, scatter_dimension=0)
     dq_head, keep, send = attention_backward(
         scalars, query_at, query_begin, lse, head_out, query, d_out, mine, other
     )
-    dq_head, gate_across = tie(dq_head, gate_across)
     d_keys = (keep + swap(send, 1).astype(single)).astype(bfloat)
     if groups > 1:
         moved = jnp.moveaxis(d_keys.reshape(blk_size, 2, groups, part_rows, HEAD_DIM), 2, 0)
@@ -1124,20 +1133,21 @@
             moved, "far", scatter_dimension=0, axis_index_groups=head_groups(far_size, groups)
         )
         d_keys = moved
+    d_keys, gate_across = tie(d_keys, gate_across)
     d_stack = jnp.concatenate(
         [dq_head.reshape(blk_size, 1, part_rows, HEAD_DIM), d_keys], axis=1
     )
     d_split = line_from_heads(d_stack, far_size)
-    d_split, up_across, mixed_sum = tie(d_split, up_across, mixed_sum)
-    mixed = (residual_mid + mixed_sum.astype(single)).astype(bfloat)
+    d_split, up_across = tie(d_split, up_across)
     gain_parts, means = rotated_sums(d_split, lin, recips, plane_gains, cosine, sine)
-    means, down_sent = tie(sum_plane(means), down_sent)
-    down_across = swap(down_sent, 2)
+    means, first_down = tie(sum_plane(means), down_sent[0])
+    first_down = swap(first_down, 2)
     means = columns(means / width)
     d_lin = rotated_back(d_split, lin, recips, means, plane_gains, cosine, sine)
     grads = jnp.einsum("td,to->do", normed, d_lin, preferred_element_type=single)
     grads = grads.astype(bfloat).reshape(ulysses_size, far_size, 2 * weight_rows, 3 * plane_width)
     grads = jnp.transpose(grads, (1, 0, 2, 3)).reshape(-1, 3 * plane_width)
+    grads, d_lin, summed = tie(grads, d_lin, summed)
     grads = lax.psum_scatter(grads, "far", scatter_dimension=0, tiled=True)
     d_normed_part = dot_nt(d_lin, w_qkv)
     grad_attn_part = jnp.sum(d_normed_part * norm_parts(plane_input.astype(single))[0], axis=0)
@@ -1159,10 +1169,15 @@
 
     grad_w_gate = whole_sum(gate_kept, gate_got, gate_across)
     grad_w_up = whole_sum(up_kept, up_got, up_across)
-    d_normed, (grad_w_gate, grad_w_up, grad_attn_part, grad_w_out) = scatter_sum_plane(
-        near_rows, (grad_w_gate, grad_w_up, grad_attn_part, grad_w_out)
-    )
-    grad_w_out = grad_w_out.astype(single)
+    d_normed, beside = scatter_sum_plane(
+        near_rows,
+        (grad_w_gate, grad_w_up, grad_attn_part, summed, first_down, down_sent[1]),
+    )
+    grad_w_gate, grad_w_up, grad_attn_part, summed, first_down, second_down = beside
+    d_normed, second_down = tie(d_normed, swap(second_down, 2))
+    down_across = jnp.stack([first_down, second_down])
+    grad_w_out = summed[:weight_rows].astype(single)
+    mixed = (residual_mid + summed[weight_rows:].astype(single)).astype(bfloat)
     grad_w_down = whole_sum(down_kept, down_got, down_across)
     input_grad = d_mid + norm_back(d_normed * attn_g, hat_one, recip_one)
 

time: 810 us -> 801 us (0.989)
    ppermute x50 -> x51, waiting for transfers between devices: 73.9 us -> 89.4 us  [swap(): return lax.ppermute(values, axis, [(i, i ^ bit) for i in range(size)])]
    all_to_all x1, waiting for transfers between devices: 16.1 us -> 7.49 us  [per_device(): lax.all_to_all(d_halves, BLK, split_axis=0, concat_axis=0, tiled=True)]
    unnamed x115 -> x113, local copies, waits for them, and re-layouts: 20.4 us -> 17.8 us
    ppermute x50 -> x51, starting transfers between devices: 29.5 us -> 30.5 us  [swap(): return lax.ppermute(values, axis, [(i, i ^ bit) for i in range(size)])]
  transfers between devices with their start and end apart: 72 -> 72, of which waited for: 28 -> 31; matrix products, arithmetic and copies ran while one was open for 22% -> 20% of each run, Pallas kernels for 15% -> 15%
where the time goes in v4:
time: 801 us; the launch traced here: 794 us
  waiting for transfers between devices  309 us (39%)
  Pallas kernels  172 us (21%)
  other arithmetic  108 us (13%)
  starting transfers between devices  78.6 us (10%)
  local copies, waits for them, and re-layouts  60.8 us (8%)
  blocking collectives  26.5 us (3%)
  matrix products  22.7 us (3%)
  between operations  16 us (2%)
    ppermute x51, waiting for transfers between devices, swap(): return lax.ppermute(values, axis, [(i, i ^ bit) for i in range(size)])  89.4 us
    pallas_call x1, Pallas kernels, expert_rows(): pl.pallas_call(expert_kernel, grid_spec=pltpu.PrefetchScalarGridSpec(num_...  49.4 us
    all_gather x1, waiting for transfers between devices, per_device(): ffn_all = lax.all_gather(ffn_in, BLK, axis=0)  47.5 us
    pallas_call x1, Pallas kernels, expert_grads(): pl.pallas_call(grads_kernel, grid=(2, 8), in_specs=[whole_spec(slot_map.s...  43.1 us
    ppermute x3, waiting for transfers between devices, gather_line(): lax.ppermute(above, 'far', down)  42.9 us
    all_to_all x1, waiting for transfers between devices, line_from_heads(): back = lax.all_to_all(back, 'far', split_axis=0, concat_axis=0, tiled=True)  39.1 us
    all_to_all x1, waiting for transfers between devices, line_to_heads(): both = lax.all_to_all(both, 'far', split_axis=0, concat_axis=0, tiled=True)  36.8 us
    ppermute x51, starting transfers between devices, swap(): return lax.ppermute(values, axis, [(i, i ^ bit) for i in range(size)])  30.5 us
  transfers between devices with their start and end apart: 72, of which 31 were waited for; matrix products, arithmetic and copies ran while one was open for 20% of the time, Pallas kernels for 15%

profile of v4, /device:TPU:0, one launch (start us, length us, event | category | flops | bytes accessed | tf_op | source)
XLA Modules:
  0.0 793.6 jit_solution(1832220578195550966)
XLA Ops:
  62.9 15.1 %collective-permute-done.10 = bf16[4,128,768]{2,1,0:T(8,128)(2,1)S(1)} collective-permute-done((bf16[4,128,768]{2,1,0:T(8,128)(2,1)S(1)}, bf16[4,128,768]{2,1,0:T(8,128)(2,1)S(1)}, u32[]{:S(2)}, u32[]{:S(2)}) %collective-permute-start.10) | collective-permute-done | bytes 786464 | tf_op jit(solution)/shard_map/ppermute | solution.py:81
  78.6 13.5 %collective-permute-done.13 = bf16[4,128,768]{2,1,0:T(8,128)(2,1)S(1)} collective-permute-done((bf16[4,128,768]{2,1,0:T(8,128)(2,1)S(1)}, bf16[4,128,768]{2,1,0:T(8,128)(2,1)S(1)}, u32[]{:S(2)}, u32[]{:S(2)}) %collective-permute-start.13) | collective-permute-done | bytes 786464 | tf_op jit(solution)/shard_map/ppermute | solution.py:81
  98.1 14.6 %collective-permute-done.14 = bf16[4,128,768]{2,1,0:T(8,128)(2,1)S(1)} collective-permute-done((bf16[4,128,768]{2,1,0:T(8,128)(2,1)S(1)}, bf16[4,128,768]{2,1,0:T(8,128)(2,1)S(1)}, u32[]{:S(2)}, u32[]{:S(2)}) %collective-permute-start.14) | collective-permute-done | bytes 786464 | tf_op jit(solution)/shard_map/ppermute | solution.py:81
  117.9 14.7 %collective-permute-done.15 = bf16[4,128,768]{2,1,0:T(8,128)(2,1)S(1)} collective-permute-done((bf16[4,128,768]{2,1,0:T(8,128)(2,1)S(1)}, bf16[4,128,768]{2,1,0:T(8,128)(2,1)S(1)}, u32[]{:S(2)}, u32[]{:S(2)}) %collective-permute-start.15) | collective-permute-done | bytes 786464 | tf_op jit(solution)/shard_map/ppermute | solution.py:81
  168.2 36.8 %all-to-all-done.2 = bf16[4,2,3,256,128]{4,3,2,1,0:T(8,128)(2,1)S(1)} async-done(((bf16[4,2,3,256,128]{4,3,2,1,0:T(8,128)(2,1)}), bf16[4,2,3,256,128]{4,3,2,1,0:T(8,128)(2,1)S(1)}, u32[]{:S(2)}, u32[]{:S(2)}) %all-to-all-start.2) | async-done | bytes 1572896 | tf_op jit(solution)/shard_map/all_to_all | solution.py:160
  210.5 20.0 %attention_forward.1 = (f32[8,256,128]{2,1,0:T(8,128)S(1)}, f32[8,1,256]{2,1,0:T(1,128)S(1)}) custom-call(s32[1]{0:T(128)} %bitcast.core_ref, s32[8]{0:T(128)S(1)} %get-tuple-element.218.low_ref, s32[8]{0:T(128)S(1)} %get-tuple-element.216.open_ref, s32[8]{0:T(128)S(1)} %get-tuple-element.215.close_ref, s32[8]{0:T(128)S(1)} %get-tuple-element.217.high_ref, ...), custom_call_target="tpu_custom_call" | custom-call | flops 22000001024 | tf_op jit(solution)/shard_map/attention_forward/pallas_call | solution.py:363
  231.6 26.5 %all_to_all.50 = bf16[8,256,128]{2,1,0:T(8,128)(2,1)S(1)} all-to-all(bf16[8,256,128]{2,1,0:T(8,128)(2,1)S(1)} %convert_element_type.240), channel_id=1, replica_groups=mesh['ulysses'=4,'far'=4,'near'=2] {'far','near'}, dimensions={0} | all-to-all | bytes 1048576 | tf_op jit(solution)/shard_map/all_to_all | solution.py:184
  270.8 12.3 %collective-permute-done.29 = bf16[128,2048]{1,0:T(8,128)(2,1)S(1)} collective-permute-done((bf16[128,2048]{1,0:T(8,128)(2,1)S(1)}, bf16[128,2048]{1,0:T(8,128)(2,1)S(1)}, u32[]{:S(2)}, u32[]{:S(2)}) %collective-permute-start.29) | collective-permute-done | bytes 524320 | tf_op jit(solution)/shard_map/ppermute | solution.py:52
  293.4 14.3 %pad_maximum_fusion.gate_ref.up_ref.gate_tile_ref.up_tile_ref = bf16[4,2,2,2048,256]{4,3,2,1,0:T(8,128)(2,1)} fusion(bf16[1,2,2,2048,256]{4,3,2,1,0:T(8,128)(2,1)} %bitcast.63, bf16[1,2,2,2048,256]{4,3,2,1,0:T(8,128)(2,1)} %bitcast.261, bf16[1,2,2,2048,256]{4,3,2,1,0:T(8,128)(2,1)} %bitcast.61, bf16[1,2,2,2048,256]{4,3,2,1,0:T(8,128)(2,1)} %bitcast.60), kind=kLoop, calls=%fused_computation | loop fusion | flops 25165824 | bytes 33554432 | tf_op jit(solution)/shard_map/stack | solution.py:1060
  307.8 6.2 pad_maximum_fusion.1.down_ref.down_tile_ref
  314.0 47.5 %all-gather.8.cloned.1.call-done = bf16[1024,2048]{1,0:T(8,128)(2,1)} async-done(((bf16[128,2048]{1,0:T(8,128)(2,1)}), bf16[1024,2048]{1,0:T(8,128)(2,1)}) %all-gather.8.cloned.1.call-update) | async-done | bytes 4194320 | tf_op jit(solution)/shard_map/all_gather | solution.py:1059
  361.5 49.4 %expert_rows.1 = (bf16[2,640,2048]{2,1,0:T(8,128)(2,1)}, bf16[2,640,2048]{2,1,0:T(8,128)(2,1)}, f32[2,640,1]{2,1,0:T(8,128)}, bf16[2,640,1024]{2,1,0:T(8,128)(2,...) custom-call(s32[1]{0:T(128)} %bitcast.57.blk_ref, ...), custom_call_target="tpu_custom_call" | custom-call | flops 54999998464 | tf_op jit(solution)/shard_map/expert_rows/pallas_call | solution.py:802
  415.2 12.5 %expert_down_grads.1 = (bf16[2,2,256,2048]{3,2,1,0:T(8,128)(2,1)}, f32[2,2,256,2048]{3,2,1,0:T(8,128)}) custom-call(bf16[2,640,2048]{2,1,0:T(8,128)(2,1)S(1)} %copy-done.14, f32[2,640,1]{2,1,0:T(8,128)S(1)} %copy-done.16, bf16[2,640,1024]{2,1,0:T(8,128)(2,1)S(1)} %copy-done.15), custom_call_target="tpu_custom_call" | custom-call | flops 12000000000 | tf_op jit(solution)/shard_map/expert_down_grads/pallas_call | solution.py:844
  427.7 43.1 %expert_grads.1 = (bf16[2,2,2048,256]{3,2,1,0:T(8,128)(2,1)}, bf16[2,2,2048,256]{3,2,1,0:T(8,128)(2,1)}, f32[2,2,2048,256]{3,2,1,0:T(8,128)}, f32[2,2,2048,256]{...) custom-call(f32[8,2,128]{2,1,0:T(2,128)} %copy-done.45, ...), custom_call_target="tpu_custom_call" | custom-call | flops 38999998464 | tf_op jit(solution)/shard_map/expert_grads/pallas_call | solution.py:862
  474.8 5.7 dynamic_update_slice.116
  483.6 13.8 %reduce-scatter.4.cloned.1.call-done = bf16[1,128,2048]{2,1,0:T(8,128)(2,1)} async-done(((bf16[8,128,2048]{2,1,0:T(8,128)(2,1)}), bf16[1,128,2048]{2,1,0:T(8,128)(2,1)}) %reduce-scatter.4.cloned.1.call-update) | async-done | bytes 524304 | tf_op jit(solution)/shard_map/reduce_scatter | solution.py:1077
  508.3 12.9 %collective-permute-done.39 = f32[17,512]{1,0:T(8,128)S(1)} collective-permute-done((f32[17,512]{1,0:T(8,128)S(1)}, f32[17,512]{1,0:T(8,128)S(1)}, u32[]{:S(2)}, u32[]{:S(2)}) %collective-permute-start.39) | collective-permute-done | bytes 34848 | tf_op jit(solution)/shard_map/ppermute | solution.py:52
  542.5 7.5 all-to-all-done.6.do_ref
  554.5 25.1 %attention_backward.1 = (bf16[8,256,128]{2,1,0:T(8,128)(2,1)}, f32[8,2,256,128]{3,2,1,0:T(8,128)}, bf16[8,2,256,128]{3,2,1,0:T(8,128)(2,1)}) custom-call(s32[1]{0:T(128)} %bitcast.core_ref, s32[8]{0:T(128)} %copy-done.12, s32[8]{0:T(128)} %copy-done.10, s32[8]{0:T(128)} %copy-done.9, s32[8]{0:T(128)} %copy-done.11, s32[8,1,256]{2,1,0:T(1,128)} %copy-done.7, ...), custom_call_target="tpu_custom_call" | custom-call | flops 1000000000 | tf_op jit(solution)/shard_map/attention_backward/pallas_call | solution.py:391
  584.6 14.9 %collective-permute-done.42 = bf16[2,2048,256]{2,1,0:T(8,128)(2,1)} collective-permute-done((bf16[2,2048,256]{2,1,0:T(8,128)(2,1)S(1)}, bf16[2,2048,256]{2,1,0:T(8,128)(2,1)}, u32[]{:S(2)}, u32[]{:S(2)}) %collective-permute-start.42) | collective-permute-done | bytes 2097184 | tf_op jit(solution)/shard_map/ppermute | solution.py:52
  605.9 39.1 %all-to-all-done.7 = bf16[4,2,3,256,128]{4,3,2,1,0:T(8,128)(2,1)S(1)} async-done(((bf16[4,2,3,256,128]{4,3,2,1,0:T(8,128)(2,1)}), bf16[4,2,3,256,128]{4,3,2,1,0:T(8,128)(2,1)S(1)}, u32[]{:S(2)}, u32[]{:S(2)}) %all-to-all-start.7) | async-done | bytes 1572896 | tf_op jit(solution)/shard_map/all_to_all | solution.py:167
  668.0 5.3 rotated_back.1
  673.3 6.3 convolution_convert_fusion
  682.6 5.8 multiply_reduce_fusion
  700.6 6.1 bitcast_add_fusion.2
  711.9 5.8 collective-permute-done.51
  717.7 6.4 collective-permute-done.50
  731.9 6.2 all-to-all-start.9
  739.9 6.2 all-to-all-done.9
  750.4 15.4 %collective-permute-done.53 = bf16[256,2048]{1,0:T(8,128)(2,1)} collective-permute-done((bf16[256,2048]{1,0:T(8,128)(2,1)}, bf16[256,2048]{1,0:T(8,128)(2,1)}, u32[]{:S(2)}, u32[]{:S(2)}) %collective-permute-start.53) | collective-permute-done | bytes 1048608 | tf_op jit(solution)/shard_map/ppermute | solution.py:52
  771.2 6.3 bitcast_add_fusion
  777.5 5.8 all-to-all-done.8.in_ref
  (406 shorter events, 256.6 us)
Async XLA Ops:
  7.2 30.5 %collective-permute-start = (bf16[128,2048]{1,0:T(8,128)(2,1)}, bf16[128,2048]{1,0:T(8,128)(2,1)S(1)}, u32[]{:S(2)}, u32[]{:S(2)}) collective-permute-start(bf16[128,2048]{1,0:T(8,128)(2,1)} %param.17), channel_id=1, source_target_pairs={{0,8},{8,0},{16,24},{24,16},{1,9},{9,1},{17,25},{25,17},{2,10},{10... | collective-permute-start | bytes 1572872 | tf_op jit(solution)/shard_map/ppermute | solution.py:52
  7.7 28.4 %collective-permute-start.1 = (bf16[128,2048]{1,0:T(8,128)(2,1)}, bf16[128,2048]{1,0:T(8,128)(2,1)}, u32[]{:S(2)}, u32[]{:S(2)}) collective-permute-start(bf16[128,2048]{1,0:T(8,128)(2,1)} %param.17), channel_id=1, source_target_pairs={{0,16},{8,24},{16,0},{24,8},{1,17},{9,25},{17,1},{25,9},{2,18},{10... | collective-permute-start | bytes 1572872 | tf_op jit(solution)/shard_map/ppermute | solution.py:52
  10.3 35.8 %collective-permute-start.3 = (bf16[128,2048]{1,0:T(8,128)(2,1)}, bf16[128,2048]{1,0:T(8,128)(2,1)}, u32[]{:S(2)}, u32[]{:S(2)}) collective-permute-start(bf16[128,2048]{1,0:T(8,128)(2,1)} %param.17), channel_id=1, source_target_pairs={{0,1},{1,0},{2,3},{3,2},{4,5},{5,4},{6,7},{7,6},{8,9},{9,8},{10,11... | collective-permute-start | bytes 1572872 | tf_op jit(solution)/shard_map/ppermute | solution.py:52
  14.0 20.0 %collective-permute-start.7 = (bf16[20,64]{1,0:T(8,128)(2,1)S(1)}, bf16[20,64]{1,0:T(8,128)(2,1)S(1)}, u32[]{:S(2)}, u32[]{:S(2)}) collective-permute-start(bf16[20,64]{1,0:T(8,128)(2,1)S(1)} %concatenate.57), channel_id=1, source_target_pairs={{0,8},{8,0},{16,24},{24,16},{1,9},{9,1},{17,25},{25,17},{2,10},{10... | collective-permute-start | bytes 7688 | tf_op jit(solution)/shard_map/ppermute | solution.py:52
  22.7 118.1 %all-gather.6.cloned.1.call-start = ((), (), s32[]{:S(2)}) async-start(), calls=%async_computation.13 | async-start | bytes 2359296 | tf_op jit(solution)/shard_map/all_gather | solution.py:1001
  34.1 106.8 %collective-permute-start.16 = (bf16[2,2,2048,256]{3,2,1,0:T(8,128)(2,1)}, bf16[2,2,2048,256]{3,2,1,0:T(8,128)(2,1)}, u32[]{:S(2)}, u32[]{:S(2)}) collective-permute-start(bf16[2,2,2048,256]{3,2,1,0:T(8,128)(2,1)} %pad_maximum_fusion.2), channel_id=1, source_target_pairs={{0,16},{8,24},{16,0},{24,8},{1,17},{9,25},{17,1},{25,9},{2,18},{10... | collective-permute-start | bytes 12582920 | tf_op jit(solution)/shard_map/ppermute | solution.py:52
  46.1 31.9 %collective-permute-start.10 = (bf16[4,128,768]{2,1,0:T(8,128)(2,1)S(1)}, bf16[4,128,768]{2,1,0:T(8,128)(2,1)S(1)}, u32[]{:S(2)}, u32[]{:S(2)}) collective-permute-start(bf16[4,128,768]{2,1,0:T(8,128)(2,1)S(1)} %bitcast.277), channel_id=1, source_target_pairs={{0,2},{2,4},{4,6},{1,3},{3,5},{5,7},{8,10},{10,12},{12,14},{9,11},... | collective-permute-start | bytes 2359304 | tf_op jit(solution)/shard_map/ppermute | solution.py:81
  53.9 38.2 %collective-permute-start.13 = (bf16[4,128,768]{2,1,0:T(8,128)(2,1)S(1)}, bf16[4,128,768]{2,1,0:T(8,128)(2,1)S(1)}, u32[]{:S(2)}, u32[]{:S(2)}) collective-permute-start(bf16[4,128,768]{2,1,0:T(8,128)(2,1)S(1)} %bitcast.278), channel_id=1, source_target_pairs={{6,4},{4,2},{2,0},{7,5},{5,3},{3,1},{14,12},{12,10},{10,8},{15,13}... | collective-permute-start | bytes 2359304 | tf_op jit(solution)/shard_map/ppermute | solution.py:81
  55.2 38.2 %collective-permute-start.6 = (bf16[128,2048]{1,0:T(8,128)(2,1)}, bf16[128,2048]{1,0:T(8,128)(2,1)S(1)}, u32[]{:S(2)}, u32[]{:S(2)}) collective-permute-start(bf16[128,2048]{1,0:T(8,128)(2,1)} %collective-permute-done.5), channel_id=1, source_target_pairs={{0,8},{8,0},{16,24},{24,16},{1,9},{9,1},{17,25},{25,17},{2,10},{10... | collective-permute-start | bytes 1572872 | tf_op jit(solution)/shard_map/ppermute | solution.py:52
  92.1 20.6 %collective-permute-start.14 = (bf16[4,128,768]{2,1,0:T(8,128)(2,1)S(1)}, bf16[4,128,768]{2,1,0:T(8,128)(2,1)S(1)}, u32[]{:S(2)}, u32[]{:S(2)}) collective-permute-start(bf16[4,128,768]{2,1,0:T(8,128)(2,1)S(1)} %collective-permute-done.13), channel_id=1, source_target_pairs={{4,2},{2,0},{5,3},{3,1},{12,10},{10,8},{13,11},{11,9},{20,18},{18,... | collective-permute-start | bytes 2359304 | tf_op jit(solution)/shard_map/ppermute | solution.py:81
  97.4 20.1 %collective-permute-start.12 = (bf16[4,128,768]{2,1,0:T(8,128)(2,1)S(1)}, bf16[4,128,768]{2,1,0:T(8,128)(2,1)S(1)}, u32[]{:S(2)}, u32[]{:S(2)}) collective-permute-start(bf16[4,128,768]{2,1,0:T(8,128)(2,1)S(1)} %collective-permute-done.11), channel_id=1, source_target_pairs={{4,6},{5,7},{12,14},{13,15},{20,22},{21,23},{28,30},{29,31}} | collective-permute-start | bytes 2359304 | tf_op jit(solution)/shard_map/ppermute | solution.py:81
  112.8 19.8 %collective-permute-start.15 = (bf16[4,128,768]{2,1,0:T(8,128)(2,1)S(1)}, bf16[4,128,768]{2,1,0:T(8,128)(2,1)S(1)}, u32[]{:S(2)}, u32[]{:S(2)}) collective-permute-start(bf16[4,128,768]{2,1,0:T(8,128)(2,1)S(1)} %collective-permute-done.14), channel_id=1, source_target_pairs={{2,0},{3,1},{10,8},{11,9},{18,16},{19,17},{26,24},{27,25}} | collective-permute-start | bytes 2359304 | tf_op jit(solution)/shard_map/ppermute | solution.py:81
  164.0 41.1 %all-to-all-start.2 = ((bf16[4,2,3,256,128]{4,3,2,1,0:T(8,128)(2,1)}), bf16[4,2,3,256,128]{4,3,2,1,0:T(8,128)(2,1)S(1)}, u32[]{:S(2)}, u32[]{:S(2)}) async-start(bf16[4,2,3,256,128]{4,3,2,1,0:T(8,128)(2,1)} %bitcast.273), calls=%async_computation.2 | async-start | bytes 3145728 | tf_op jit(solution)/shard_map/all_to_all | solution.py:160
  167.5 146.4 %all-gather.10.cloned.1.call-start = ((), (), s32[]{:S(2)}) async-start(), calls=%async_computation.18 | async-start | bytes 4718592 | tf_op jit(solution)/shard_map/all_gather | solution.py:1015
  206.4 155.1 %all-gather.8.cloned.1.call-start = ((), (), s32[]{:S(2)}) async-start(), calls=%async_computation.17 | async-start | bytes 4718592 | tf_op jit(solution)/shard_map/all_gather | solution.py:1059
  209.0 51.5 %collective-permute-start.24 = (bf16[2,2,2048,256]{3,2,1,0:T(8,128)(2,1)}, bf16[2,2,2048,256]{3,2,1,0:T(8,128)(2,1)}, u32[]{:S(2)}, u32[]{:S(2)}) collective-permute-start(bf16[2,2,2048,256]{3,2,1,0:T(8,128)(2,1)} %pad_maximum_fusion.2), channel_id=1, source_target_pairs={{0,8},{8,0},{16,24},{24,16},{1,9},{9,1},{17,25},{25,17},{2,10},{10... | collective-permute-start | bytes 12582920 | tf_op jit(solution)/shard_map/ppermute | solution.py:52
  209.1 51.4 %collective-permute-start.25 = (bf16[2,2,2048,256]{3,2,1,0:T(8,128)(2,1)}, bf16[2,2,2048,256]{3,2,1,0:T(8,128)(2,1)}, u32[]{:S(2)}, u32[]{:S(2)}) collective-permute-start(bf16[2,2,2048,256]{3,2,1,0:T(8,128)(2,1)} %collective-permute-done.16), channel_id=1, source_target_pairs={{0,8},{8,0},{16,24},{24,16},{1,9},{9,1},{17,25},{25,17},{2,10},{10... | collective-permute-start | bytes 12582920 | tf_op jit(solution)/shard_map/ppermute | solution.py:52
  209.9 50.6 %collective-permute-start.23 = (bf16[2,256,2048]{2,1,0:T(8,128)(2,1)}, bf16[2,256,2048]{2,1,0:T(8,128)(2,1)}, u32[]{:S(2)}, u32[]{:S(2)}) collective-permute-start(bf16[2,256,2048]{2,1,0:T(8,128)(2,1)} %convert_element_type.235), channel_id=1, source_target_pairs={{0,16},{8,24},{16,0},{24,8},{1,17},{9,25},{17,1},{25,9},{2,18},{10... | collective-permute-start | bytes 6291464 | tf_op jit(solution)/shard_map/ppermute | solution.py:52
  210.5 50.0 %collective-permute-start.26 = (bf16[2,256,2048]{2,1,0:T(8,128)(2,1)}, bf16[2,256,2048]{2,1,0:T(8,128)(2,1)}, u32[]{:S(2)}, u32[]{:S(2)}) collective-permute-start(bf16[2,256,2048]{2,1,0:T(8,128)(2,1)} %convert_element_type.235), channel_id=1, source_target_pairs={{0,8},{8,0},{16,24},{24,16},{1,9},{9,1},{17,25},{25,17},{2,10},{10... | collective-permute-start | bytes 6291464 | tf_op jit(solution)/shard_map/ppermute | solution.py:52
  288.1 25.9 %all-to-all-start.4 = ((f32[8,2,128]{2,1,0:T(2,128)}), f32[8,2,128]{2,1,0:T(2,128)S(1)}, u32[]{:S(2)}, u32[]{:S(2)}) async-start(f32[8,2,128]{2,1,0:T(2,128)} %bitcast.52), calls=%async_computation.4 | async-start | bytes 16384 | tf_op jit(solution)/shard_map/all_to_all | solution.py:1014
  293.3 204.2 %reduce-scatter.4.cloned.1.call-start = ((), (), s32[]{:S(2)}) async-start(), calls=%async_computation.14 | async-start | bytes 4718592 | tf_op jit(solution)/shard_map/reduce_scatter | solution.py:1077
  427.7 43.1 %collective-permute-start.31 = (bf16[2,2,256,2048]{3,2,1,0:T(8,128)(2,1)}, bf16[2,2,256,2048]{3,2,1,0:T(8,128)(2,1)}, u32[]{:S(2)}, u32[]{:S(2)}) collective-permute-start(bf16[2,2,256,2048]{3,2,1,0:T(8,128)(2,1)} %get-tuple-element.157), channel_id=1, source_target_pairs={{0,8},{8,0},{16,24},{24,16},{1,9},{9,1},{17,25},{25,17},{2,10},{10... | collective-permute-start | bytes 12582920 | tf_op jit(solution)/shard_map/ppermute | solution.py:52
  470.8 27.8 %collective-permute-start.33 = (bf16[2,2,2048,256]{3,2,1,0:T(8,128)(2,1)}, bf16[2,2,2048,256]{3,2,1,0:T(8,128)(2,1)}, u32[]{:S(2)}, u32[]{:S(2)}) collective-permute-start(bf16[2,2,2048,256]{3,2,1,0:T(8,128)(2,1)} %get-tuple-element.160), channel_id=1, source_target_pairs={{0,8},{8,0},{16,24},{24,16},{1,9},{9,1},{17,25},{25,17},{2,10},{10... | collective-permute-start | bytes 12582920 | tf_op jit(solution)/shard_map/ppermute | solution.py:52
  471.4 32.0 %collective-permute-start.32 = (bf16[2,2,2048,256]{3,2,1,0:T(8,128)(2,1)}, bf16[2,2,2048,256]{3,2,1,0:T(8,128)(2,1)}, u32[]{:S(2)}, u32[]{:S(2)}) collective-permute-start(bf16[2,2,2048,256]{3,2,1,0:T(8,128)(2,1)} %get-tuple-element.158), channel_id=1, source_target_pairs={{0,8},{8,0},{16,24},{24,16},{1,9},{9,1},{17,25},{25,17},{2,10},{10... | collective-permute-start | bytes 12582920 | tf_op jit(solution)/shard_map/ppermute | solution.py:52
  535.1 146.5 %reduce-scatter.6.cloned.1.call-start = ((), (), s32[]{:S(2)}) async-start(), calls=%async_computation.15 | async-start | bytes 7077888 | tf_op jit(solution)/shard_map/reduce_scatter | solution.py:1125
  553.1 46.4 %collective-permute-start.42 = (bf16[2,2048,256]{2,1,0:T(8,128)(2,1)S(1)}, bf16[2,2048,256]{2,1,0:T(8,128)(2,1)}, u32[]{:S(2)}, u32[]{:S(2)}) collective-permute-start(bf16[2,2048,256]{2,1,0:T(8,128)(2,1)S(1)} %copy-done.32), channel_id=1, source_target_pairs={{0,16},{8,24},{16,0},{24,8},{1,17},{9,25},{17,1},{25,9},{2,18},{10... | collective-permute-start | bytes 6291464 | tf_op jit(solution)/shard_map/ppermute | solution.py:52
  600.7 44.3 %all-to-all-start.7 = ((bf16[4,2,3,256,128]{4,3,2,1,0:T(8,128)(2,1)}), bf16[4,2,3,256,128]{4,3,2,1,0:T(8,128)(2,1)S(1)}, u32[]{:S(2)}, u32[]{:S(2)}) async-start(bf16[4,2,3,256,128]{4,3,2,1,0:T(8,128)(2,1)} %pad_maximum_fusion.3), calls=%async_computation.8 | async-start | bytes 3145728 | tf_op jit(solution)/shard_map/all_to_all | solution.py:167
  604.3 163.0 %reduce-scatter.8.cloned.1.call-start = ((), (), s32[]{:S(2)}) async-start(), calls=%async_computation.16 | async-start | bytes 3932160 | tf_op jit(solution)/shard_map/reduce_scatter | solution.py:1151
  604.4 46.4 %collective-permute-start.44 = (bf16[2,2048,256]{2,1,0:T(8,128)(2,1)}, bf16[2,2048,256]{2,1,0:T(8,128)(2,1)}, u32[]{:S(2)}, u32[]{:S(2)}) collective-permute-start(bf16[2,2048,256]{2,1,0:T(8,128)(2,1)} %fusion.1), channel_id=1, source_target_pairs={{0,16},{8,24},{16,0},{24,8},{1,17},{9,25},{17,1},{25,9},{2,18},{10... | collective-permute-start | bytes 6291464 | tf_op jit(solution)/shard_map/ppermute | solution.py:52
  691.9 25.8 %collective-permute-start.51 = (bf16[256,2048]{1,0:T(8,128)(2,1)}, bf16[256,2048]{1,0:T(8,128)(2,1)S(1)}, u32[]{:S(2)}, u32[]{:S(2)}) collective-permute-start(bf16[256,2048]{1,0:T(8,128)(2,1)} %get-tuple-element.188), channel_id=1, source_target_pairs={{0,16},{8,24},{16,0},{24,8},{1,17},{9,25},{17,1},{25,9},{2,18},{10... | collective-permute-start | bytes 3145736 | tf_op jit(solution)/shard_map/ppermute | solution.py:52
  698.5 25.6 %collective-permute-start.50 = (bf16[2,128,2048]{2,1,0:T(8,128)(2,1)S(1)}, bf16[2,128,2048]{2,1,0:T(8,128)(2,1)S(1)}, u32[]{:S(2)}, u32[]{:S(2)}) collective-permute-start(bf16[2,128,2048]{2,1,0:T(8,128)(2,1)S(1)} %pad_maximum_fusion.6), channel_id=1, source_target_pairs={{0,1},{1,0},{2,3},{3,2},{4,5},{5,4},{6,7},{7,6},{8,9},{9,8},{10,11... | collective-permute-start | bytes 3145736 | tf_op jit(solution)/shard_map/ppermute | solution.py:52
  730.4 35.4 %collective-permute-start.53 = (bf16[256,2048]{1,0:T(8,128)(2,1)}, bf16[256,2048]{1,0:T(8,128)(2,1)}, u32[]{:S(2)}, u32[]{:S(2)}) collective-permute-start(bf16[256,2048]{1,0:T(8,128)(2,1)} %get-tuple-element.191), channel_id=1, source_target_pairs={{0,16},{8,24},{16,0},{24,8},{1,17},{9,25},{17,1},{25,9},{2,18},{10... | collective-permute-start | bytes 3145736 | tf_op jit(solution)/shard_map/ppermute | solution.py:52
  (93 other events, 1000.8 us)
Sparse Core Ops, SparseCore 0:
  26.2 61.9 all-gather.5
  206.5 73.8 all-gather.9
  287.3 74.0 all-gather.7
  411.0 86.4 reduce-scatter.3
  551.6 123.9 reduce-scatter.5
  692.7 62.5 reduce-scatter.7

commit v5 on v4

--- a/solution.py
+++ b/solution.py
@@ -1091,7 +1091,9 @@
     summed = lax.dynamic_update_slice(
         jnp.zeros((blk_size, weight_rows + own_tokens, width), bfloat), mixed_part, (0, weight_rows, 0)
     )
-    d_ffn_in, summed, up_got, gate_sent = tie(d_ffn_in, summed, up_got, gate_sent)
+    d_ffn_in, summed, up_got, gate_sent, second_down = tie(
+        d_ffn_in, summed, up_got, gate_sent, swap(down_sent[1], 2)
+    )
 
     router_probs = lax.dynamic_index_in_dim(probs_all, blk, 0, keepdims=False)
     d_logits = (
@@ -1171,10 +1173,9 @@
     grad_w_up = whole_sum(up_kept, up_got, up_across)
     d_normed, beside = scatter_sum_plane(
         near_rows,
-        (grad_w_gate, grad_w_up, grad_attn_part, summed, first_down, down_sent[1]),
-    )
-    grad_w_gate, grad_w_up, grad_attn_part, summed, first_down, second_down = beside
-    d_normed, second_down = tie(d_normed, swap(second_down, 2))
+        (grad_w_gate, grad_w_up, grad_attn_part, summed, first_down),
+    )
+    grad_w_gate, grad_w_up, grad_attn_part, summed, first_down = beside
     down_across = jnp.stack([first_down, second_down])
     grad_w_out = summed[:weight_rows].astype(single)
     mixed = (residual_mid + summed[weight_rows:].astype(single)).astype(bfloat)
@@ -1191,7 +1192,8 @@
         jnp.zeros((2, local_width), single), gain_parts, side * plane_width, 1
     )
     last = own_columns(grad_attn_part[None])
-    gains = scatter_sum_blk_small(jnp.concatenate([last, narrow, gain_parts]))
+    grads, gains = tie(grads, jnp.concatenate([last, narrow, gain_parts]))
+    gains = scatter_sum_blk_small(gains)
     grads = grads.reshape(plane_size, weight_rows, 3 * plane_width)
     grads = lax.all_to_all(grads, PLANE, split_axis=0, concat_axis=0, tiled=True)
     grads = unpacked(grads)

time: 801 us -> 809 us (level)
  waiting for transfers between devices: 309 us -> 321 us
    ppermute x51, waiting for transfers between devices: 89.4 us -> 97.9 us  [swap(): return lax.ppermute(values, axis, [(i, i ^ bit) for i in range(size)])]
    unnamed x113 -> x115, local copies, waits for them, and re-layouts: 17.8 us -> 18.1 us
  transfers between devices with their start and end apart: 72 -> 72, of which waited for: 31 -> 35; matrix products, arithmetic and copies ran while one was open for 20% -> 19% of each run, Pallas kernels for 15% -> 14%
where the time goes in v5:
time: 809 us; the launch traced here: 801 us
  waiting for transfers between devices  321 us (40%)
  Pallas kernels  172 us (21%)
  other arithmetic  102 us (13%)
  starting transfers between devices  80.5 us (10%)
  local copies, waits for them, and re-layouts  60.6 us (7%)
  blocking collectives  26.3 us (3%)
  matrix products  22.7 us (3%)
  between operations  15.9 us (2%)
    ppermute x51, waiting for transfers between devices, swap(): return lax.ppermute(values, axis, [(i, i ^ bit) for i in range(size)])  97.9 us
    pallas_call x1, Pallas kernels, expert_rows(): pl.pallas_call(expert_kernel, grid_spec=pltpu.PrefetchScalarGridSpec(num_...  49.4 us
    all_gather x1, waiting for transfers between devices, per_device(): ffn_all = lax.all_gather(ffn_in, BLK, axis=0)  47.5 us
    pallas_call x1, Pallas kernels, expert_grads(): pl.pallas_call(grads_kernel, grid=(2, 8), in_specs=[whole_spec(slot_map.s...  43.3 us
    ppermute x3, waiting for transfers between devices, gather_line(): lax.ppermute(above, 'far', down)  42.6 us
    all_to_all x1, waiting for transfers between devices, line_from_heads(): back = lax.all_to_all(back, 'far', split_axis=0, concat_axis=0, tiled=True)  39.2 us
    all_to_all x1, waiting for transfers between devices, line_to_heads(): both = lax.all_to_all(both, 'far', split_axis=0, concat_axis=0, tiled=True)  36.8 us
    ppermute x51, starting transfers between devices, swap(): return lax.ppermute(values, axis, [(i, i ^ bit) for i in range(size)])  32.8 us
  transfers between devices with their start and end apart: 72, of which 35 were waited for; matrix products, arithmetic and copies ran while one was open for 19% of the time, Pallas kernels for 14%

profile of v5, /device:TPU:0, one launch (start us, length us, event | category | flops | bytes accessed | tf_op | source)
XLA Modules:
  0.0 801.3 jit_solution(15217687119645004780)
XLA Ops:
  62.9 15.1 %collective-permute-done.10 = bf16[4,128,768]{2,1,0:T(8,128)(2,1)S(1)} collective-permute-done((bf16[4,128,768]{2,1,0:T(8,128)(2,1)S(1)}, bf16[4,128,768]{2,1,0:T(8,128)(2,1)S(1)}, u32[]{:S(2)}, u32[]{:S(2)}) %collective-permute-start.10) | collective-permute-done | bytes 786464 | tf_op jit(solution)/shard_map/ppermute | solution.py:81
  78.6 13.5 %collective-permute-done.13 = bf16[4,128,768]{2,1,0:T(8,128)(2,1)S(1)} collective-permute-done((bf16[4,128,768]{2,1,0:T(8,128)(2,1)S(1)}, bf16[4,128,768]{2,1,0:T(8,128)(2,1)S(1)}, u32[]{:S(2)}, u32[]{:S(2)}) %collective-permute-start.13) | collective-permute-done | bytes 786464 | tf_op jit(solution)/shard_map/ppermute | solution.py:81
  98.1 14.6 %collective-permute-done.14 = bf16[4,128,768]{2,1,0:T(8,128)(2,1)S(1)} collective-permute-done((bf16[4,128,768]{2,1,0:T(8,128)(2,1)S(1)}, bf16[4,128,768]{2,1,0:T(8,128)(2,1)S(1)}, u32[]{:S(2)}, u32[]{:S(2)}) %collective-permute-start.14) | collective-permute-done | bytes 786464 | tf_op jit(solution)/shard_map/ppermute | solution.py:81
  118.1 14.4 %collective-permute-done.15 = bf16[4,128,768]{2,1,0:T(8,128)(2,1)S(1)} collective-permute-done((bf16[4,128,768]{2,1,0:T(8,128)(2,1)S(1)}, bf16[4,128,768]{2,1,0:T(8,128)(2,1)S(1)}, u32[]{:S(2)}, u32[]{:S(2)}) %collective-permute-start.15) | collective-permute-done | bytes 786464 | tf_op jit(solution)/shard_map/ppermute | solution.py:81
  168.2 36.8 %all-to-all-done.2 = bf16[4,2,3,256,128]{4,3,2,1,0:T(8,128)(2,1)S(1)} async-done(((bf16[4,2,3,256,128]{4,3,2,1,0:T(8,128)(2,1)}), bf16[4,2,3,256,128]{4,3,2,1,0:T(8,128)(2,1)S(1)}, u32[]{:S(2)}, u32[]{:S(2)}) %all-to-all-start.2) | async-done | bytes 1572896 | tf_op jit(solution)/shard_map/all_to_all | solution.py:160
  210.5 20.0 %attention_forward.1 = (f32[8,256,128]{2,1,0:T(8,128)S(1)}, f32[8,1,256]{2,1,0:T(1,128)S(1)}) custom-call(s32[1]{0:T(128)} %bitcast.core_ref, s32[8]{0:T(128)S(1)} %get-tuple-element.220.low_ref, s32[8]{0:T(128)S(1)} %get-tuple-element.218.open_ref, s32[8]{0:T(128)S(1)} %get-tuple-element.217.close_ref, s32[8]{0:T(128)S(1)} %get-tuple-element.219.high_ref, ...), custom_call_target="tpu_custom_call" | custom-call | flops 22000001024 | tf_op jit(solution)/shard_map/attention_forward/pallas_call | solution.py:363
  231.6 26.3 %all_to_all.50 = bf16[8,256,128]{2,1,0:T(8,128)(2,1)S(1)} all-to-all(bf16[8,256,128]{2,1,0:T(8,128)(2,1)S(1)} %convert_element_type.240), channel_id=1, replica_groups=mesh['ulysses'=4,'far'=4,'near'=2] {'far','near'}, dimensions={0} | all-to-all | bytes 1048576 | tf_op jit(solution)/shard_map/all_to_all | solution.py:184
  270.5 12.4 %collective-permute-done.29 = bf16[128,2048]{1,0:T(8,128)(2,1)S(1)} collective-permute-done((bf16[128,2048]{1,0:T(8,128)(2,1)S(1)}, bf16[128,2048]{1,0:T(8,128)(2,1)S(1)}, u32[]{:S(2)}, u32[]{:S(2)}) %collective-permute-start.29) | collective-permute-done | bytes 524320 | tf_op jit(solution)/shard_map/ppermute | solution.py:52
  293.1 14.3 %pad_maximum_fusion.gate_ref.up_ref.gate_tile_ref.up_tile_ref = bf16[4,2,2,2048,256]{4,3,2,1,0:T(8,128)(2,1)} fusion(bf16[1,2,2,2048,256]{4,3,2,1,0:T(8,128)(2,1)} %bitcast.63, bf16[1,2,2,2048,256]{4,3,2,1,0:T(8,128)(2,1)} %bitcast.264, bf16[1,2,2,2048,256]{4,3,2,1,0:T(8,128)(2,1)} %bitcast.61, bf16[1,2,2,2048,256]{4,3,2,1,0:T(8,128)(2,1)} %bitcast.60), kind=kLoop, calls=%fused_computation | loop fusion | flops 25165824 | bytes 33554432 | tf_op jit(solution)/shard_map/stack | solution.py:1060
  307.4 6.2 pad_maximum_fusion.1.down_ref.down_tile_ref
  313.6 47.5 %all-gather.8.cloned.1.call-done = bf16[1024,2048]{1,0:T(8,128)(2,1)} async-done(((bf16[128,2048]{1,0:T(8,128)(2,1)}), bf16[1024,2048]{1,0:T(8,128)(2,1)}) %all-gather.8.cloned.1.call-update) | async-done | bytes 4194320 | tf_op jit(solution)/shard_map/all_gather | solution.py:1059
  361.1 49.4 %expert_rows.1 = (bf16[2,640,2048]{2,1,0:T(8,128)(2,1)}, bf16[2,640,2048]{2,1,0:T(8,128)(2,1)}, f32[2,640,1]{2,1,0:T(8,128)}, bf16[2,640,1024]{2,1,0:T(8,128)(2,...) custom-call(s32[1]{0:T(128)} %bitcast.57.blk_ref, ...), custom_call_target="tpu_custom_call" | custom-call | flops 54999998464 | tf_op jit(solution)/shard_map/expert_rows/pallas_call | solution.py:802
  414.8 12.5 %expert_down_grads.1 = (bf16[2,2,256,2048]{3,2,1,0:T(8,128)(2,1)}, f32[2,2,256,2048]{3,2,1,0:T(8,128)}) custom-call(bf16[2,640,2048]{2,1,0:T(8,128)(2,1)S(1)} %copy-done.14, f32[2,640,1]{2,1,0:T(8,128)S(1)} %copy-done.16, bf16[2,640,1024]{2,1,0:T(8,128)(2,1)S(1)} %copy-done.15), custom_call_target="tpu_custom_call" | custom-call | flops 12000000000 | tf_op jit(solution)/shard_map/expert_down_grads/pallas_call | solution.py:844
  427.3 43.3 %expert_grads.1 = (bf16[2,2,2048,256]{3,2,1,0:T(8,128)(2,1)}, bf16[2,2,2048,256]{3,2,1,0:T(8,128)(2,1)}, f32[2,2,2048,256]{3,2,1,0:T(8,128)}, f32[2,2,2048,256]{...) custom-call(f32[8,2,128]{2,1,0:T(2,128)} %copy-done.44, ...), custom_call_target="tpu_custom_call" | custom-call | flops 38999998464 | tf_op jit(solution)/shard_map/expert_grads/pallas_call | solution.py:862
  474.6 5.7 dynamic_update_slice.116
  489.7 7.4 reduce-scatter.4.cloned.1.call-done
  503.0 9.9 %collective-permute-done.34 = bf16[256,2048]{1,0:T(8,128)(2,1)S(1)} collective-permute-done((bf16[256,2048]{1,0:T(8,128)(2,1)S(1)}, bf16[256,2048]{1,0:T(8,128)(2,1)S(1)}, u32[]{:S(2)}, u32[]{:S(2)}) %collective-permute-start.34) | collective-permute-done | bytes 1048608 | tf_op jit(solution)/shard_map/ppermute | solution.py:52
  518.1 12.6 %collective-permute-done.40 = f32[17,512]{1,0:T(8,128)S(1)} collective-permute-done((f32[17,512]{1,0:T(8,128)S(1)}, f32[17,512]{1,0:T(8,128)S(1)}, u32[]{:S(2)}, u32[]{:S(2)}) %collective-permute-start.40) | collective-permute-done | bytes 34848 | tf_op jit(solution)/shard_map/ppermute | solution.py:52
  540.3 5.6 all-to-all-start.6
  553.5 7.3 all-to-all-done.6.do_ref
  565.3 25.1 %attention_backward.1 = (bf16[8,256,128]{2,1,0:T(8,128)(2,1)}, f32[8,2,256,128]{3,2,1,0:T(8,128)}, bf16[8,2,256,128]{3,2,1,0:T(8,128)(2,1)}) custom-call(s32[1]{0:T(128)} %bitcast.core_ref, s32[8]{0:T(128)} %copy-done.12, s32[8]{0:T(128)} %copy-done.10, s32[8]{0:T(128)} %copy-done.9, s32[8]{0:T(128)} %copy-done.11, s32[8,1,256]{2,1,0:T(1,128)} %copy-done.7, ...), custom_call_target="tpu_custom_call" | custom-call | flops 1000000000 | tf_op jit(solution)/shard_map/attention_backward/pallas_call | solution.py:391
  595.4 14.8 %collective-permute-done.43 = bf16[2,2048,256]{2,1,0:T(8,128)(2,1)} collective-permute-done((bf16[2,2048,256]{2,1,0:T(8,128)(2,1)S(1)}, bf16[2,2048,256]{2,1,0:T(8,128)(2,1)}, u32[]{:S(2)}, u32[]{:S(2)}) %collective-permute-start.43) | collective-permute-done | bytes 2097184 | tf_op jit(solution)/shard_map/ppermute | solution.py:52
  616.6 39.2 %all-to-all-done.7 = bf16[4,2,3,256,128]{4,3,2,1,0:T(8,128)(2,1)S(1)} async-done(((bf16[4,2,3,256,128]{4,3,2,1,0:T(8,128)(2,1)}), bf16[4,2,3,256,128]{4,3,2,1,0:T(8,128)(2,1)S(1)}, u32[]{:S(2)}, u32[]{:S(2)}) %all-to-all-start.7) | async-done | bytes 1572896 | tf_op jit(solution)/shard_map/all_to_all | solution.py:167
  677.0 5.3 rotated_back.1
  682.3 6.2 convolution_convert_fusion
  691.6 5.8 multiply_reduce_fusion
  708.3 6.5 bitcast_add_fusion.2
  720.1 6.7 collective-permute-done.52
  742.4 11.2 %collective-permute-done.56 = f32[1,512]{1,0:T(1,128)S(1)} collective-permute-done((f32[1,512]{1,0:T(1,128)S(1)}, f32[1,512]{1,0:T(1,128)S(1)}, u32[]{:S(2)}, u32[]{:S(2)}) %collective-permute-start.56) | collective-permute-done | bytes 2080 | tf_op jit(solution)/shard_map/ppermute | solution.py:52
  755.5 7.8 reduce-scatter.8.cloned.1.call-done
  768.7 6.7 all-to-all-done.9
  782.6 8.4 %all-to-all-done.8.in_ref = bf16[8,64,768]{2,1,0:T(8,128)(2,1)S(1)} async-done(((bf16[8,64,768]{2,1,0:T(8,128)(2,1)}), bf16[8,64,768]{2,1,0:T(8,128)(2,1)S(1)}, u32[]{:S(2)}, u32[]{:S(2)}) %all-to-all-start.8) | async-done | bytes 786464 | tf_op jit(solution)/shard_map/all_to_all | solution.py:1198
  (408 shorter events, 266.9 us)
Async XLA Ops:
  7.2 30.5 %collective-permute-start = (bf16[128,2048]{1,0:T(8,128)(2,1)}, bf16[128,2048]{1,0:T(8,128)(2,1)S(1)}, u32[]{:S(2)}, u32[]{:S(2)}) collective-permute-start(bf16[128,2048]{1,0:T(8,128)(2,1)} %param.17), channel_id=1, source_target_pairs={{0,8},{8,0},{16,24},{24,16},{1,9},{9,1},{17,25},{25,17},{2,10},{10... | collective-permute-start | bytes 1572872 | tf_op jit(solution)/shard_map/ppermute | solution.py:52
  7.7 28.4 %collective-permute-start.1 = (bf16[128,2048]{1,0:T(8,128)(2,1)}, bf16[128,2048]{1,0:T(8,128)(2,1)}, u32[]{:S(2)}, u32[]{:S(2)}) collective-permute-start(bf16[128,2048]{1,0:T(8,128)(2,1)} %param.17), channel_id=1, source_target_pairs={{0,16},{8,24},{16,0},{24,8},{1,17},{9,25},{17,1},{25,9},{2,18},{10... | collective-permute-start | bytes 1572872 | tf_op jit(solution)/shard_map/ppermute | solution.py:52
  10.3 35.8 %collective-permute-start.3 = (bf16[128,2048]{1,0:T(8,128)(2,1)}, bf16[128,2048]{1,0:T(8,128)(2,1)}, u32[]{:S(2)}, u32[]{:S(2)}) collective-permute-start(bf16[128,2048]{1,0:T(8,128)(2,1)} %param.17), channel_id=1, source_target_pairs={{0,1},{1,0},{2,3},{3,2},{4,5},{5,4},{6,7},{7,6},{8,9},{9,8},{10,11... | collective-permute-start | bytes 1572872 | tf_op jit(solution)/shard_map/ppermute | solution.py:52
  14.0 20.0 %collective-permute-start.7 = (bf16[20,64]{1,0:T(8,128)(2,1)S(1)}, bf16[20,64]{1,0:T(8,128)(2,1)S(1)}, u32[]{:S(2)}, u32[]{:S(2)}) collective-permute-start(bf16[20,64]{1,0:T(8,128)(2,1)S(1)} %concatenate.57), channel_id=1, source_target_pairs={{0,8},{8,0},{16,24},{24,16},{1,9},{9,1},{17,25},{25,17},{2,10},{10... | collective-permute-start | bytes 7688 | tf_op jit(solution)/shard_map/ppermute | solution.py:52
  22.7 118.1 %all-gather.6.cloned.1.call-start = ((), (), s32[]{:S(2)}) async-start(), calls=%async_computation.13 | async-start | bytes 2359296 | tf_op jit(solution)/shard_map/all_gather | solution.py:1001
  34.1 106.8 %collective-permute-start.16 = (bf16[2,2,2048,256]{3,2,1,0:T(8,128)(2,1)}, bf16[2,2,2048,256]{3,2,1,0:T(8,128)(2,1)}, u32[]{:S(2)}, u32[]{:S(2)}) collective-permute-start(bf16[2,2,2048,256]{3,2,1,0:T(8,128)(2,1)} %pad_maximum_fusion.2), channel_id=1, source_target_pairs={{0,16},{8,24},{16,0},{24,8},{1,17},{9,25},{17,1},{25,9},{2,18},{10... | collective-permute-start | bytes 12582920 | tf_op jit(solution)/shard_map/ppermute | solution.py:52
  46.1 31.9 %collective-permute-start.10 = (bf16[4,128,768]{2,1,0:T(8,128)(2,1)S(1)}, bf16[4,128,768]{2,1,0:T(8,128)(2,1)S(1)}, u32[]{:S(2)}, u32[]{:S(2)}) collective-permute-start(bf16[4,128,768]{2,1,0:T(8,128)(2,1)S(1)} %bitcast.282), channel_id=1, source_target_pairs={{0,2},{2,4},{4,6},{1,3},{3,5},{5,7},{8,10},{10,12},{12,14},{9,11},... | collective-permute-start | bytes 2359304 | tf_op jit(solution)/shard_map/ppermute | solution.py:81
  53.9 38.2 %collective-permute-start.13 = (bf16[4,128,768]{2,1,0:T(8,128)(2,1)S(1)}, bf16[4,128,768]{2,1,0:T(8,128)(2,1)S(1)}, u32[]{:S(2)}, u32[]{:S(2)}) collective-permute-start(bf16[4,128,768]{2,1,0:T(8,128)(2,1)S(1)} %bitcast.283), channel_id=1, source_target_pairs={{6,4},{4,2},{2,0},{7,5},{5,3},{3,1},{14,12},{12,10},{10,8},{15,13}... | collective-permute-start | bytes 2359304 | tf_op jit(solution)/shard_map/ppermute | solution.py:81
  55.2 38.2 %collective-permute-start.6 = (bf16[128,2048]{1,0:T(8,128)(2,1)}, bf16[128,2048]{1,0:T(8,128)(2,1)S(1)}, u32[]{:S(2)}, u32[]{:S(2)}) collective-permute-start(bf16[128,2048]{1,0:T(8,128)(2,1)} %collective-permute-done.5), channel_id=1, source_target_pairs={{0,8},{8,0},{16,24},{24,16},{1,9},{9,1},{17,25},{25,17},{2,10},{10... | collective-permute-start | bytes 1572872 | tf_op jit(solution)/shard_map/ppermute | solution.py:52
  92.1 20.6 %collective-permute-start.14 = (bf16[4,128,768]{2,1,0:T(8,128)(2,1)S(1)}, bf16[4,128,768]{2,1,0:T(8,128)(2,1)S(1)}, u32[]{:S(2)}, u32[]{:S(2)}) collective-permute-start(bf16[4,128,768]{2,1,0:T(8,128)(2,1)S(1)} %collective-permute-done.13), channel_id=1, source_target_pairs={{4,2},{2,0},{5,3},{3,1},{12,10},{10,8},{13,11},{11,9},{20,18},{18,... | collective-permute-start | bytes 2359304 | tf_op jit(solution)/shard_map/ppermute | solution.py:81
  97.4 20.4 %collective-permute-start.12 = (bf16[4,128,768]{2,1,0:T(8,128)(2,1)S(1)}, bf16[4,128,768]{2,1,0:T(8,128)(2,1)S(1)}, u32[]{:S(2)}, u32[]{:S(2)}) collective-permute-start(bf16[4,128,768]{2,1,0:T(8,128)(2,1)S(1)} %collective-permute-done.11), channel_id=1, source_target_pairs={{4,6},{5,7},{12,14},{13,15},{20,22},{21,23},{28,30},{29,31}} | collective-permute-start | bytes 2359304 | tf_op jit(solution)/shard_map/ppermute | solution.py:81
  163.9 41.1 %all-to-all-start.2 = ((bf16[4,2,3,256,128]{4,3,2,1,0:T(8,128)(2,1)}), bf16[4,2,3,256,128]{4,3,2,1,0:T(8,128)(2,1)S(1)}, u32[]{:S(2)}, u32[]{:S(2)}) async-start(bf16[4,2,3,256,128]{4,3,2,1,0:T(8,128)(2,1)} %bitcast.278), calls=%async_computation.2 | async-start | bytes 3145728 | tf_op jit(solution)/shard_map/all_to_all | solution.py:160
  167.5 146.0 %all-gather.10.cloned.1.call-start = ((), (), s32[]{:S(2)}) async-start(), calls=%async_computation.18 | async-start | bytes 4718592 | tf_op jit(solution)/shard_map/all_gather | solution.py:1015
  206.3 154.7 %all-gather.8.cloned.1.call-start = ((), (), s32[]{:S(2)}) async-start(), calls=%async_computation.17 | async-start | bytes 4718592 | tf_op jit(solution)/shard_map/all_gather | solution.py:1059
  209.0 51.3 %collective-permute-start.24 = (bf16[2,2,2048,256]{3,2,1,0:T(8,128)(2,1)}, bf16[2,2,2048,256]{3,2,1,0:T(8,128)(2,1)}, u32[]{:S(2)}, u32[]{:S(2)}) collective-permute-start(bf16[2,2,2048,256]{3,2,1,0:T(8,128)(2,1)} %pad_maximum_fusion.2), channel_id=1, source_target_pairs={{0,8},{8,0},{16,24},{24,16},{1,9},{9,1},{17,25},{25,17},{2,10},{10... | collective-permute-start | bytes 12582920 | tf_op jit(solution)/shard_map/ppermute | solution.py:52
  209.1 51.2 %collective-permute-start.25 = (bf16[2,2,2048,256]{3,2,1,0:T(8,128)(2,1)}, bf16[2,2,2048,256]{3,2,1,0:T(8,128)(2,1)}, u32[]{:S(2)}, u32[]{:S(2)}) collective-permute-start(bf16[2,2,2048,256]{3,2,1,0:T(8,128)(2,1)} %collective-permute-done.16), channel_id=1, source_target_pairs={{0,8},{8,0},{16,24},{24,16},{1,9},{9,1},{17,25},{25,17},{2,10},{10... | collective-permute-start | bytes 12582920 | tf_op jit(solution)/shard_map/ppermute | solution.py:52
  209.9 50.3 %collective-permute-start.23 = (bf16[2,256,2048]{2,1,0:T(8,128)(2,1)}, bf16[2,256,2048]{2,1,0:T(8,128)(2,1)}, u32[]{:S(2)}, u32[]{:S(2)}) collective-permute-start(bf16[2,256,2048]{2,1,0:T(8,128)(2,1)} %convert_element_type.235), channel_id=1, source_target_pairs={{0,16},{8,24},{16,0},{24,8},{1,17},{9,25},{17,1},{25,9},{2,18},{10... | collective-permute-start | bytes 6291464 | tf_op jit(solution)/shard_map/ppermute | solution.py:52
  210.5 49.8 %collective-permute-start.26 = (bf16[2,256,2048]{2,1,0:T(8,128)(2,1)}, bf16[2,256,2048]{2,1,0:T(8,128)(2,1)}, u32[]{:S(2)}, u32[]{:S(2)}) collective-permute-start(bf16[2,256,2048]{2,1,0:T(8,128)(2,1)} %convert_element_type.235), channel_id=1, source_target_pairs={{0,8},{8,0},{16,24},{24,16},{1,9},{9,1},{17,25},{25,17},{2,10},{10... | collective-permute-start | bytes 6291464 | tf_op jit(solution)/shard_map/ppermute | solution.py:52
  287.8 25.7 %all-to-all-start.4 = ((f32[8,2,128]{2,1,0:T(2,128)}), f32[8,2,128]{2,1,0:T(2,128)S(1)}, u32[]{:S(2)}, u32[]{:S(2)}) async-start(f32[8,2,128]{2,1,0:T(2,128)} %bitcast.52), calls=%async_computation.4 | async-start | bytes 16384 | tf_op jit(solution)/shard_map/all_to_all | solution.py:1014
  292.9 204.1 %reduce-scatter.4.cloned.1.call-start = ((), (), s32[]{:S(2)}) async-start(), calls=%async_computation.14 | async-start | bytes 4718592 | tf_op jit(solution)/shard_map/reduce_scatter | solution.py:1077
  427.3 43.4 %collective-permute-start.31 = (bf16[2,2,256,2048]{3,2,1,0:T(8,128)(2,1)}, bf16[2,2,256,2048]{3,2,1,0:T(8,128)(2,1)}, u32[]{:S(2)}, u32[]{:S(2)}) collective-permute-start(bf16[2,2,256,2048]{3,2,1,0:T(8,128)(2,1)} %get-tuple-element.157), channel_id=1, source_target_pairs={{0,8},{8,0},{16,24},{24,16},{1,9},{9,1},{17,25},{25,17},{2,10},{10... | collective-permute-start | bytes 12582920 | tf_op jit(solution)/shard_map/ppermute | solution.py:52
  470.6 27.6 %collective-permute-start.33 = (bf16[2,2,2048,256]{3,2,1,0:T(8,128)(2,1)}, bf16[2,2,2048,256]{3,2,1,0:T(8,128)(2,1)}, u32[]{:S(2)}, u32[]{:S(2)}) collective-permute-start(bf16[2,2,2048,256]{3,2,1,0:T(8,128)(2,1)} %get-tuple-element.160), channel_id=1, source_target_pairs={{0,8},{8,0},{16,24},{24,16},{1,9},{9,1},{17,25},{25,17},{2,10},{10... | collective-permute-start | bytes 12582920 | tf_op jit(solution)/shard_map/ppermute | solution.py:52
  471.2 41.7 %collective-permute-start.32 = (bf16[2,2,2048,256]{3,2,1,0:T(8,128)(2,1)}, bf16[2,2,2048,256]{3,2,1,0:T(8,128)(2,1)}, u32[]{:S(2)}, u32[]{:S(2)}) collective-permute-start(bf16[2,2,2048,256]{3,2,1,0:T(8,128)(2,1)} %get-tuple-element.158), channel_id=1, source_target_pairs={{0,8},{8,0},{16,24},{24,16},{1,9},{9,1},{17,25},{25,17},{2,10},{10... | collective-permute-start | bytes 12582920 | tf_op jit(solution)/shard_map/ppermute | solution.py:52
  488.2 24.7 %collective-permute-start.34 = (bf16[256,2048]{1,0:T(8,128)(2,1)S(1)}, bf16[256,2048]{1,0:T(8,128)(2,1)S(1)}, u32[]{:S(2)}, u32[]{:S(2)}) collective-permute-start(bf16[256,2048]{1,0:T(8,128)(2,1)S(1)} %get-tuple-element.230), channel_id=1, source_target_pairs={{0,16},{8,24},{16,0},{24,8},{1,17},{9,25},{17,1},{25,9},{2,18},{10... | collective-permute-start | bytes 3145736 | tf_op jit(solution)/shard_map/ppermute | solution.py:52
  540.3 20.5 %all-to-all-start.6 = ((bf16[8,256,128]{2,1,0:T(8,128)(2,1)}), bf16[8,256,128]{2,1,0:T(8,128)(2,1)}, u32[]{:S(2)}, u32[]{:S(2)}) async-start(bf16[8,256,128]{2,1,0:T(8,128)(2,1)} %bitcast.85), calls=%async_computation.7 | async-start | bytes 1048576 | tf_op jit(solution)/shard_map/all_to_all | solution.py:1122
  545.9 144.7 %reduce-scatter.6.cloned.1.call-start = ((), (), s32[]{:S(2)}) async-start(), calls=%async_computation.15 | async-start | bytes 7077888 | tf_op jit(solution)/shard_map/reduce_scatter | solution.py:1127
  563.8 46.3 %collective-permute-start.43 = (bf16[2,2048,256]{2,1,0:T(8,128)(2,1)S(1)}, bf16[2,2048,256]{2,1,0:T(8,128)(2,1)}, u32[]{:S(2)}, u32[]{:S(2)}) collective-permute-start(bf16[2,2048,256]{2,1,0:T(8,128)(2,1)S(1)} %copy-done.31), channel_id=1, source_target_pairs={{0,16},{8,24},{16,0},{24,8},{1,17},{9,25},{17,1},{25,9},{2,18},{10... | collective-permute-start | bytes 6291464 | tf_op jit(solution)/shard_map/ppermute | solution.py:52
  611.4 44.4 %all-to-all-start.7 = ((bf16[4,2,3,256,128]{4,3,2,1,0:T(8,128)(2,1)}), bf16[4,2,3,256,128]{4,3,2,1,0:T(8,128)(2,1)S(1)}, u32[]{:S(2)}, u32[]{:S(2)}) async-start(bf16[4,2,3,256,128]{4,3,2,1,0:T(8,128)(2,1)} %pad_maximum_fusion.3), calls=%async_computation.8 | async-start | bytes 3145728 | tf_op jit(solution)/shard_map/all_to_all | solution.py:167
  615.0 148.2 %reduce-scatter.8.cloned.1.call-start = ((), (), s32[]{:S(2)}) async-start(), calls=%async_computation.16 | async-start | bytes 3932160 | tf_op jit(solution)/shard_map/reduce_scatter | solution.py:1153
  615.1 46.2 %collective-permute-start.45 = (bf16[2,2048,256]{2,1,0:T(8,128)(2,1)}, bf16[2,2048,256]{2,1,0:T(8,128)(2,1)}, u32[]{:S(2)}, u32[]{:S(2)}) collective-permute-start(bf16[2,2048,256]{2,1,0:T(8,128)(2,1)} %fusion.1), channel_id=1, source_target_pairs={{0,16},{8,24},{16,0},{24,8},{1,17},{9,25},{17,1},{25,9},{2,18},{10... | collective-permute-start | bytes 6291464 | tf_op jit(solution)/shard_map/ppermute | solution.py:52
  701.0 25.8 %collective-permute-start.52 = (bf16[256,2048]{1,0:T(8,128)(2,1)}, bf16[256,2048]{1,0:T(8,128)(2,1)S(1)}, u32[]{:S(2)}, u32[]{:S(2)}) collective-permute-start(bf16[256,2048]{1,0:T(8,128)(2,1)} %get-tuple-element.188), channel_id=1, source_target_pairs={{0,16},{8,24},{16,0},{24,8},{1,17},{9,25},{17,1},{25,9},{2,18},{10... | collective-permute-start | bytes 3145736 | tf_op jit(solution)/shard_map/ppermute | solution.py:52
  706.1 25.6 %collective-permute-start.51 = (bf16[2,128,2048]{2,1,0:T(8,128)(2,1)S(1)}, bf16[2,128,2048]{2,1,0:T(8,128)(2,1)S(1)}, u32[]{:S(2)}, u32[]{:S(2)}) collective-permute-start(bf16[2,128,2048]{2,1,0:T(8,128)(2,1)S(1)} %pad_maximum_fusion.6), channel_id=1, source_target_pairs={{0,1},{1,0},{2,3},{3,2},{4,5},{5,4},{6,7},{7,6},{8,9},{9,8},{10,11... | collective-permute-start | bytes 3145736 | tf_op jit(solution)/shard_map/ppermute | solution.py:52
  (94 other events, 1015.5 us)
Sparse Core Ops, SparseCore 0:
  26.2 61.9 all-gather.5
  206.5 73.5 all-gather.9
  287.1 73.9 all-gather.7
  410.6 86.4 reduce-scatter.3
  562.4 124.0 reduce-scatter.5
  701.1 62.1 reduce-scatter.7
